TPU v7x, 512 devices: a whole 4x8x8 slice. The times are simulated.
512 devices in a mesh: grp: 64 (over y_hi, x, z), blk: 8 (over y_lo, core).
Axes of the slice: x: 4, y: 8 (y_hi: 2, y_lo: 4; y = y_hi * 4 + y_lo), z: 8, core: 2. Of those that a mesh axis runs over, the one named last changes fastest.
Arguments:
- features: float32 [65536, 256], P(('grp', 'blk')), may hold values from -1.5 to 1.5
- factor_u: float32 [65536, 128], P(('grp', 'blk')), may hold values from -1.8 to 1.8
- factor_v: float32 [65536, 128], P(('grp', 'blk')), may hold values from -1.8 to 1.8
- tile_mask: int32 [512, 512], P(('grp', 'blk')), may hold values 0 or 1
- matching: int32 [3, 64], replicated, may hold values from 0 to 63, each once within a row
Outputs:
- u_new: float32 [65536, 128], P(('grp', 'blk'))
- held_v: float32 [65536, 128], P(('grp', 'blk'))
Inputs may be any that keep to these rules, and one draw needn't show every extreme that they name: `matching`: each row is a permutation of the 64 groups.
All inputs are finite; a program needn't handle non-finite values. No bound on the sum of `tile_mask` on one device may be relied on, other than what follows from the above.
Results may differ from a plain program's by a relative error of at most 0.017.
Values may be sent and summed in bfloat16 or wider, within the bound.
No kernel may reach another device: no remote copies, remote signals or barrier semaphores. Data moves between devices by JAX's collectives and lax.ppermute only.
A program may use at most 64 MiB of HBM per device.

v0:
```python
import jax
import jax.numpy as jnp
from jax import lax
from jax.sharding import PartitionSpec as P

TILE = 128
TPD = 1
SUB = 4


def passed_along(array, axis, by):
    length = lax.axis_size(axis)
    return lax.ppermute(array, axis, [(i, (i + by) % length) for i in range(length)])


def pair_rows(left_rows, right_rows):
    return lax.dot_general(
        left_rows, right_rows, (((1,), (1,)), ((), ())), preferred_element_type=jnp.float32
    )


def invert(destinations, group_count):
    labels = jnp.arange(group_count, dtype=jnp.int32)
    matches = (destinations[None, :] == labels[:, None]).astype(jnp.int32)
    return jnp.sum(matches * labels[None, :], axis=1)


def local(features, factor_u, factor_v, tile_mask, matching):
    groups = lax.axis_size("grp")
    blocks = lax.axis_size("blk")
    group_index = lax.axis_index("grp")
    part_index = lax.axis_index("blk")
    slot_rows = factor_u.shape[0]
    rank_width = factor_u.shape[1]
    feature_width = features.shape[1]
    step_size = 4.0 / slot_rows
    own_bf = features.astype(jnp.bfloat16)
    left_factor = factor_u
    right_factor = factor_v
    carried_x = own_bf
    holdings = jnp.arange(groups, dtype=jnp.int32)
    for sub_epoch in range(SUB):
        col_block = holdings[group_index]
        for cycle_step in range(blocks):
            col_part = (part_index - cycle_step) % blocks
            column_bf = carried_x
            tile_start = (col_block * blocks + col_part) * TPD
            picked = lax.dynamic_slice_in_dim(tile_mask, tile_start, TPD, 1).astype(jnp.float32)
            keeping = jnp.broadcast_to(picked[:, None, :, None], (TPD, TILE, TPD, TILE)).reshape(
                slot_rows, slot_rows
            )
            similar = pair_rows(own_bf, column_bf)
            u_bf = left_factor.astype(jnp.bfloat16)
            v_bf = right_factor.astype(jnp.bfloat16)
            predicted = pair_rows(u_bf, v_bf)
            residual = (keeping * (predicted - similar)).astype(jnp.bfloat16)
            grad_u = jnp.dot(residual, v_bf, preferred_element_type=jnp.float32)
            grad_v = lax.dot_general(
                residual, u_bf, (((0,), (0,)), ((), ())), preferred_element_type=jnp.float32
            )
            left_factor = left_factor - step_size * grad_u
            right_factor = right_factor - step_size * grad_v
            right_factor = passed_along(right_factor, "blk", 1)
            carried_x = passed_along(carried_x, "blk", 1)
        if sub_epoch + 1 < SUB:
            inverse = invert(matching[sub_epoch], groups)
            holdings = jnp.take(holdings, inverse)
            spread_v = lax.all_to_all(
                right_factor.reshape(groups, -1).astype(jnp.bfloat16),
                "grp",
                split_axis=0,
                concat_axis=0,
                tiled=True,
            ).astype(jnp.float32)
            spread_x = lax.all_to_all(
                carried_x.reshape(groups, -1), "grp", split_axis=0, concat_axis=0, tiled=True
            )
            chosen_v = jnp.take(spread_v, inverse, axis=0)
            chosen_x = jnp.take(spread_x, inverse, axis=0)
            arrived_v = lax.all_to_all(
                chosen_v.astype(jnp.bfloat16), "grp", split_axis=0, concat_axis=0, tiled=True
            ).astype(chosen_v.dtype)
            arrived_x = lax.all_to_all(chosen_x, "grp", split_axis=0, concat_axis=0, tiled=True)
            right_factor = arrived_v.reshape(slot_rows, rank_width)
            carried_x = arrived_x.reshape(slot_rows, feature_width)
    return (left_factor, right_factor)


def solution(mesh):
    in_specs = (
        P(("grp", "blk"), None),
        P(("grp", "blk"), None),
        P(("grp", "blk"), None),
        P(("grp", "blk"), None),
        P(),
    )
    out_specs = (P(("grp", "blk"), None), P(("grp", "blk"), None))
    return jax.shard_map(local, mesh=mesh, in_specs=in_specs, out_specs=out_specs, check_vma=False)
```

profile of v0, /device:TPU:1, one launch (start us, length us, event | category | flops | bytes accessed | tf_op | source)
XLA Modules:
  0.0 583.6 jit_solution(15783075077946066712)
XLA Ops:
  1.5 4.6 collective-permute-start.1
  21.3 3.4 collective-permute-start.2
  35.1 3.4 collective-permute-done.4
  43.0 2.5 collective-permute-start.7
  45.5 2.8 collective-permute-done.6
  54.7 3.4 collective-permute-done.8
  64.5 3.4 collective-permute-done.10
  74.3 3.4 collective-permute-done.12
  82.1 5.4 collective-permute-done.14
  89.6 13.5 %all-to-all-start = ((bf16[64,2,128]{2,1,0:T(2,128)(2,1)}), bf16[64,2,128]{2,1,0:T(2,128)(2,1)S(1)}, u32[]{:S(2)}, u32[]{:S(2)}) async-start(bf16[64,2,128]{2,1,0:T(2,128)(2,1)} %reshape.484), calls=%async_computation | async-start | bytes 65536 | tf_op jit(solution)/shard_map/all_to_all | solution.py:68
  105.0 11.3 %all-to-all-done = bf16[64,2,128]{2,1,0:T(2,128)(2,1)S(1)} async-done(((bf16[64,2,128]{2,1,0:T(2,128)(2,1)}), bf16[64,2,128]{2,1,0:T(2,128)(2,1)S(1)}, u32[]{:S(2)}, u32[]{:S(2)}) %all-to-all-start) | async-done | bytes 32800 | tf_op jit(solution)/shard_map/all_to_all | solution.py:68
  118.4 4.6 all-to-all-start.1
  131.9 4.2 all-to-all-done.1
  136.1 10.4 %all-to-all-start.2 = ((bf16[64,2,256]{2,1,0:T(2,128)(2,1)}), bf16[64,2,256]{2,1,0:T(2,128)(2,1)S(1)}, u32[]{:S(2)}, u32[]{:S(2)}) async-start(bf16[64,2,256]{2,1,0:T(2,128)(2,1)} %reshape.488), calls=%async_computation.2 | async-start | bytes 131072 | tf_op jit(solution)/shard_map/all_to_all | solution.py:75
  146.9 12.9 %all-to-all-done.2 = bf16[64,2,256]{2,1,0:T(2,128)(2,1)S(1)} async-done(((bf16[64,2,256]{2,1,0:T(2,128)(2,1)}), bf16[64,2,256]{2,1,0:T(2,128)(2,1)S(1)}, u32[]{:S(2)}, u32[]{:S(2)}) %all-to-all-start.2) | async-done | bytes 65568 | tf_op jit(solution)/shard_map/all_to_all | solution.py:75
  162.0 4.6 all-to-all-start.3
  166.8 13.1 %all-to-all-done.3 = bf16[64,2,256]{2,1,0:T(2,128)(2,1)S(1)} async-done(((bf16[64,2,256]{2,1,0:T(2,128)(2,1)}), bf16[64,2,256]{2,1,0:T(2,128)(2,1)S(1)}, u32[]{:S(2)}, u32[]{:S(2)}) %all-to-all-start.3) | async-done | bytes 65568 | tf_op jit(solution)/shard_map/all_to_all | solution.py:83
  180.4 4.0 collective-permute-start.17
  186.9 4.8 collective-permute-done.17
  191.8 2.3 collective-permute-done.16
  198.5 3.4 collective-permute-done.18
  208.3 3.4 collective-permute-done.20
  218.1 3.4 collective-permute-done.22
  227.9 3.4 collective-permute-done.24
  237.7 3.4 collective-permute-done.26
  247.5 3.4 collective-permute-done.28
  253.3 2.1 collective-permute-start.30
  255.4 5.2 collective-permute-done.30
  262.1 4.6 all-to-all-start.4
  268.6 11.2 %all-to-all-done.4 = bf16[64,2,128]{2,1,0:T(2,128)(2,1)S(1)} async-done(((bf16[64,2,128]{2,1,0:T(2,128)(2,1)}), bf16[64,2,128]{2,1,0:T(2,128)(2,1)S(1)}, u32[]{:S(2)}, u32[]{:S(2)}) %all-to-all-start.4) | async-done | bytes 32800 | tf_op jit(solution)/shard_map/all_to_all | solution.py:68
  282.0 4.6 all-to-all-start.5
  293.2 6.5 %all-to-all-done.5 = bf16[64,2,128]{2,1,0:T(2,128)(2,1)S(1)} async-done(((bf16[64,2,128]{2,1,0:T(2,128)(2,1)}), bf16[64,2,128]{2,1,0:T(2,128)(2,1)S(1)}, u32[]{:S(2)}, u32[]{:S(2)}) %all-to-all-start.5) | async-done | bytes 32800 | tf_op jit(solution)/shard_map/all_to_all | solution.py:80
  299.7 8.2 %all-to-all-start.6 = ((bf16[64,2,256]{2,1,0:T(2,128)(2,1)}), bf16[64,2,256]{2,1,0:T(2,128)(2,1)S(1)}, u32[]{:S(2)}, u32[]{:S(2)}) async-start(bf16[64,2,256]{2,1,0:T(2,128)(2,1)} %reshape.496), calls=%async_computation.6 | async-start | bytes 131072 | tf_op jit(solution)/shard_map/all_to_all | solution.py:75
  308.2 12.9 %all-to-all-done.6 = bf16[64,2,256]{2,1,0:T(2,128)(2,1)S(1)} async-done(((bf16[64,2,256]{2,1,0:T(2,128)(2,1)}), bf16[64,2,256]{2,1,0:T(2,128)(2,1)S(1)}, u32[]{:S(2)}, u32[]{:S(2)}) %all-to-all-start.6) | async-done | bytes 65568 | tf_op jit(solution)/shard_map/all_to_all | solution.py:75
  323.4 4.6 all-to-all-start.7
  328.1 13.1 %all-to-all-done.7 = bf16[64,2,256]{2,1,0:T(2,128)(2,1)S(1)} async-done(((bf16[64,2,256]{2,1,0:T(2,128)(2,1)}), bf16[64,2,256]{2,1,0:T(2,128)(2,1)S(1)}, u32[]{:S(2)}, u32[]{:S(2)}) %all-to-all-start.7) | async-done | bytes 65568 | tf_op jit(solution)/shard_map/all_to_all | solution.py:83
  341.7 3.8 collective-permute-start.33
  348.0 4.8 collective-permute-done.33
  352.9 2.3 collective-permute-done.32
  359.6 3.4 collective-permute-done.34
  369.4 3.4 collective-permute-done.36
  379.2 3.4 collective-permute-done.38
  389.0 3.4 collective-permute-done.40
  398.8 3.4 collective-permute-done.42
  408.6 3.4 collective-permute-done.44
  416.3 5.4 collective-permute-done.46
  423.3 4.6 all-to-all-start.8
  429.8 11.2 %all-to-all-done.8 = bf16[64,2,128]{2,1,0:T(2,128)(2,1)S(1)} async-done(((bf16[64,2,128]{2,1,0:T(2,128)(2,1)}), bf16[64,2,128]{2,1,0:T(2,128)(2,1)S(1)}, u32[]{:S(2)}, u32[]{:S(2)}) %all-to-all-start.8) | async-done | bytes 32800 | tf_op jit(solution)/shard_map/all_to_all | solution.py:68
  443.1 4.6 all-to-all-start.9
  454.3 6.5 %all-to-all-done.9 = bf16[64,2,128]{2,1,0:T(2,128)(2,1)S(1)} async-done(((bf16[64,2,128]{2,1,0:T(2,128)(2,1)}), bf16[64,2,128]{2,1,0:T(2,128)(2,1)S(1)}, u32[]{:S(2)}, u32[]{:S(2)}) %all-to-all-start.9) | async-done | bytes 32800 | tf_op jit(solution)/shard_map/all_to_all | solution.py:80
  460.8 8.1 %all-to-all-start.10 = ((bf16[64,2,256]{2,1,0:T(2,128)(2,1)}), bf16[64,2,256]{2,1,0:T(2,128)(2,1)S(1)}, u32[]{:S(2)}, u32[]{:S(2)}) async-start(bf16[64,2,256]{2,1,0:T(2,128)(2,1)} %reshape.504), calls=%async_computation.10 | async-start | bytes 131072 | tf_op jit(solution)/shard_map/all_to_all | solution.py:75
  469.4 12.9 %all-to-all-done.10 = bf16[64,2,256]{2,1,0:T(2,128)(2,1)S(1)} async-done(((bf16[64,2,256]{2,1,0:T(2,128)(2,1)}), bf16[64,2,256]{2,1,0:T(2,128)(2,1)S(1)}, u32[]{:S(2)}, u32[]{:S(2)}) %all-to-all-start.10) | async-done | bytes 65568 | tf_op jit(solution)/shard_map/all_to_all | solution.py:75
  484.5 4.6 all-to-all-start.11
  489.2 13.1 %all-to-all-done.11 = bf16[64,2,256]{2,1,0:T(2,128)(2,1)S(1)} async-done(((bf16[64,2,256]{2,1,0:T(2,128)(2,1)}), bf16[64,2,256]{2,1,0:T(2,128)(2,1)S(1)}, u32[]{:S(2)}, u32[]{:S(2)}) %all-to-all-start.11) | async-done | bytes 65568 | tf_op jit(solution)/shard_map/all_to_all | solution.py:83
  502.8 3.8 collective-permute-start.49
  509.1 4.8 collective-permute-done.49
  514.1 2.3 collective-permute-done.48
  520.7 3.4 collective-permute-done.50
  530.5 3.4 collective-permute-done.52
  540.3 3.4 collective-permute-done.54
  550.1 3.4 collective-permute-done.56
  559.9 3.4 collective-permute-done.58
  569.7 3.4 collective-permute-done.60
  578.2 4.7 collective-permute-done.62
  (318 shorter events, 209.3 us)
Async XLA Ops:
  1.5 19.1 %collective-permute-start.1 = (bf16[128,256]{1,0:T(8,128)(2,1)S(1)}, bf16[128,256]{1,0:T(8,128)(2,1)S(1)}, u32[]{:S(2)}, u32[]{:S(2)}) collective-permute-start(bf16[128,256]{1,0:T(8,128)(2,1)S(1)} %convert_element_type.465), channel_id=1, source_target_pairs={{0,1},{1,2},{2,3},{3,4},{4,5},{5,6},{6,7},{7,0},{8,9},{9,10},{10,1... | collective-permute-start | bytes 196616 | tf_op jit(solution)/shard_map/ppermute | solution.py:13
  21.3 7.4 %collective-permute-start.2 = (f32[128,128]{1,0:T(8,128)S(1)}, f32[128,128]{1,0:T(8,128)S(1)}, u32[]{:S(2)}, u32[]{:S(2)}) collective-permute-start(f32[128,128]{1,0:T(8,128)S(1)} %fusion.111), channel_id=1, source_target_pairs={{0,1},{1,2},{2,3},{3,4},{4,5},{5,6},{6,7},{7,0},{8,9},{9,10},{10,1... | collective-permute-start | bytes 196616 | tf_op jit(solution)/shard_map/ppermute | solution.py:13
  31.1 7.4 %collective-permute-start.4 = (f32[128,128]{1,0:T(8,128)S(1)}, f32[128,128]{1,0:T(8,128)S(1)}, u32[]{:S(2)}, u32[]{:S(2)}) collective-permute-start(f32[128,128]{1,0:T(8,128)S(1)} %fusion.108), channel_id=1, source_target_pairs={{0,1},{1,2},{2,3},{3,4},{4,5},{5,6},{6,7},{7,0},{8,9},{9,10},{10,1... | collective-permute-start | bytes 196616 | tf_op jit(solution)/shard_map/ppermute | solution.py:13
  33.2 7.4 %collective-permute-start.5 = (bf16[128,256]{1,0:T(8,128)(2,1)S(1)}, bf16[128,256]{1,0:T(8,128)(2,1)S(1)}, u32[]{:S(2)}, u32[]{:S(2)}) collective-permute-start(bf16[128,256]{1,0:T(8,128)(2,1)S(1)} %collective-permute-done.3), channel_id=1, source_target_pairs={{0,1},{1,2},{2,3},{3,4},{4,5},{5,6},{6,7},{7,0},{8,9},{9,10},{10,1... | collective-permute-start | bytes 196616 | tf_op jit(solution)/shard_map/ppermute | solution.py:13
  40.9 7.4 %collective-permute-start.6 = (f32[128,128]{1,0:T(8,128)S(1)}, f32[128,128]{1,0:T(8,128)S(1)}, u32[]{:S(2)}, u32[]{:S(2)}) collective-permute-start(f32[128,128]{1,0:T(8,128)S(1)} %fusion.105), channel_id=1, source_target_pairs={{0,1},{1,2},{2,3},{3,4},{4,5},{5,6},{6,7},{7,0},{8,9},{9,10},{10,1... | collective-permute-start | bytes 196616 | tf_op jit(solution)/shard_map/ppermute | solution.py:13
  43.0 7.4 %collective-permute-start.7 = (bf16[128,256]{1,0:T(8,128)(2,1)S(1)}, bf16[128,256]{1,0:T(8,128)(2,1)S(1)}, u32[]{:S(2)}, u32[]{:S(2)}) collective-permute-start(bf16[128,256]{1,0:T(8,128)(2,1)S(1)} %collective-permute-done.5), channel_id=1, source_target_pairs={{0,1},{1,2},{2,3},{3,4},{4,5},{5,6},{6,7},{7,0},{8,9},{9,10},{10,1... | collective-permute-start | bytes 196616 | tf_op jit(solution)/shard_map/ppermute | solution.py:13
  50.7 7.4 %collective-permute-start.8 = (f32[128,128]{1,0:T(8,128)S(1)}, f32[128,128]{1,0:T(8,128)S(1)}, u32[]{:S(2)}, u32[]{:S(2)}) collective-permute-start(f32[128,128]{1,0:T(8,128)S(1)} %fusion.102), channel_id=1, source_target_pairs={{0,1},{1,2},{2,3},{3,4},{4,5},{5,6},{6,7},{7,0},{8,9},{9,10},{10,1... | collective-permute-start | bytes 196616 | tf_op jit(solution)/shard_map/ppermute | solution.py:13
  52.8 7.4 %collective-permute-start.9 = (bf16[128,256]{1,0:T(8,128)(2,1)S(1)}, bf16[128,256]{1,0:T(8,128)(2,1)S(1)}, u32[]{:S(2)}, u32[]{:S(2)}) collective-permute-start(bf16[128,256]{1,0:T(8,128)(2,1)S(1)} %collective-permute-done.7), channel_id=1, source_target_pairs={{0,1},{1,2},{2,3},{3,4},{4,5},{5,6},{6,7},{7,0},{8,9},{9,10},{10,1... | collective-permute-start | bytes 196616 | tf_op jit(solution)/shard_map/ppermute | solution.py:13
  60.5 7.4 %collective-permute-start.10 = (f32[128,128]{1,0:T(8,128)S(1)}, f32[128,128]{1,0:T(8,128)S(1)}, u32[]{:S(2)}, u32[]{:S(2)}) collective-permute-start(f32[128,128]{1,0:T(8,128)S(1)} %fusion.99), channel_id=1, source_target_pairs={{0,1},{1,2},{2,3},{3,4},{4,5},{5,6},{6,7},{7,0},{8,9},{9,10},{10,1... | collective-permute-start | bytes 196616 | tf_op jit(solution)/shard_map/ppermute | solution.py:13
  62.6 7.4 %collective-permute-start.11 = (bf16[128,256]{1,0:T(8,128)(2,1)S(1)}, bf16[128,256]{1,0:T(8,128)(2,1)S(1)}, u32[]{:S(2)}, u32[]{:S(2)}) collective-permute-start(bf16[128,256]{1,0:T(8,128)(2,1)S(1)} %collective-permute-done.9), channel_id=1, source_target_pairs={{0,1},{1,2},{2,3},{3,4},{4,5},{5,6},{6,7},{7,0},{8,9},{9,10},{10,1... | collective-permute-start | bytes 196616 | tf_op jit(solution)/shard_map/ppermute | solution.py:13
  70.3 7.4 %collective-permute-start.12 = (f32[128,128]{1,0:T(8,128)S(1)}, f32[128,128]{1,0:T(8,128)S(1)}, u32[]{:S(2)}, u32[]{:S(2)}) collective-permute-start(f32[128,128]{1,0:T(8,128)S(1)} %fusion.96), channel_id=1, source_target_pairs={{0,1},{1,2},{2,3},{3,4},{4,5},{5,6},{6,7},{7,0},{8,9},{9,10},{10,1... | collective-permute-start | bytes 196616 | tf_op jit(solution)/shard_map/ppermute | solution.py:13
  72.4 7.4 %collective-permute-start.13 = (bf16[128,256]{1,0:T(8,128)(2,1)S(1)}, bf16[128,256]{1,0:T(8,128)(2,1)S(1)}, u32[]{:S(2)}, u32[]{:S(2)}) collective-permute-start(bf16[128,256]{1,0:T(8,128)(2,1)S(1)} %collective-permute-done.11), channel_id=1, source_target_pairs={{0,1},{1,2},{2,3},{3,4},{4,5},{5,6},{6,7},{7,0},{8,9},{9,10},{10,1... | collective-permute-start | bytes 196616 | tf_op jit(solution)/shard_map/ppermute | solution.py:13
  89.6 26.7 %all-to-all-start = ((bf16[64,2,128]{2,1,0:T(2,128)(2,1)}), bf16[64,2,128]{2,1,0:T(2,128)(2,1)S(1)}, u32[]{:S(2)}, u32[]{:S(2)}) async-start(bf16[64,2,128]{2,1,0:T(2,128)(2,1)} %reshape.484), calls=%async_computation | async-start | bytes 65536 | tf_op jit(solution)/shard_map/all_to_all | solution.py:68
  103.0 27.1 %collective-permute-start.15 = (bf16[128,256]{1,0:T(8,128)(2,1)S(1)}, bf16[128,256]{1,0:T(8,128)(2,1)S(1)}, u32[]{:S(2)}, u32[]{:S(2)}) collective-permute-start(bf16[128,256]{1,0:T(8,128)(2,1)S(1)} %collective-permute-done.13), channel_id=1, source_target_pairs={{0,1},{1,2},{2,3},{3,4},{4,5},{5,6},{6,7},{7,0},{8,9},{9,10},{10,1... | collective-permute-start | bytes 196616 | tf_op jit(solution)/shard_map/ppermute | solution.py:13
  118.4 17.7 %all-to-all-start.1 = ((bf16[64,2,128]{2,1,0:T(2,128)(2,1)}), bf16[64,2,128]{2,1,0:T(2,128)(2,1)S(1)}, u32[]{:S(2)}, u32[]{:S(2)}) async-start(bf16[64,2,128]{2,1,0:T(2,128)(2,1)} %reshape.486), calls=%async_computation.1 | async-start | bytes 65536 | tf_op jit(solution)/shard_map/all_to_all | solution.py:80
  136.1 23.7 %all-to-all-start.2 = ((bf16[64,2,256]{2,1,0:T(2,128)(2,1)}), bf16[64,2,256]{2,1,0:T(2,128)(2,1)S(1)}, u32[]{:S(2)}, u32[]{:S(2)}) async-start(bf16[64,2,256]{2,1,0:T(2,128)(2,1)} %reshape.488), calls=%async_computation.2 | async-start | bytes 131072 | tf_op jit(solution)/shard_map/all_to_all | solution.py:75
  162.0 17.9 %all-to-all-start.3 = ((bf16[64,2,256]{2,1,0:T(2,128)(2,1)}), bf16[64,2,256]{2,1,0:T(2,128)(2,1)S(1)}, u32[]{:S(2)}, u32[]{:S(2)}) async-start(bf16[64,2,256]{2,1,0:T(2,128)(2,1)} %reshape.490), calls=%async_computation.3 | async-start | bytes 131072 | tf_op jit(solution)/shard_map/all_to_all | solution.py:83
  180.4 11.3 %collective-permute-start.17 = (bf16[128,256]{1,0:T(8,128)(2,1)S(1)}, bf16[128,256]{1,0:T(8,128)(2,1)S(1)}, u32[]{:S(2)}, u32[]{:S(2)}) collective-permute-start(bf16[128,256]{1,0:T(8,128)(2,1)S(1)} %reshape.318), channel_id=1, source_target_pairs={{0,1},{1,2},{2,3},{3,4},{4,5},{5,6},{6,7},{7,0},{8,9},{9,10},{10,1... | collective-permute-start | bytes 196616 | tf_op jit(solution)/shard_map/ppermute | solution.py:13
  184.9 9.2 %collective-permute-start.16 = (f32[128,128]{1,0:T(8,128)S(1)}, f32[128,128]{1,0:T(8,128)S(1)}, u32[]{:S(2)}, u32[]{:S(2)}) collective-permute-start(f32[128,128]{1,0:T(8,128)S(1)} %fusion.89), channel_id=1, source_target_pairs={{0,1},{1,2},{2,3},{3,4},{4,5},{5,6},{6,7},{7,0},{8,9},{9,10},{10,1... | collective-permute-start | bytes 196616 | tf_op jit(solution)/shard_map/ppermute | solution.py:13
  194.5 7.4 %collective-permute-start.18 = (f32[128,128]{1,0:T(8,128)S(1)}, f32[128,128]{1,0:T(8,128)S(1)}, u32[]{:S(2)}, u32[]{:S(2)}) collective-permute-start(f32[128,128]{1,0:T(8,128)S(1)} %fusion.86), channel_id=1, source_target_pairs={{0,1},{1,2},{2,3},{3,4},{4,5},{5,6},{6,7},{7,0},{8,9},{9,10},{10,1... | collective-permute-start | bytes 196616 | tf_op jit(solution)/shard_map/ppermute | solution.py:13
  196.5 7.4 %collective-permute-start.19 = (bf16[128,256]{1,0:T(8,128)(2,1)S(1)}, bf16[128,256]{1,0:T(8,128)(2,1)S(1)}, u32[]{:S(2)}, u32[]{:S(2)}) collective-permute-start(bf16[128,256]{1,0:T(8,128)(2,1)S(1)} %collective-permute-done.17), channel_id=1, source_target_pairs={{0,1},{1,2},{2,3},{3,4},{4,5},{5,6},{6,7},{7,0},{8,9},{9,10},{10,1... | collective-permute-start | bytes 196616 | tf_op jit(solution)/shard_map/ppermute | solution.py:13
  204.3 7.4 %collective-permute-start.20 = (f32[128,128]{1,0:T(8,128)S(1)}, f32[128,128]{1,0:T(8,128)S(1)}, u32[]{:S(2)}, u32[]{:S(2)}) collective-permute-start(f32[128,128]{1,0:T(8,128)S(1)} %fusion.82), channel_id=1, source_target_pairs={{0,1},{1,2},{2,3},{3,4},{4,5},{5,6},{6,7},{7,0},{8,9},{9,10},{10,1... | collective-permute-start | bytes 196616 | tf_op jit(solution)/shard_map/ppermute | solution.py:13
  206.3 7.4 %collective-permute-start.21 = (bf16[128,256]{1,0:T(8,128)(2,1)S(1)}, bf16[128,256]{1,0:T(8,128)(2,1)S(1)}, u32[]{:S(2)}, u32[]{:S(2)}) collective-permute-start(bf16[128,256]{1,0:T(8,128)(2,1)S(1)} %collective-permute-done.19), channel_id=1, source_target_pairs={{0,1},{1,2},{2,3},{3,4},{4,5},{5,6},{6,7},{7,0},{8,9},{9,10},{10,1... | collective-permute-start | bytes 196616 | tf_op jit(solution)/shard_map/ppermute | solution.py:13
  214.1 7.4 %collective-permute-start.22 = (f32[128,128]{1,0:T(8,128)S(1)}, f32[128,128]{1,0:T(8,128)S(1)}, u32[]{:S(2)}, u32[]{:S(2)}) collective-permute-start(f32[128,128]{1,0:T(8,128)S(1)} %fusion.78), channel_id=1, source_target_pairs={{0,1},{1,2},{2,3},{3,4},{4,5},{5,6},{6,7},{7,0},{8,9},{9,10},{10,1... | collective-permute-start | bytes 196616 | tf_op jit(solution)/shard_map/ppermute | solution.py:13
  216.1 7.4 %collective-permute-start.23 = (bf16[128,256]{1,0:T(8,128)(2,1)S(1)}, bf16[128,256]{1,0:T(8,128)(2,1)S(1)}, u32[]{:S(2)}, u32[]{:S(2)}) collective-permute-start(bf16[128,256]{1,0:T(8,128)(2,1)S(1)} %collective-permute-done.21), channel_id=1, source_target_pairs={{0,1},{1,2},{2,3},{3,4},{4,5},{5,6},{6,7},{7,0},{8,9},{9,10},{10,1... | collective-permute-start | bytes 196616 | tf_op jit(solution)/shard_map/ppermute | solution.py:13
  223.9 7.4 %collective-permute-start.24 = (f32[128,128]{1,0:T(8,128)S(1)}, f32[128,128]{1,0:T(8,128)S(1)}, u32[]{:S(2)}, u32[]{:S(2)}) collective-permute-start(f32[128,128]{1,0:T(8,128)S(1)} %fusion.74), channel_id=1, source_target_pairs={{0,1},{1,2},{2,3},{3,4},{4,5},{5,6},{6,7},{7,0},{8,9},{9,10},{10,1... | collective-permute-start | bytes 196616 | tf_op jit(solution)/shard_map/ppermute | solution.py:13
  233.7 7.4 %collective-permute-start.26 = (f32[128,128]{1,0:T(8,128)S(1)}, f32[128,128]{1,0:T(8,128)S(1)}, u32[]{:S(2)}, u32[]{:S(2)}) collective-permute-start(f32[128,128]{1,0:T(8,128)S(1)} %fusion.70), channel_id=1, source_target_pairs={{0,1},{1,2},{2,3},{3,4},{4,5},{5,6},{6,7},{7,0},{8,9},{9,10},{10,1... | collective-permute-start | bytes 196616 | tf_op jit(solution)/shard_map/ppermute | solution.py:13
  235.7 7.4 %collective-permute-start.27 = (bf16[128,256]{1,0:T(8,128)(2,1)S(1)}, bf16[128,256]{1,0:T(8,128)(2,1)S(1)}, u32[]{:S(2)}, u32[]{:S(2)}) collective-permute-start(bf16[128,256]{1,0:T(8,128)(2,1)S(1)} %collective-permute-done.25), channel_id=1, source_target_pairs={{0,1},{1,2},{2,3},{3,4},{4,5},{5,6},{6,7},{7,0},{8,9},{9,10},{10,1... | collective-permute-start | bytes 196616 | tf_op jit(solution)/shard_map/ppermute | solution.py:13
  243.5 7.4 %collective-permute-start.28 = (f32[128,128]{1,0:T(8,128)S(1)}, f32[128,128]{1,0:T(8,128)S(1)}, u32[]{:S(2)}, u32[]{:S(2)}) collective-permute-start(f32[128,128]{1,0:T(8,128)S(1)} %fusion.66), channel_id=1, source_target_pairs={{0,1},{1,2},{2,3},{3,4},{4,5},{5,6},{6,7},{7,0},{8,9},{9,10},{10,1... | collective-permute-start | bytes 196616 | tf_op jit(solution)/shard_map/ppermute | solution.py:13
  245.5 7.4 %collective-permute-start.29 = (bf16[128,256]{1,0:T(8,128)(2,1)S(1)}, bf16[128,256]{1,0:T(8,128)(2,1)S(1)}, u32[]{:S(2)}, u32[]{:S(2)}) collective-permute-start(bf16[128,256]{1,0:T(8,128)(2,1)S(1)} %collective-permute-done.27), channel_id=1, source_target_pairs={{0,1},{1,2},{2,3},{3,4},{4,5},{5,6},{6,7},{7,0},{8,9},{9,10},{10,1... | collective-permute-start | bytes 196616 | tf_op jit(solution)/shard_map/ppermute | solution.py:13
  262.1 17.7 %all-to-all-start.4 = ((bf16[64,2,128]{2,1,0:T(2,128)(2,1)}), bf16[64,2,128]{2,1,0:T(2,128)(2,1)S(1)}, u32[]{:S(2)}, u32[]{:S(2)}) async-start(bf16[64,2,128]{2,1,0:T(2,128)(2,1)} %reshape.492), calls=%async_computation.4 | async-start | bytes 65536 | tf_op jit(solution)/shard_map/all_to_all | solution.py:68
  266.7 24.8 %collective-permute-start.31 = (bf16[128,256]{1,0:T(8,128)(2,1)S(1)}, bf16[128,256]{1,0:T(8,128)(2,1)S(1)}, u32[]{:S(2)}, u32[]{:S(2)}) collective-permute-start(bf16[128,256]{1,0:T(8,128)(2,1)S(1)} %collective-permute-done.29), channel_id=1, source_target_pairs={{0,1},{1,2},{2,3},{3,4},{4,5},{5,6},{6,7},{7,0},{8,9},{9,10},{10,1... | collective-permute-start | bytes 196616 | tf_op jit(solution)/shard_map/ppermute | solution.py:13
  282.0 17.7 %all-to-all-start.5 = ((bf16[64,2,128]{2,1,0:T(2,128)(2,1)}), bf16[64,2,128]{2,1,0:T(2,128)(2,1)S(1)}, u32[]{:S(2)}, u32[]{:S(2)}) async-start(bf16[64,2,128]{2,1,0:T(2,128)(2,1)} %reshape.494), calls=%async_computation.5 | async-start | bytes 65536 | tf_op jit(solution)/shard_map/all_to_all | solution.py:80
  299.7 21.4 %all-to-all-start.6 = ((bf16[64,2,256]{2,1,0:T(2,128)(2,1)}), bf16[64,2,256]{2,1,0:T(2,128)(2,1)S(1)}, u32[]{:S(2)}, u32[]{:S(2)}) async-start(bf16[64,2,256]{2,1,0:T(2,128)(2,1)} %reshape.496), calls=%async_computation.6 | async-start | bytes 131072 | tf_op jit(solution)/shard_map/all_to_all | solution.py:75
  323.4 17.9 %all-to-all-start.7 = ((bf16[64,2,256]{2,1,0:T(2,128)(2,1)}), bf16[64,2,256]{2,1,0:T(2,128)(2,1)S(1)}, u32[]{:S(2)}, u32[]{:S(2)}) async-start(bf16[64,2,256]{2,1,0:T(2,128)(2,1)} %reshape.498), calls=%async_computation.7 | async-start | bytes 131072 | tf_op jit(solution)/shard_map/all_to_all | solution.py:83
  341.7 11.1 %collective-permute-start.33 = (bf16[128,256]{1,0:T(8,128)(2,1)S(1)}, bf16[128,256]{1,0:T(8,128)(2,1)S(1)}, u32[]{:S(2)}, u32[]{:S(2)}) collective-permute-start(bf16[128,256]{1,0:T(8,128)(2,1)S(1)} %reshape.327), channel_id=1, source_target_pairs={{0,1},{1,2},{2,3},{3,4},{4,5},{5,6},{6,7},{7,0},{8,9},{9,10},{10,1... | collective-permute-start | bytes 196616 | tf_op jit(solution)/shard_map/ppermute | solution.py:13
  346.1 9.2 %collective-permute-start.32 = (f32[128,128]{1,0:T(8,128)S(1)}, f32[128,128]{1,0:T(8,128)S(1)}, u32[]{:S(2)}, u32[]{:S(2)}) collective-permute-start(f32[128,128]{1,0:T(8,128)S(1)} %fusion.58), channel_id=1, source_target_pairs={{0,1},{1,2},{2,3},{3,4},{4,5},{5,6},{6,7},{7,0},{8,9},{9,10},{10,1... | collective-permute-start | bytes 196616 | tf_op jit(solution)/shard_map/ppermute | solution.py:13
  355.6 7.4 %collective-permute-start.34 = (f32[128,128]{1,0:T(8,128)S(1)}, f32[128,128]{1,0:T(8,128)S(1)}, u32[]{:S(2)}, u32[]{:S(2)}) collective-permute-start(f32[128,128]{1,0:T(8,128)S(1)} %fusion.55), channel_id=1, source_target_pairs={{0,1},{1,2},{2,3},{3,4},{4,5},{5,6},{6,7},{7,0},{8,9},{9,10},{10,1... | collective-permute-start | bytes 196616 | tf_op jit(solution)/shard_map/ppermute | solution.py:13
  365.4 7.4 %collective-permute-start.36 = (f32[128,128]{1,0:T(8,128)S(1)}, f32[128,128]{1,0:T(8,128)S(1)}, u32[]{:S(2)}, u32[]{:S(2)}) collective-permute-start(f32[128,128]{1,0:T(8,128)S(1)} %fusion.51), channel_id=1, source_target_pairs={{0,1},{1,2},{2,3},{3,4},{4,5},{5,6},{6,7},{7,0},{8,9},{9,10},{10,1... | collective-permute-start | bytes 196616 | tf_op jit(solution)/shard_map/ppermute | solution.py:13
  367.5 7.4 %collective-permute-start.37 = (bf16[128,256]{1,0:T(8,128)(2,1)S(1)}, bf16[128,256]{1,0:T(8,128)(2,1)S(1)}, u32[]{:S(2)}, u32[]{:S(2)}) collective-permute-start(bf16[128,256]{1,0:T(8,128)(2,1)S(1)} %collective-permute-done.35), channel_id=1, source_target_pairs={{0,1},{1,2},{2,3},{3,4},{4,5},{5,6},{6,7},{7,0},{8,9},{9,10},{10,1... | collective-permute-start | bytes 196616 | tf_op jit(solution)/shard_map/ppermute | solution.py:13
  375.2 7.4 %collective-permute-start.38 = (f32[128,128]{1,0:T(8,128)S(1)}, f32[128,128]{1,0:T(8,128)S(1)}, u32[]{:S(2)}, u32[]{:S(2)}) collective-permute-start(f32[128,128]{1,0:T(8,128)S(1)} %fusion.47), channel_id=1, source_target_pairs={{0,1},{1,2},{2,3},{3,4},{4,5},{5,6},{6,7},{7,0},{8,9},{9,10},{10,1... | collective-permute-start | bytes 196616 | tf_op jit(solution)/shard_map/ppermute | solution.py:13
  385.0 7.4 %collective-permute-start.40 = (f32[128,128]{1,0:T(8,128)S(1)}, f32[128,128]{1,0:T(8,128)S(1)}, u32[]{:S(2)}, u32[]{:S(2)}) collective-permute-start(f32[128,128]{1,0:T(8,128)S(1)} %fusion.43), channel_id=1, source_target_pairs={{0,1},{1,2},{2,3},{3,4},{4,5},{5,6},{6,7},{7,0},{8,9},{9,10},{10,1... | collective-permute-start | bytes 196616 | tf_op jit(solution)/shard_map/ppermute | solution.py:13
  387.1 7.4 %collective-permute-start.41 = (bf16[128,256]{1,0:T(8,128)(2,1)S(1)}, bf16[128,256]{1,0:T(8,128)(2,1)S(1)}, u32[]{:S(2)}, u32[]{:S(2)}) collective-permute-start(bf16[128,256]{1,0:T(8,128)(2,1)S(1)} %collective-permute-done.39), channel_id=1, source_target_pairs={{0,1},{1,2},{2,3},{3,4},{4,5},{5,6},{6,7},{7,0},{8,9},{9,10},{10,1... | collective-permute-start | bytes 196616 | tf_op jit(solution)/shard_map/ppermute | solution.py:13
  394.8 7.4 %collective-permute-start.42 = (f32[128,128]{1,0:T(8,128)S(1)}, f32[128,128]{1,0:T(8,128)S(1)}, u32[]{:S(2)}, u32[]{:S(2)}) collective-permute-start(f32[128,128]{1,0:T(8,128)S(1)} %fusion.39), channel_id=1, source_target_pairs={{0,1},{1,2},{2,3},{3,4},{4,5},{5,6},{6,7},{7,0},{8,9},{9,10},{10,1... | collective-permute-start | bytes 196616 | tf_op jit(solution)/shard_map/ppermute | solution.py:13
  396.9 7.4 %collective-permute-start.43 = (bf16[128,256]{1,0:T(8,128)(2,1)S(1)}, bf16[128,256]{1,0:T(8,128)(2,1)S(1)}, u32[]{:S(2)}, u32[]{:S(2)}) collective-permute-start(bf16[128,256]{1,0:T(8,128)(2,1)S(1)} %collective-permute-done.41), channel_id=1, source_target_pairs={{0,1},{1,2},{2,3},{3,4},{4,5},{5,6},{6,7},{7,0},{8,9},{9,10},{10,1... | collective-permute-start | bytes 196616 | tf_op jit(solution)/shard_map/ppermute | solution.py:13
  404.6 7.4 %collective-permute-start.44 = (f32[128,128]{1,0:T(8,128)S(1)}, f32[128,128]{1,0:T(8,128)S(1)}, u32[]{:S(2)}, u32[]{:S(2)}) collective-permute-start(f32[128,128]{1,0:T(8,128)S(1)} %fusion.35), channel_id=1, source_target_pairs={{0,1},{1,2},{2,3},{3,4},{4,5},{5,6},{6,7},{7,0},{8,9},{9,10},{10,1... | collective-permute-start | bytes 196616 | tf_op jit(solution)/shard_map/ppermute | solution.py:13
  406.7 7.4 %collective-permute-start.45 = (bf16[128,256]{1,0:T(8,128)(2,1)S(1)}, bf16[128,256]{1,0:T(8,128)(2,1)S(1)}, u32[]{:S(2)}, u32[]{:S(2)}) collective-permute-start(bf16[128,256]{1,0:T(8,128)(2,1)S(1)} %collective-permute-done.43), channel_id=1, source_target_pairs={{0,1},{1,2},{2,3},{3,4},{4,5},{5,6},{6,7},{7,0},{8,9},{9,10},{10,1... | collective-permute-start | bytes 196616 | tf_op jit(solution)/shard_map/ppermute | solution.py:13
  423.3 17.7 %all-to-all-start.8 = ((bf16[64,2,128]{2,1,0:T(2,128)(2,1)}), bf16[64,2,128]{2,1,0:T(2,128)(2,1)S(1)}, u32[]{:S(2)}, u32[]{:S(2)}) async-start(bf16[64,2,128]{2,1,0:T(2,128)(2,1)} %reshape.500), calls=%async_computation.8 | async-start | bytes 65536 | tf_op jit(solution)/shard_map/all_to_all | solution.py:68
  427.9 24.7 %collective-permute-start.47 = (bf16[128,256]{1,0:T(8,128)(2,1)S(1)}, bf16[128,256]{1,0:T(8,128)(2,1)S(1)}, u32[]{:S(2)}, u32[]{:S(2)}) collective-permute-start(bf16[128,256]{1,0:T(8,128)(2,1)S(1)} %collective-permute-done.45), channel_id=1, source_target_pairs={{0,1},{1,2},{2,3},{3,4},{4,5},{5,6},{6,7},{7,0},{8,9},{9,10},{10,1... | collective-permute-start | bytes 196616 | tf_op jit(solution)/shard_map/ppermute | solution.py:13
  443.1 17.7 %all-to-all-start.9 = ((bf16[64,2,128]{2,1,0:T(2,128)(2,1)}), bf16[64,2,128]{2,1,0:T(2,128)(2,1)S(1)}, u32[]{:S(2)}, u32[]{:S(2)}) async-start(bf16[64,2,128]{2,1,0:T(2,128)(2,1)} %reshape.502), calls=%async_computation.9 | async-start | bytes 65536 | tf_op jit(solution)/shard_map/all_to_all | solution.py:80
  460.8 21.4 %all-to-all-start.10 = ((bf16[64,2,256]{2,1,0:T(2,128)(2,1)}), bf16[64,2,256]{2,1,0:T(2,128)(2,1)S(1)}, u32[]{:S(2)}, u32[]{:S(2)}) async-start(bf16[64,2,256]{2,1,0:T(2,128)(2,1)} %reshape.504), calls=%async_computation.10 | async-start | bytes 131072 | tf_op jit(solution)/shard_map/all_to_all | solution.py:75
  484.5 17.9 %all-to-all-start.11 = ((bf16[64,2,256]{2,1,0:T(2,128)(2,1)}), bf16[64,2,256]{2,1,0:T(2,128)(2,1)S(1)}, u32[]{:S(2)}, u32[]{:S(2)}) async-start(bf16[64,2,256]{2,1,0:T(2,128)(2,1)} %reshape.506), calls=%async_computation.11 | async-start | bytes 131072 | tf_op jit(solution)/shard_map/all_to_all | solution.py:83
  502.8 11.1 %collective-permute-start.49 = (bf16[128,256]{1,0:T(8,128)(2,1)S(1)}, bf16[128,256]{1,0:T(8,128)(2,1)S(1)}, u32[]{:S(2)}, u32[]{:S(2)}) collective-permute-start(bf16[128,256]{1,0:T(8,128)(2,1)S(1)} %reshape.336), channel_id=1, source_target_pairs={{0,1},{1,2},{2,3},{3,4},{4,5},{5,6},{6,7},{7,0},{8,9},{9,10},{10,1... | collective-permute-start | bytes 196616 | tf_op jit(solution)/shard_map/ppermute | solution.py:13
  507.2 9.2 %collective-permute-start.48 = (f32[128,128]{1,0:T(8,128)S(1)}, f32[128,128]{1,0:T(8,128)S(1)}, u32[]{:S(2)}, u32[]{:S(2)}) collective-permute-start(f32[128,128]{1,0:T(8,128)S(1)} %fusion.27), channel_id=1, source_target_pairs={{0,1},{1,2},{2,3},{3,4},{4,5},{5,6},{6,7},{7,0},{8,9},{9,10},{10,1... | collective-permute-start | bytes 196616 | tf_op jit(solution)/shard_map/ppermute | solution.py:13
  516.7 7.4 %collective-permute-start.50 = (f32[128,128]{1,0:T(8,128)S(1)}, f32[128,128]{1,0:T(8,128)S(1)}, u32[]{:S(2)}, u32[]{:S(2)}) collective-permute-start(f32[128,128]{1,0:T(8,128)S(1)} %fusion.24), channel_id=1, source_target_pairs={{0,1},{1,2},{2,3},{3,4},{4,5},{5,6},{6,7},{7,0},{8,9},{9,10},{10,1... | collective-permute-start | bytes 196616 | tf_op jit(solution)/shard_map/ppermute | solution.py:13
  526.5 7.4 %collective-permute-start.52 = (f32[128,128]{1,0:T(8,128)S(1)}, f32[128,128]{1,0:T(8,128)S(1)}, u32[]{:S(2)}, u32[]{:S(2)}) collective-permute-start(f32[128,128]{1,0:T(8,128)S(1)} %fusion.20), channel_id=1, source_target_pairs={{0,1},{1,2},{2,3},{3,4},{4,5},{5,6},{6,7},{7,0},{8,9},{9,10},{10,1... | collective-permute-start | bytes 196616 | tf_op jit(solution)/shard_map/ppermute | solution.py:13
  528.6 7.4 %collective-permute-start.53 = (bf16[128,256]{1,0:T(8,128)(2,1)S(1)}, bf16[128,256]{1,0:T(8,128)(2,1)S(1)}, u32[]{:S(2)}, u32[]{:S(2)}) collective-permute-start(bf16[128,256]{1,0:T(8,128)(2,1)S(1)} %collective-permute-done.51), channel_id=1, source_target_pairs={{0,1},{1,2},{2,3},{3,4},{4,5},{5,6},{6,7},{7,0},{8,9},{9,10},{10,1... | collective-permute-start | bytes 196616 | tf_op jit(solution)/shard_map/ppermute | solution.py:13
  536.3 7.4 %collective-permute-start.54 = (f32[128,128]{1,0:T(8,128)S(1)}, f32[128,128]{1,0:T(8,128)S(1)}, u32[]{:S(2)}, u32[]{:S(2)}) collective-permute-start(f32[128,128]{1,0:T(8,128)S(1)} %fusion.16), channel_id=1, source_target_pairs={{0,1},{1,2},{2,3},{3,4},{4,5},{5,6},{6,7},{7,0},{8,9},{9,10},{10,1... | collective-permute-start | bytes 196616 | tf_op jit(solution)/shard_map/ppermute | solution.py:13
  546.1 7.4 %collective-permute-start.56 = (f32[128,128]{1,0:T(8,128)S(1)}, f32[128,128]{1,0:T(8,128)S(1)}, u32[]{:S(2)}, u32[]{:S(2)}) collective-permute-start(f32[128,128]{1,0:T(8,128)S(1)} %fusion.12), channel_id=1, source_target_pairs={{0,1},{1,2},{2,3},{3,4},{4,5},{5,6},{6,7},{7,0},{8,9},{9,10},{10,1... | collective-permute-start | bytes 196616 | tf_op jit(solution)/shard_map/ppermute | solution.py:13
  548.2 7.4 %collective-permute-start.57 = (bf16[128,256]{1,0:T(8,128)(2,1)S(1)}, bf16[128,256]{1,0:T(8,128)(2,1)S(1)}, u32[]{:S(2)}, u32[]{:S(2)}) collective-permute-start(bf16[128,256]{1,0:T(8,128)(2,1)S(1)} %collective-permute-done.55), channel_id=1, source_target_pairs={{0,1},{1,2},{2,3},{3,4},{4,5},{5,6},{6,7},{7,0},{8,9},{9,10},{10,1... | collective-permute-start | bytes 196616 | tf_op jit(solution)/shard_map/ppermute | solution.py:13
  555.9 7.4 %collective-permute-start.58 = (f32[128,128]{1,0:T(8,128)S(1)}, f32[128,128]{1,0:T(8,128)S(1)}, u32[]{:S(2)}, u32[]{:S(2)}) collective-permute-start(f32[128,128]{1,0:T(8,128)S(1)} %fusion.8), channel_id=1, source_target_pairs={{0,1},{1,2},{2,3},{3,4},{4,5},{5,6},{6,7},{7,0},{8,9},{9,10},{10,1... | collective-permute-start | bytes 196616 | tf_op jit(solution)/shard_map/ppermute | solution.py:13
  558.0 7.4 %collective-permute-start.59 = (bf16[128,256]{1,0:T(8,128)(2,1)S(1)}, bf16[128,256]{1,0:T(8,128)(2,1)S(1)}, u32[]{:S(2)}, u32[]{:S(2)}) collective-permute-start(bf16[128,256]{1,0:T(8,128)(2,1)S(1)} %collective-permute-done.57), channel_id=1, source_target_pairs={{0,1},{1,2},{2,3},{3,4},{4,5},{5,6},{6,7},{7,0},{8,9},{9,10},{10,1... | collective-permute-start | bytes 196616 | tf_op jit(solution)/shard_map/ppermute | solution.py:13
  565.7 7.4 %collective-permute-start.60 = (f32[128,128]{1,0:T(8,128)S(1)}, f32[128,128]{1,0:T(8,128)S(1)}, u32[]{:S(2)}, u32[]{:S(2)}) collective-permute-start(f32[128,128]{1,0:T(8,128)S(1)} %fusion.4), channel_id=1, source_target_pairs={{0,1},{1,2},{2,3},{3,4},{4,5},{5,6},{6,7},{7,0},{8,9},{9,10},{10,1... | collective-permute-start | bytes 196616 | tf_op jit(solution)/shard_map/ppermute | solution.py:13
  575.5 7.4 %collective-permute-start.62 = (f32[128,128]{1,0:T(8,128)S(1)}, f32[128,128]{1,0:T(8,128)S(1)}, u32[]{:S(2)}, u32[]{:S(2)}) collective-permute-start(f32[128,128]{1,0:T(8,128)S(1)} %fusion), channel_id=1, source_target_pairs={{0,1},{1,2},{2,3},{3,4},{4,5},{5,6},{6,7},{7,0},{8,9},{9,10},{10,1... | collective-permute-start | bytes 196616 | tf_op jit(solution)/shard_map/ppermute | solution.py:13
  (15 other events, 87.9 us)
where the time goes:
time: 589 us; the launch traced here: 584 us
  waiting for transfers between devices  297 us (50%)
  starting transfers between devices  209 us (35%)
  between operations  24.3 us (4%)
  local copies, waits for them, and re-layouts  20.2 us (3%)
  matrix products  20.1 us (3%)
  other arithmetic  13.1 us (2%)
    ppermute x63, waiting for transfers between devices, passed_along(): lax.ppermute(array, axis, [(i, (i + by) % length) for i in range(length)])  168 us
    ppermute x63, starting transfers between devices, passed_along(): lax.ppermute(array, axis, [(i, (i + by) % length) for i in range(length)])  132 us
    all_to_all x3, waiting for transfers between devices, local(): lax.all_to_all(chosen_x, 'grp', split_axis=0, concat_axis=0, tiled=True)  39.4 us
    all_to_all x3, waiting for transfers between devices, local(): lax.all_to_all(carried_x.reshape(groups, -1), 'grp', split_axis=0, concat...  38.7 us
    all_to_all x3, waiting for transfers between devices, local(): lax.all_to_all(right_factor.reshape(groups, -1).astype(jnp.bfloat16), 'gr...  33.7 us
    all_to_all x3, starting transfers between devices, local(): lax.all_to_all(carried_x.reshape(groups, -1), 'grp', split_axis=0, concat...  26.7 us
    all_to_all x3, starting transfers between devices, local(): lax.all_to_all(right_factor.reshape(groups, -1).astype(jnp.bfloat16), 'gr...  22.7 us
    all_to_all x3, waiting for transfers between devices, local(): lax.all_to_all(chosen_v.astype(jnp.bfloat16), 'grp', split_axis=0, concat...  17.2 us
  transfers between devices with their start and end apart: 75, of which 71 were waited for; matrix products, arithmetic and copies ran while one was open for 5% of the time, Pallas kernels for 0%

commit v1 on v0

v1 whole, which is shorter than its diff:
```python
import functools

import jax
import jax.numpy as jnp
from jax import lax
from jax.experimental import pallas as pl
from jax.experimental.pallas import tpu as pltpu
from jax.sharding import Mesh, PartitionSpec as P

SUB = 4
GRP = ("yh", "x", "z")
BLK = ("yl", "core")
ALL = GRP + BLK
BF = jnp.bfloat16
F32 = jnp.float32
LANES = 128
SMEM = pl.BlockSpec(memory_space=pltpu.SMEM)
VMEM = pl.BlockSpec(memory_space=pltpu.VMEM)


def tables_kernel(groups, leaves, levels, matching_ref, leaf_ref, node_ref, held_ref, inv_ref):
    def invert(e, carry):
        for t in range(levels - 1):
            inv_ref[t * groups + matching_ref[t, e]] = e
        return carry

    lax.fori_loop(0, groups, invert, 0)

    def trace_back(d, carry):
        held = [d]
        for t in range(1, levels):
            e = d
            for s in range(t - 1, -1, -1):
                e = inv_ref[s * groups + e]
            held.append(e)
        for t in range(levels):
            held_ref[t * groups + d] = held[t]
        nodes = {(): d}
        for t in range(levels - 2, -1, -1):
            for path in [p for p in nodes if len(p) == levels - 2 - t]:
                nodes[path + (0,)] = nodes[path]
                nodes[path + (1,)] = inv_ref[t * groups + nodes[path]]
        for k in range(leaves):
            bits = tuple((k >> (levels - 2 - i)) & 1 for i in range(levels - 1))
            leaf_ref[d * leaves + k] = nodes[bits]
            for t in range(levels):
                node_ref[(d * leaves + k) * levels + t] = nodes[bits[: levels - 1 - t]]
        return carry

    lax.fori_loop(0, groups, trace_back, 0)


def tables_call(matching, leaves):
    levels, groups = matching.shape[0] + 1, matching.shape[1]
    return pl.pallas_call(
        functools.partial(tables_kernel, groups, leaves, levels),
        out_shape=(
            jax.ShapeDtypeStruct((groups * leaves,), jnp.int32),
            jax.ShapeDtypeStruct((groups * leaves * levels,), jnp.int32),
            jax.ShapeDtypeStruct((groups * levels,), jnp.int32),
        ),
        in_specs=[SMEM],
        out_specs=(SMEM, SMEM, SMEM),
        scratch_shapes=[pltpu.SMEM((groups * (levels - 1),), jnp.int32)],
        cost_estimate=pl.CostEstimate(flops=2000000, bytes_accessed=4096, transcendentals=0),
    )(matching)


def pick_kernel(leaves, leaf_ref, pieces_ref, out_ref):
    def one(d, carry):
        for k in range(leaves):
            out_ref[d, k] = pieces_ref[leaf_ref[d * leaves + k]]
        return carry

    lax.fori_loop(0, out_ref.shape[0], one, 0)


def pick_call(leaf_table, pieces, leaves):
    groups = pieces.shape[0]
    return pl.pallas_call(
        functools.partial(pick_kernel, leaves),
        out_shape=jax.ShapeDtypeStruct((groups, leaves) + pieces.shape[1:], pieces.dtype),
        in_specs=[SMEM, VMEM],
        out_specs=VMEM,
        compiler_params=pltpu.CompilerParams(vmem_limit_bytes=16 << 20),
        cost_estimate=pl.CostEstimate(flops=1000000, bytes_accessed=2 << 20, transcendentals=0),
    )(leaf_table, pieces)


def sub_epoch_kernel(blocks, step_size, level, last, info_ref, keep_ref, *refs):
    if level == 0:
        x_ref, uv_ref, *refs = refs
    else:
        left_ref, right_ref, xl_ref, xr_ref, *refs = refs
    *outs, ls, rs, lb, rb = refs
    rank = ls.shape[2]
    for b in range(blocks):
        if level == 0:
            left, right = uv_ref[b, 0], uv_ref[b, 1]
            ls[b], rs[b] = left.astype(F32), right.astype(F32)
            lx = rx = x_ref
        else:
            left, right = left_ref[b].astype(BF), right_ref[b]
            ls[b], rs[b] = left_ref[b], right.astype(F32)
            lx, rx = xl_ref, xr_ref
        lb[b, :, :rank], rb[b, :, :rank] = left, right
        for half in range(2):
            span = slice((half + 1) * rank, (half + 2) * rank)
            lb[b, :, span] = lx[b, half]
            rb[b, :, span] = -rx[b, half]
    flip = info_ref[1 + level]

    def cycle_step(step, carry):
        shift = jnp.where(flip == 1, step, blocks - step)
        places = [lax.rem(b + shift, blocks) for b in range(blocks)]
        diffs = [
            lax.dot_general(lb[b], rb[places[b]], (((1,), (1,)), ((), ())), preferred_element_type=F32)
            for b in range(blocks)
        ]
        resids = []
        for b in range(blocks):
            row = jnp.where(flip == 1, places[b], b)
            col = jnp.where(flip == 1, b, places[b])
            resids.append((keep_ref[row, level * blocks + col] * diffs[b]).astype(BF))
        grads_l = [
            jnp.dot(resids[b], rb[places[b], :, :rank], preferred_element_type=F32) for b in range(blocks)
        ]
        grads_r = [
            lax.dot_general(resids[b], lb[b, :, :rank], (((0,), (0,)), ((), ())), preferred_element_type=F32)
            for b in range(blocks)
        ]
        for b in range(blocks):
            new_left = ls[b] - step_size * grads_l[b]
            ls[b] = new_left
            lb[b, :, :rank] = new_left.astype(BF)
        for b in range(blocks):
            new_right = rs[places[b]] - step_size * grads_r[b]
            rs[places[b]] = new_right
            rb[places[b], :, :rank] = new_right.astype(BF)
        return carry

    lax.fori_loop(0, blocks, cycle_step, 0)
    me = info_ref[0]
    if last:
        uo_ref, vo_ref = outs

        @pl.when(flip == 0)
        def _():
            uo_ref[...] = ls[me]
            vo_ref[...] = rs[me]

        @pl.when(flip == 1)
        def _():
            uo_ref[...] = rs[me]
            vo_ref[...] = ls[me]
    else:
        kept_ref, sent_ref = outs
        same = info_ref[2 + level] == flip

        @pl.when(same)
        def _():
            kept_ref[...] = ls[...]
            sent_ref[...] = lb[:, :, :rank]

        @pl.when(jnp.logical_not(same))
        def _():
            kept_ref[...] = rs[...]
            sent_ref[...] = rb[:, :, :rank]


def sub_epoch_call(level, last, info, keeps, *arrays):
    blocks, _, slot_rows, rank = arrays[-1].shape
    whole = (blocks, slot_rows, rank)
    if last:
        outs = (jax.ShapeDtypeStruct((slot_rows, rank), F32),) * 2
    else:
        outs = (jax.ShapeDtypeStruct(whole, F32), jax.ShapeDtypeStruct(whole, BF))
    state, operand = pltpu.VMEM(whole, F32), pltpu.VMEM((blocks, slot_rows, 3 * rank), BF)
    return pl.pallas_call(
        functools.partial(sub_epoch_kernel, blocks, 4.0 / slot_rows, level, last),
        out_shape=outs,
        in_specs=[SMEM, SMEM] + [VMEM] * len(arrays),
        out_specs=(VMEM, VMEM),
        scratch_shapes=[state, state, operand, operand],
        compiler_params=pltpu.CompilerParams(vmem_limit_bytes=24 << 20),
        cost_estimate=pl.CostEstimate(
            flops=2 * blocks * blocks * slot_rows * slot_rows * 5 * rank,
            bytes_accessed=4 << 20,
            transcendentals=0,
        ),
    )(info, keeps, *arrays)


def swapped(array, bit, count):
    return lax.ppermute(array, BLK, [(i, i ^ (1 << bit)) for i in range(count)])


def local(features, factor_u, factor_v, tile_mask, matching):
    groups = lax.axis_size(GRP)
    blocks = lax.axis_size(BLK)
    group = lax.axis_index(GRP)
    part = lax.axis_index(BLK).astype(jnp.int32)
    slot_rows, rank = factor_u.shape
    piece_rows = 4 * slot_rows // groups

    packed = jnp.concatenate([features[:, :rank], features[:, rank:], factor_u, factor_v], axis=0).astype(BF)
    pieces = packed.reshape(groups, piece_rows, rank)
    pieces = lax.all_to_all(pieces, GRP, split_axis=0, concat_axis=0, tiled=True)

    leaf_table, node_table, held_table = tables_call(matching, blocks)
    held = lax.dynamic_index_in_dim(held_table.reshape(SUB, groups), group, 1, keepdims=False)
    row = jnp.take(tile_mask.reshape(groups, blocks).astype(F32), held, axis=0).reshape(1, 1, SUB * blocks)
    row = jnp.broadcast_to(jnp.pad(row, ((0, 0), (0, 0), (0, LANES - SUB * blocks))), (groups, 1, LANES))
    rows = lax.all_to_all(row, GRP, split_axis=0, concat_axis=0, tiled=True)[:, 0, : SUB * blocks]
    nodes = lax.dynamic_index_in_dim(node_table.reshape(groups, blocks * SUB), group, 0, keepdims=False)
    picked = jnp.take(rows, nodes, axis=0).reshape(blocks, SUB, SUB, blocks)
    picked = jnp.stack([picked[:, t, t] for t in range(SUB)], axis=1).reshape(blocks, 1, SUB * blocks)
    picked = jnp.pad(picked, ((0, 0), (0, 0), (0, LANES - SUB * blocks)))
    keeps = lax.all_to_all(picked, BLK, split_axis=0, concat_axis=0, tiled=True)[:, 0, : SUB * blocks]

    sends = pick_call(leaf_table, pieces, blocks)
    got = lax.all_to_all(sends, GRP, split_axis=0, concat_axis=0, tiled=True)
    got = jnp.transpose(got, (1, 0, 2, 3))
    half = groups // 2
    x = lax.all_to_all(got[:, :half], BLK, split_axis=0, concat_axis=0, tiled=True)
    uv = lax.all_to_all(got[:, half:], BLK, split_axis=0, concat_axis=0, tiled=True)
    x = x.reshape(blocks, 2, slot_rows, rank)
    uv = uv.reshape(blocks, 2, slot_rows, rank)

    bits = [(part >> t) & 1 for t in range(SUB - 1)]
    info = jnp.stack([part, jnp.zeros((), jnp.int32)] + bits)
    kept, sent = sub_epoch_call(0, False, info, keeps, x, uv)
    left_x = x
    for level in range(1, SUB):
        right_x = swapped(left_x, level - 1, blocks)
        right = swapped(sent, level - 1, blocks)
        last = level + 1 == SUB
        kept, sent = sub_epoch_call(level, last, info, keeps, kept, right, left_x, right_x)
        if not last:
            left_x = jnp.where(bits[level] == bits[level - 1], left_x, right_x)
    return kept, sent


def solution(mesh):
    fine = Mesh(mesh.devices.reshape(2, 4, 8, 4, 2), ALL)
    in_specs = (P(ALL, None), P(ALL, None), P(ALL, None), P(ALL, None), P())
    out_specs = (P(ALL, None), P(ALL, None))
    return jax.shard_map(local, mesh=fine, in_specs=in_specs, out_specs=out_specs, check_vma=False)
```

time: 589 us -> 213 us (0.36)
  waiting for transfers between devices: 297 us -> 99.1 us
  starting transfers between devices: 209 us -> 68.7 us
  Pallas kernels: 0 us -> 33.9 us
  between operations: 24.3 us -> 0.91 us
  matrix products: 20.1 us -> 0 us
  local copies, waits for them, and re-layouts: 20.2 us -> 7.06 us
  other arithmetic: 13.1 us -> 2.26 us
    ppermute x63 -> x6, waiting for transfers between devices: 168 us -> 28 us  [swapped(): return lax.ppermute(array, BLK, [(i, i ^ 1 << bit) for i in range(count)])]
    ppermute x63 -> x6, starting transfers between devices: 132 us -> 15.9 us  [swapped(): return lax.ppermute(array, BLK, [(i, i ^ 1 << bit) for i in range(count)])]
    all_to_all x12 -> x6, waiting for transfers between devices: 129 us -> 71.1 us  [the longest x1 21.3 us: local(): got = lax.all_to_all(sends, GRP, split_axis=0, concat_axis=0, tiled=True)]
    pallas_call x0 -> x6, Pallas kernels: none -> 33.9 us  [the longest x4 26.9 us: sub_epoch_call(): pl.pallas_call(functools.partial(sub_epoch_kernel, blocks, 4.0 / slot_row...]
    all_to_all x12 -> x6, starting transfers between devices: 77 us -> 52.8 us  [the longest x1 19.6 us: local(): lax.all_to_all(pieces, GRP, split_axis=0, concat_axis=0, tiled=True)]
    dot_general x128 -> x0, matrix products: 20.1 us -> none  [the longest x64 9.25 us: pair_rows(): lax.dot_general(left_rows, right_rows, (((1,), (1,)), ((), ())), preferre...]
    all_to_all x21 -> x0, other arithmetic: 9.36 us -> none  [the longest x9 3.42 us: local(): lax.all_to_all(chosen_x, 'grp', split_axis=0, concat_axis=0, tiled=True)]
    unnamed x36 -> x12, local copies, waits for them, and re-layouts: 9.47 us -> 2.02 us
  transfers between devices with their start and end apart: 75 -> 12, of which waited for: 71 -> 9; matrix products, arithmetic and copies ran while one was open for 5% -> 2% of each run, Pallas kernels for 0% -> 11%
where the time goes in v1:
time: 213 us; the launch traced here: 212 us
  waiting for transfers between devices  99.1 us (47%)
  starting transfers between devices  68.7 us (32%)
  Pallas kernels  33.9 us (16%)
  local copies, waits for them, and re-layouts  7.06 us (3%)
  other arithmetic  2.26 us (1%)
    ppermute x6, waiting for transfers between devices, swapped(): return lax.ppermute(array, BLK, [(i, i ^ 1 << bit) for i in range(count)])  28 us
    pallas_call x4, Pallas kernels, sub_epoch_call(): pl.pallas_call(functools.partial(sub_epoch_kernel, blocks, 4.0 / slot_row...  26.9 us
    all_to_all x1, waiting for transfers between devices, local(): got = lax.all_to_all(sends, GRP, split_axis=0, concat_axis=0, tiled=True)  21.3 us
    all_to_all x1, starting transfers between devices, local(): lax.all_to_all(pieces, GRP, split_axis=0, concat_axis=0, tiled=True)  19.6 us
    ppermute x6, starting transfers between devices, swapped(): return lax.ppermute(array, BLK, [(i, i ^ 1 << bit) for i in range(count)])  15.9 us
    all_to_all x1, starting transfers between devices, local(): lax.all_to_all(row, GRP, split_axis=0, concat_axis=0, tiled=True)  14.9 us
    all_to_all x1, waiting for transfers between devices, local(): lax.all_to_all(got[:, :half], BLK, split_axis=0, concat_axis=0, tiled=True)  13.6 us
    all_to_all x1, waiting for transfers between devices, local(): lax.all_to_all(row, GRP, split_axis=0, concat_axis=0, tiled=True)  12.2 us
  transfers between devices with their start and end apart: 12, of which 9 were waited for; matrix products, arithmetic and copies ran while one was open for 2% of the time, Pallas kernels for 11%

profile of v1, /device:TPU:1, one launch (start us, length us, event | category | flops | bytes accessed | tf_op | source)
XLA Modules:
  0.0 212.0 jit_solution(12641618701512876329)
XLA Ops:
  0.6 0.0 copy-start.2
  0.6 0.0 copy-start.1
  0.6 0.9 convert.13
  1.5 0.0 copy-done.2
  1.5 0.1 copy-done.1
  1.6 0.7 maximum_bitcast_fusion
  2.3 19.6 %all-to-all-start.2 = ((bf16[64,8,128]{2,1,0:T(8,128)(2,1)}), bf16[64,8,128]{2,1,0:T(8,128)(2,1)S(1)}, u32[]{:S(2)}, u32[]{:S(2)}) async-start(bf16[64,8,128]{2,1,0:T(8,128)(2,1)} %maximum_bitcast_fusion), calls=%async_computation.2 | async-start | bytes 262144 | tf_op jit(solution)/shard_map/all_to_all | solution.py:208
  21.9 4.5 %shard_map.68 = (s32[512]{0:T(512)}, s32[2048]{0:T(1024)}, s32[256]{0:T(256)}) custom-call(s32[3,64]{1,0:T(4,128)} %matching_ref.1), custom_call_target="tpu_custom_call" | custom-call | flops 2000000 | bytes 4096 | tf_op jit(solution)/shard_map/pallas_call | solution.py:55
  26.4 9.1 %all-to-all-done.2.pieces_ref = bf16[64,8,128]{2,1,0:T(8,128)(2,1)S(1)} async-done(((bf16[64,8,128]{2,1,0:T(8,128)(2,1)}), bf16[64,8,128]{2,1,0:T(8,128)(2,1)S(1)}, u32[]{:S(2)}, u32[]{:S(2)}) %all-to-all-start.2) | async-done | bytes 131104 | tf_op jit(solution)/shard_map/all_to_all | solution.py:208
  35.5 0.7 copy-done
  36.2 2.5 %shard_map.69 = bf16[64,8,8,128]{3,2,1,0:T(8,128)(2,1)} custom-call(s32[512]{0:T(512)S(1)} %copy-done, bf16[64,8,128]{2,1,0:T(8,128)(2,1)S(1)} %all-to-all-done.2.pieces_ref), custom_call_target="tpu_custom_call" | custom-call | flops 1000000 | bytes 2097152 | tf_op jit(solution)/shard_map/pallas_call | solution.py:80
  38.6 5.6 %all-to-all-start.3 = ((bf16[64,8,8,128]{3,2,1,0:T(8,128)(2,1)}), bf16[64,8,8,128]{3,2,1,0:T(8,128)(2,1)S(1)}, u32[]{:S(2)}, u32[]{:S(2)}) async-start(bf16[64,8,8,128]{3,2,1,0:T(8,128)(2,1)} %shard_map.69), calls=%async_computation.3 | async-start | bytes 2097152 | tf_op jit(solution)/shard_map/all_to_all | solution.py:222
  44.2 0.0 copy-start.3
  44.3 0.0 copy-start.5
  44.3 0.7 copy-done.5
  44.9 0.1 reshape.94
  45.0 0.0 copy-done.3
  45.0 0.1 reshape.93
  45.1 0.1 squeeze.14
  45.2 0.6 copy-done.4
  45.8 0.1 convert_element_type.16
  45.9 0.2 fusion
  46.1 0.6 gather_fusion
  46.7 0.2 and_reduce_fusion
  46.9 0.1 broadcast_select_fusion.2
  46.9 0.1 select_n.67
  47.0 21.3 %all-to-all-done.3 = bf16[64,8,8,128]{3,2,1,0:T(8,128)(2,1)S(1)} async-done(((bf16[64,8,8,128]{3,2,1,0:T(8,128)(2,1)}), bf16[64,8,8,128]{3,2,1,0:T(8,128)(2,1)S(1)}, u32[]{:S(2)}, u32[]{:S(2)}) %all-to-all-start.3) | async-done | bytes 1048608 | tf_op jit(solution)/shard_map/all_to_all | solution.py:222
  68.4 0.6 broadcast_in_dim.31
  69.0 14.9 %all-to-all-start = ((f32[64,1,128]{2,1,0:T(1,128)}), f32[64,1,128]{2,1,0:T(1,128)S(1)}, u32[]{:S(2)}, u32[]{:S(2)}) async-start(f32[64,1,128]{2,1,0:T(1,128)} %broadcast_in_dim.31), calls=%async_computation | async-start | bytes 65536 | tf_op jit(solution)/shard_map/all_to_all | solution.py:214
  83.9 0.1 fusion.3
  84.0 0.9 copy.34
  84.9 12.2 %all-to-all-done = f32[64,1,128]{2,1,0:T(1,128)S(1)} async-done(((f32[64,1,128]{2,1,0:T(1,128)}), f32[64,1,128]{2,1,0:T(1,128)S(1)}, u32[]{:S(2)}, u32[]{:S(2)}) %all-to-all-start) | async-done | bytes 32800 | tf_op jit(solution)/shard_map/all_to_all | solution.py:214
  97.0 5.4 %all-to-all-start.4 = ((bf16[8,32,8,128]{3,2,1,0:T(8,128)(2,1)}), bf16[8,32,8,128]{3,2,1,0:T(8,128)(2,1)S(1)}, u32[]{:S(2)}, u32[]{:S(2)}) async-start(bf16[8,32,8,128]{3,2,1,0:T(8,128)(2,1)} %copy.34), calls=%async_computation.4 | async-start | bytes 1048576 | tf_op jit(solution)/shard_map/all_to_all | solution.py:225
  102.4 0.1 copy.28
  102.5 0.6 gather_fusion.1
  103.1 0.1 gather.12
  103.2 0.1 copy_select_fusion
  103.3 13.6 %all-to-all-done.4 = bf16[8,32,8,128]{3,2,1,0:T(8,128)(2,1)S(1)} async-done(((bf16[8,32,8,128]{3,2,1,0:T(8,128)(2,1)}), bf16[8,32,8,128]{3,2,1,0:T(8,128)(2,1)S(1)}, u32[]{:S(2)}, u32[]{:S(2)}) %all-to-all-start.4) | async-done | bytes 524320 | tf_op jit(solution)/shard_map/all_to_all | solution.py:225
  116.9 2.8 %collective-permute-start.1 = (bf16[8,2,128,128]{3,2,1,0:T(8,128)(2,1)S(1)}, bf16[8,2,128,128]{3,2,1,0:T(8,128)(2,1)S(1)}, u32[]{:S(2)}, u32[]{:S(2)}) collective-permute-start(bf16[8,2,128,128]{3,2,1,0:T(8,128)(2,1)S(1)} %bitcast.32), channel_id=1, source_target_pairs={{0,1},{1,0},{2,3},{3,2},{4,5},{5,4},{6,7},{7,6},{8,9},{9,8},{10,11... | collective-permute-start | bytes 1572872 | tf_op jit(solution)/shard_map/ppermute | solution.py:195
  119.7 0.1 reshape.95
  119.8 0.6 pad.9
  120.4 3.3 %all-to-all-start.1 = ((f32[8,1,128]{2,1,0:T(1,128)}), f32[8,1,128]{2,1,0:T(1,128)S(1)}, u32[]{:S(2)}, u32[]{:S(2)}) async-start(f32[8,1,128]{2,1,0:T(1,128)} %bitcast.13), calls=%async_computation.1 | async-start | bytes 8192 | tf_op jit(solution)/shard_map/all_to_all | solution.py:219
  123.6 0.9 copy.35
  124.5 3.9 %all-to-all-done.1 = f32[8,1,128]{2,1,0:T(1,128)S(1)} async-done(((f32[8,1,128]{2,1,0:T(1,128)}), f32[8,1,128]{2,1,0:T(1,128)S(1)}, u32[]{:S(2)}, u32[]{:S(2)}) %all-to-all-start.1) | async-done | bytes 4128 | tf_op jit(solution)/shard_map/all_to_all | solution.py:219
  128.4 4.1 %all-to-all-start.5 = ((bf16[8,32,8,128]{3,2,1,0:T(8,128)(2,1)}), bf16[8,32,8,128]{3,2,1,0:T(8,128)(2,1)S(1)}, u32[]{:S(2)}, u32[]{:S(2)}) async-start(bf16[8,32,8,128]{3,2,1,0:T(8,128)(2,1)} %copy.35), calls=%async_computation.5 | async-start | bytes 1048576 | tf_op jit(solution)/shard_map/all_to_all | solution.py:226
  132.5 0.1 stack.22.info_ref
  132.6 0.0 collective-permute-done.1.refs_3_
  132.6 0.1 broadcast_select_fusion.1.refs_2_
  132.7 3.3 %collective-permute-start.3 = (bf16[8,2,128,128]{3,2,1,0:T(8,128)(2,1)S(1)}, bf16[8,2,128,128]{3,2,1,0:T(8,128)(2,1)S(1)}, u32[]{:S(2)}, u32[]{:S(2)}) collective-permute-start(bf16[8,2,128,128]{3,2,1,0:T(8,128)(2,1)S(1)} %broadcast_select_fusion.1.refs_2_), channel_id=1, source_target_pairs={{0,2},{1,3},{2,0},{3,1},{4,6},{5,7},{6,4},{7,5},{8,10},{9,11},{10,... | collective-permute-start | bytes 1572872 | tf_op jit(solution)/shard_map/ppermute | solution.py:195
  136.0 11.0 %all-to-all-done.5 = bf16[8,32,8,128]{3,2,1,0:T(8,128)(2,1)S(1)} async-done(((bf16[8,32,8,128]{3,2,1,0:T(8,128)(2,1)}), bf16[8,32,8,128]{3,2,1,0:T(8,128)(2,1)S(1)}, u32[]{:S(2)}, u32[]{:S(2)}) %all-to-all-start.5) | async-done | bytes 524320 | tf_op jit(solution)/shard_map/all_to_all | solution.py:226
  147.0 6.6 %shard_map.70 = (f32[8,128,128]{2,1,0:T(8,128)S(1)}, bf16[8,128,128]{2,1,0:T(8,128)(2,1)S(1)}) custom-call(s32[5]{0:T(128)S(1)} %stack.22.info_ref, f32[8,32]{1,0:T(8,128)S(1)} %slice_bitcast_fusion.5.keep_ref, bf16[8,2,128,128]{3,2,1,0:T(8,128)(2,1)S(1)} %bitcast.34, bf16[8,2,128,128]{3,2,1,0:T(8,128)(2,1)S(1)} %bitcast.36), custom_call_target="tpu_custom_call" | custom-call | flops 1342177280 | bytes 4194304 | tf_op jit(solution)/shard_map/pallas_call | solution.py:179
  153.6 2.9 %collective-permute-start = (bf16[8,128,128]{2,1,0:T(8,128)(2,1)S(1)}, bf16[8,128,128]{2,1,0:T(8,128)(2,1)S(1)}, u32[]{:S(2)}, u32[]{:S(2)}) collective-permute-start(bf16[8,128,128]{2,1,0:T(8,128)(2,1)S(1)} %get-tuple-element.15), channel_id=1, source_target_pairs={{0,1},{1,0},{2,3},{3,2},{4,5},{5,4},{6,7},{7,6},{8,9},{9,8},{10,11... | collective-permute-start | bytes 786440 | tf_op jit(solution)/shard_map/ppermute | solution.py:195
  156.5 1.1 collective-permute-done.refs_1_
  157.6 6.6 %shard_map.71 = (f32[8,128,128]{2,1,0:T(8,128)S(1)}, bf16[8,128,128]{2,1,0:T(8,128)(2,1)S(1)}) custom-call(s32[5]{0:T(128)S(1)} %stack.22.info_ref, f32[8,32]{1,0:T(8,128)S(1)} %slice_bitcast_fusion.5.keep_ref, f32[8,128,128]{2,1,0:T(8,128)S(1)} %get-tuple-element.14.refs_0_, bf16[8,128,128]{2,1,0:T(8,128)(2,1)S(1)} %collective-permute-done.refs_1_, ...), custom_call_target="tpu_custom_call" | custom-call | flops 1342177280 | bytes 4194304 | tf_op jit(solution)/shard_map/pallas_call | solution.py:179
  164.2 1.9 collective-permute-start.2
  166.2 0.0 collective-permute-done.3.refs_3_
  166.2 0.1 broadcast_select_fusion.refs_2_
  166.2 3.2 %collective-permute-start.5 = (bf16[8,2,128,128]{3,2,1,0:T(8,128)(2,1)S(1)}, bf16[8,2,128,128]{3,2,1,0:T(8,128)(2,1)S(1)}, u32[]{:S(2)}, u32[]{:S(2)}) collective-permute-start(bf16[8,2,128,128]{3,2,1,0:T(8,128)(2,1)S(1)} %broadcast_select_fusion.refs_2_), channel_id=1, source_target_pairs={{0,4},{1,5},{2,6},{3,7},{4,0},{5,1},{6,2},{7,3},{8,12},{9,13},{10,... | collective-permute-start | bytes 1572872 | tf_op jit(solution)/shard_map/ppermute | solution.py:195
  169.4 6.6 %collective-permute-done.2.refs_1_ = bf16[8,128,128]{2,1,0:T(8,128)(2,1)S(1)} collective-permute-done((bf16[8,128,128]{2,1,0:T(8,128)(2,1)S(1)}, bf16[8,128,128]{2,1,0:T(8,128)(2,1)S(1)}, u32[]{:S(2)}, u32[]{:S(2)}) %collective-permute-start.2) | collective-permute-done | bytes 262176 | tf_op jit(solution)/shard_map/ppermute | solution.py:195
  176.0 6.6 %shard_map.72 = (f32[8,128,128]{2,1,0:T(8,128)S(1)}, bf16[8,128,128]{2,1,0:T(8,128)(2,1)S(1)}) custom-call(s32[5]{0:T(128)S(1)} %stack.22.info_ref, f32[8,32]{1,0:T(8,128)S(1)} %slice_bitcast_fusion.5.keep_ref, f32[8,128,128]{2,1,0:T(8,128)S(1)} %get-tuple-element.16.refs_0_, bf16[8,128,128]{2,1,0:T(8,128)(2,1)S(1)} %collective-permute-done.2.refs_1_, ...), custom_call_target="tpu_custom_call" | custom-call | flops 1342177280 | bytes 4194304 | tf_op jit(solution)/shard_map/pallas_call | solution.py:179
  182.6 1.9 collective-permute-start.4
  184.6 20.2 %collective-permute-done.4.refs_1_ = bf16[8,128,128]{2,1,0:T(8,128)(2,1)S(1)} collective-permute-done((bf16[8,128,128]{2,1,0:T(8,128)(2,1)S(1)}, bf16[8,128,128]{2,1,0:T(8,128)(2,1)S(1)}, u32[]{:S(2)}, u32[]{:S(2)}) %collective-permute-start.4) | collective-permute-done | bytes 262176 | tf_op jit(solution)/shard_map/ppermute | solution.py:195
  204.8 0.0 collective-permute-done.5.refs_3_
  204.8 7.2 %shard_map.73 = (f32[128,128]{1,0:T(8,128)}, f32[128,128]{1,0:T(8,128)}) custom-call(s32[5]{0:T(128)S(1)} %stack.22.info_ref, f32[8,32]{1,0:T(8,128)S(1)} %slice_bitcast_fusion.5.keep_ref, f32[8,128,128]{2,1,0:T(8,128)S(1)} %get-tuple-element.18.refs_0_, bf16[8,128,128]{2,1,0:T(8,128)(2,1)S(1)} %collective-permute-done.4.refs_1_, ...), custom_call_target="tpu_custom_call" | custom-call | flops 1342177280 | bytes 4194304 | tf_op jit(solution)/shard_map/pallas_call | solution.py:179
  (17 shorter events, 0.1 us)
Async XLA Ops:
  0.6 0.9 copy-start.2
  0.6 1.0 copy-start.1
  2.3 33.2 %all-to-all-start.2 = ((bf16[64,8,128]{2,1,0:T(8,128)(2,1)}), bf16[64,8,128]{2,1,0:T(8,128)(2,1)S(1)}, u32[]{:S(2)}, u32[]{:S(2)}) async-start(bf16[64,8,128]{2,1,0:T(8,128)(2,1)} %maximum_bitcast_fusion), calls=%async_computation.2 | async-start | bytes 262144 | tf_op jit(solution)/shard_map/all_to_all | solution.py:208
  35.5 0.7 copy-start
  38.6 29.7 %all-to-all-start.3 = ((bf16[64,8,8,128]{3,2,1,0:T(8,128)(2,1)}), bf16[64,8,8,128]{3,2,1,0:T(8,128)(2,1)S(1)}, u32[]{:S(2)}, u32[]{:S(2)}) async-start(bf16[64,8,8,128]{3,2,1,0:T(8,128)(2,1)} %shard_map.69), calls=%async_computation.3 | async-start | bytes 2097152 | tf_op jit(solution)/shard_map/all_to_all | solution.py:222
  44.2 0.8 copy-start.3
  44.3 0.7 copy-start.5
  45.1 0.7 copy-start.4
  69.0 28.0 %all-to-all-start = ((f32[64,1,128]{2,1,0:T(1,128)}), f32[64,1,128]{2,1,0:T(1,128)S(1)}, u32[]{:S(2)}, u32[]{:S(2)}) async-start(f32[64,1,128]{2,1,0:T(1,128)} %broadcast_in_dim.31), calls=%async_computation | async-start | bytes 65536 | tf_op jit(solution)/shard_map/all_to_all | solution.py:214
  97.0 19.9 %all-to-all-start.4 = ((bf16[8,32,8,128]{3,2,1,0:T(8,128)(2,1)}), bf16[8,32,8,128]{3,2,1,0:T(8,128)(2,1)S(1)}, u32[]{:S(2)}, u32[]{:S(2)}) async-start(bf16[8,32,8,128]{3,2,1,0:T(8,128)(2,1)} %copy.34), calls=%async_computation.4 | async-start | bytes 1048576 | tf_op jit(solution)/shard_map/all_to_all | solution.py:225
  116.9 15.7 %collective-permute-start.1 = (bf16[8,2,128,128]{3,2,1,0:T(8,128)(2,1)S(1)}, bf16[8,2,128,128]{3,2,1,0:T(8,128)(2,1)S(1)}, u32[]{:S(2)}, u32[]{:S(2)}) collective-permute-start(bf16[8,2,128,128]{3,2,1,0:T(8,128)(2,1)S(1)} %bitcast.32), channel_id=1, source_target_pairs={{0,1},{1,0},{2,3},{3,2},{4,5},{5,4},{6,7},{7,6},{8,9},{9,8},{10,11... | collective-permute-start | bytes 1572872 | tf_op jit(solution)/shard_map/ppermute | solution.py:195
  120.4 8.0 %all-to-all-start.1 = ((f32[8,1,128]{2,1,0:T(1,128)}), f32[8,1,128]{2,1,0:T(1,128)S(1)}, u32[]{:S(2)}, u32[]{:S(2)}) async-start(f32[8,1,128]{2,1,0:T(1,128)} %bitcast.13), calls=%async_computation.1 | async-start | bytes 8192 | tf_op jit(solution)/shard_map/all_to_all | solution.py:219
  128.4 18.6 %all-to-all-start.5 = ((bf16[8,32,8,128]{3,2,1,0:T(8,128)(2,1)}), bf16[8,32,8,128]{3,2,1,0:T(8,128)(2,1)S(1)}, u32[]{:S(2)}, u32[]{:S(2)}) async-start(bf16[8,32,8,128]{3,2,1,0:T(8,128)(2,1)} %copy.35), calls=%async_computation.5 | async-start | bytes 1048576 | tf_op jit(solution)/shard_map/all_to_all | solution.py:226
  132.7 33.5 %collective-permute-start.3 = (bf16[8,2,128,128]{3,2,1,0:T(8,128)(2,1)S(1)}, bf16[8,2,128,128]{3,2,1,0:T(8,128)(2,1)S(1)}, u32[]{:S(2)}, u32[]{:S(2)}) collective-permute-start(bf16[8,2,128,128]{3,2,1,0:T(8,128)(2,1)S(1)} %broadcast_select_fusion.1.refs_2_), channel_id=1, source_target_pairs={{0,2},{1,3},{2,0},{3,1},{4,6},{5,7},{6,4},{7,5},{8,10},{9,11},{10,... | collective-permute-start | bytes 1572872 | tf_op jit(solution)/shard_map/ppermute | solution.py:195
  153.6 4.0 %collective-permute-start = (bf16[8,128,128]{2,1,0:T(8,128)(2,1)S(1)}, bf16[8,128,128]{2,1,0:T(8,128)(2,1)S(1)}, u32[]{:S(2)}, u32[]{:S(2)}) collective-permute-start(bf16[8,128,128]{2,1,0:T(8,128)(2,1)S(1)} %get-tuple-element.15), channel_id=1, source_target_pairs={{0,1},{1,0},{2,3},{3,2},{4,5},{5,4},{6,7},{7,6},{8,9},{9,8},{10,11... | collective-permute-start | bytes 786440 | tf_op jit(solution)/shard_map/ppermute | solution.py:195
  164.2 11.8 %collective-permute-start.2 = (bf16[8,128,128]{2,1,0:T(8,128)(2,1)S(1)}, bf16[8,128,128]{2,1,0:T(8,128)(2,1)S(1)}, u32[]{:S(2)}, u32[]{:S(2)}) collective-permute-start(bf16[8,128,128]{2,1,0:T(8,128)(2,1)S(1)} %get-tuple-element.17), channel_id=1, source_target_pairs={{0,2},{1,3},{2,0},{3,1},{4,6},{5,7},{6,4},{7,5},{8,10},{9,11},{10,... | collective-permute-start | bytes 786440 | tf_op jit(solution)/shard_map/ppermute | solution.py:195
  166.2 38.6 %collective-permute-start.5 = (bf16[8,2,128,128]{3,2,1,0:T(8,128)(2,1)S(1)}, bf16[8,2,128,128]{3,2,1,0:T(8,128)(2,1)S(1)}, u32[]{:S(2)}, u32[]{:S(2)}) collective-permute-start(bf16[8,2,128,128]{3,2,1,0:T(8,128)(2,1)S(1)} %broadcast_select_fusion.refs_2_), channel_id=1, source_target_pairs={{0,4},{1,5},{2,6},{3,7},{4,0},{5,1},{6,2},{7,3},{8,12},{9,13},{10,... | collective-permute-start | bytes 1572872 | tf_op jit(solution)/shard_map/ppermute | solution.py:195
  182.6 22.2 %collective-permute-start.4 = (bf16[8,128,128]{2,1,0:T(8,128)(2,1)S(1)}, bf16[8,128,128]{2,1,0:T(8,128)(2,1)S(1)}, u32[]{:S(2)}, u32[]{:S(2)}) collective-permute-start(bf16[8,128,128]{2,1,0:T(8,128)(2,1)S(1)} %get-tuple-element.19), channel_id=1, source_target_pairs={{0,4},{1,5},{2,6},{3,7},{4,0},{5,1},{6,2},{7,3},{8,12},{9,13},{10,... | collective-permute-start | bytes 786440 | tf_op jit(solution)/shard_map/ppermute | solution.py:195

commit v2 on v1

v2 whole, which is shorter than its diff:
```python
import functools

import jax
import jax.numpy as jnp
from jax import lax
from jax.experimental import pallas as pl
from jax.experimental.pallas import tpu as pltpu
from jax.sharding import Mesh, PartitionSpec as P

SUB = 4
GRP = ("yh", "x", "z")
BLK = ("yl", "core")
ALL = GRP + BLK
FAR = ("yh", "yl", "z")
NEAR = ("x", "core")
YH, XS, ZS, YL, CORES = 2, 4, 8, 4, 2
GROUPS, PARTS = YH * XS * ZS, YL * CORES
BF = jnp.bfloat16
F32 = jnp.float32
LANES = 128
PIECE = 8
SMEM = pl.BlockSpec(memory_space=pltpu.SMEM)
VMEM = pl.BlockSpec(memory_space=pltpu.VMEM)


def pack_kernel(x_ref, u_ref, v_ref, out_ref):
    rows, rank = u_ref.shape
    out_ref[:rows] = x_ref[:, :rank].astype(BF)
    out_ref[rows : 2 * rows] = x_ref[:, rank:].astype(BF)
    out_ref[2 * rows : 3 * rows] = u_ref[...].astype(BF)
    out_ref[3 * rows :] = v_ref[...].astype(BF)


def pack_call(features, factor_u, factor_v):
    rows, rank = factor_u.shape
    return pl.pallas_call(
        pack_kernel,
        out_shape=jax.ShapeDtypeStruct((4 * rows, rank), BF),
        in_specs=[VMEM] * 3,
        out_specs=VMEM,
        cost_estimate=pl.CostEstimate(flops=100000, bytes_accessed=400000, transcendentals=0),
    )(features, factor_u, factor_v)


def mask_place(group, part):
    z = group % ZS
    return (group // (XS * ZS) * YL + part // CORES) * 2 + z // 4, (z % 4) * SUB * PARTS


def tables_kernel(here_ref, matching_ref, mask_ref, leaf_ref, info_ref, tile_ref, inv_ref):
    group, part = here_ref[0], here_ref[1]

    def invert(e, carry):
        for t in range(SUB - 1):
            inv_ref[t * GROUPS + matching_ref[t, e]] = e
        return carry

    lax.fori_loop(0, GROUPS, invert, 0, unroll=4)

    def before(t, e):
        return inv_ref[t * GROUPS + e]

    def trace_back(d, carry):
        nodes = [d]
        for t in range(SUB - 2, -1, -1):
            nodes = [n for e in nodes for n in (e, before(t, e))]
        base = (d // (XS * ZS) * YL * ZS + d % ZS) * PARTS + d // ZS % XS * CORES
        for k in range(PARTS):
            leaf_ref[base + k // CORES * ZS * PARTS + k % CORES] = nodes[k]
        return carry

    lax.fori_loop(0, GROUPS, trace_back, 0, unroll=2)

    info_ref[0] = part
    node = group
    for t in range(SUB - 1, -1, -1):
        info_ref[SUB + t] = node
        if t > 0:
            bit = part // (1 << (t - 1)) % 2
            info_ref[t] = bit
            node = jnp.where(bit == 1, before(t - 1, node), node)

    row, lane = mask_place(group, part)
    lanes = lax.broadcasted_iota(jnp.int32, (PIECE, LANES), 1)
    values = jnp.zeros((PIECE, LANES), jnp.int32)
    for t in range(SUB):
        held = group
        for s in range(t - 1, -1, -1):
            held = before(s, held)
        for c in range(PARTS):
            values = jnp.where(lanes == lane + t * PARTS + c, mask_ref[0, held * PARTS + c], values)
    rows = lax.broadcasted_iota(jnp.int32, (PIECE, LANES), 0)
    tile_ref[...] = jnp.where(rows == row % PIECE, values, 0).astype(F32).astype(BF)


def tables_call(here, matching, mask):
    return pl.pallas_call(
        tables_kernel,
        out_shape=(
            jax.ShapeDtypeStruct((GROUPS * PARTS,), jnp.int32),
            jax.ShapeDtypeStruct((2 * SUB,), jnp.int32),
            jax.ShapeDtypeStruct((PIECE, LANES), BF),
        ),
        in_specs=[SMEM, SMEM, SMEM],
        out_specs=(SMEM, SMEM, VMEM),
        scratch_shapes=[pltpu.SMEM((GROUPS * (SUB - 1),), jnp.int32)],
        cost_estimate=pl.CostEstimate(flops=2000000, bytes_accessed=4096, transcendentals=0),
    )(here, matching, mask)


def pick_kernel(leaf_ref, tile_ref, pieces_ref, out_ref):
    tile = tile_ref[...]

    def one(far, carry):
        for near in range(XS * CORES):
            out_ref[far, near] = pieces_ref[leaf_ref[far * XS * CORES + near]]
        out_ref[far, XS * CORES] = tile
        return carry

    lax.fori_loop(0, out_ref.shape[0], one, 0, unroll=4)


def pick_call(leaf_table, tile, pieces):
    return pl.pallas_call(
        pick_kernel,
        out_shape=jax.ShapeDtypeStruct((YH * YL * ZS, XS * CORES + 1, PIECE, LANES), BF),
        in_specs=[SMEM, VMEM, VMEM],
        out_specs=VMEM,
        compiler_params=pltpu.CompilerParams(vmem_limit_bytes=16 << 20),
        cost_estimate=pl.CostEstimate(flops=1000000, bytes_accessed=2 << 20, transcendentals=0),
    )(leaf_table, tile, pieces)


def regroup_kernel(got_ref, out_ref):
    far = YH * YL * ZS
    for near in range(XS * CORES):
        out_ref[near, :far] = got_ref[:, near]
    for yh in range(YH):
        span = far // YH
        total = jnp.sum(got_ref[yh * span : (yh + 1) * span, XS * CORES].astype(F32), axis=0).astype(BF)
        for near in range(XS * CORES):
            out_ref[near, far + yh] = total


def regroup_call(got):
    return pl.pallas_call(
        regroup_kernel,
        out_shape=jax.ShapeDtypeStruct((XS * CORES, YH * YL * ZS + YH, PIECE, LANES), BF),
        in_specs=[VMEM],
        out_specs=VMEM,
        compiler_params=pltpu.CompilerParams(vmem_limit_bytes=16 << 20),
        cost_estimate=pl.CostEstimate(flops=1000000, bytes_accessed=2 << 20, transcendentals=0),
    )(got)


def sim_kernel(xl_ref, xr_ref, out_ref, lx, rx):
    blocks, _, rows, _ = out_ref.shape
    rank, span = LANES, rows // 2
    for b in range(blocks):
        yl, core = b // CORES, b % CORES
        taken = pl.ds(yl * span, span)
        for i in range(2):
            put = pl.ds(b * rows + i * span, span)
            for half in range(2):
                near = (2 * half + i) * CORES + core
                lanes = slice(half * rank, (half + 1) * rank)
                lx[put, lanes] = xl_ref[near, taken]
                rx[put, lanes] = xr_ref[near, taken]
    for r in range(0, blocks, 2):
        right = rx[r * rows : (r + 2) * rows]
        for b in range(0, blocks, 2):
            sims = lax.dot_general(
                lx[b * rows : (b + 2) * rows], right, (((1,), (1,)), ((), ())), preferred_element_type=F32
            )
            for i in range(2):
                for j in range(2):
                    out_ref[b + i, r + j] = sims[i * rows : (i + 1) * rows, j * rows : (j + 1) * rows]


def sim_call(rows, left_x, right_x):
    operand = pltpu.VMEM((PARTS * rows, 2 * LANES), BF)
    return pl.pallas_call(
        sim_kernel,
        out_shape=jax.ShapeDtypeStruct((PARTS, PARTS, rows, rows), F32),
        in_specs=[VMEM, VMEM],
        out_specs=VMEM,
        scratch_shapes=[operand, operand],
        compiler_params=pltpu.CompilerParams(vmem_limit_bytes=24 << 20),
        cost_estimate=pl.CostEstimate(
            flops=4 * PARTS * PARTS * rows * rows * LANES, bytes_accessed=4 << 20, transcendentals=0
        ),
    )(left_x, right_x)


def sub_epoch_kernel(step_size, level, last, info_ref, mask_ref, sim_ref, *refs):
    if level == 0:
        all_ref, *refs = refs
    else:
        left_ref, right_ref, *refs = refs
    *outs, ls, rs, lb, rb, mf, kr, ks = refs
    blocks, rows, rank = ls.shape
    part, flip, node = info_ref[0], jnp.int32(0) if level == 0 else info_ref[level], info_ref[SUB + level]

    mf[...] = mask_ref[...].astype(F32)
    for b in range(blocks):
        row, lane = mask_place(node, b)
        kr[pl.ds(b, 1)] = mf[node // ZS % XS * CORES + b % CORES, pl.ds(row, 1)]
    values = kr[...]
    lanes = lax.broadcasted_iota(jnp.int32, values.shape, 1)
    for c in range(blocks):
        mine = jnp.where(lanes == lane + level * PARTS + c, values, 0.0)
        ks[c] = jnp.broadcast_to(jnp.sum(mine, axis=1, keepdims=True), values.shape)

    span = rows // 2
    for b in range(blocks):
        if level == 0:
            yl, core = b // CORES, b % CORES
            moved = pl.ds((YL + yl) * span, span)
            for i in range(2):
                put = pl.ds(i * span, span)
                left = all_ref[i * CORES + core, moved]
                right = all_ref[(2 + i) * CORES + core, moved]
                ls[b, put], rs[b, put] = left.astype(F32), right.astype(F32)
                lb[b, put], rb[b, put] = left, right
        else:
            ls[b], rs[b] = left_ref[b], right_ref[b].astype(F32)
            lb[b], rb[b] = left_ref[b].astype(BF), right_ref[b]

    def cycle_step(step, carry):
        shift = jnp.where(flip == 1, step, blocks - step)
        places = [lax.rem(b + shift, blocks) for b in range(blocks)]
        preds = [
            lax.dot_general(lb[b], rb[places[b]], (((1,), (1,)), ((), ())), preferred_element_type=F32)
            for b in range(blocks)
        ]
        resids = []
        for b in range(blocks):
            row = jnp.where(flip == 1, places[b], b)
            col = jnp.where(flip == 1, b, places[b])
            resids.append((ks[col, pl.ds(row, 1)] * (preds[b] - sim_ref[b, places[b]])).astype(BF))
        grads_l = [jnp.dot(resids[b], rb[places[b]], preferred_element_type=F32) for b in range(blocks)]
        grads_r = [
            lax.dot_general(resids[b], lb[b], (((0,), (0,)), ((), ())), preferred_element_type=F32)
            for b in range(blocks)
        ]
        for b in range(blocks):
            new_left = ls[b] - step_size * grads_l[b]
            ls[b] = new_left
            lb[b] = new_left.astype(BF)
        for b in range(blocks):
            new_right = rs[places[b]] - step_size * grads_r[b]
            rs[places[b]] = new_right
            rb[places[b]] = new_right.astype(BF)
        return carry

    lax.fori_loop(0, blocks, cycle_step, 0)
    if last:
        uo_ref, vo_ref = outs

        @pl.when(flip == 0)
        def _():
            uo_ref[...] = ls[part]
            vo_ref[...] = rs[part]

        @pl.when(flip == 1)
        def _():
            uo_ref[...] = rs[part]
            vo_ref[...] = ls[part]
    else:
        kept_ref, sent_ref = outs
        same = info_ref[1 + level] == flip

        @pl.when(same)
        def _():
            kept_ref[...] = ls[...]
            sent_ref[...] = lb[...]

        @pl.when(jnp.logical_not(same))
        def _():
            kept_ref[...] = rs[...]
            sent_ref[...] = rb[...]


def sub_epoch_call(level, rows, info, mask, sims, *arrays):
    rank, last = LANES, level + 1 == SUB
    whole = (PARTS, rows, rank)
    if last:
        outs = (jax.ShapeDtypeStruct((rows, rank), F32),) * 2
    else:
        outs = (jax.ShapeDtypeStruct(whole, F32), jax.ShapeDtypeStruct(whole, BF))
    return pl.pallas_call(
        functools.partial(sub_epoch_kernel, 4.0 / rows, level, last),
        out_shape=outs,
        in_specs=[SMEM] + [VMEM] * (2 + len(arrays)),
        out_specs=(VMEM, VMEM),
        scratch_shapes=[
            pltpu.VMEM(whole, F32),
            pltpu.VMEM(whole, F32),
            pltpu.VMEM(whole, BF),
            pltpu.VMEM(whole, BF),
            pltpu.VMEM(mask.shape, F32),
            pltpu.VMEM((PARTS, LANES), F32),
            pltpu.VMEM((PARTS, PARTS, LANES), F32),
        ],
        compiler_params=pltpu.CompilerParams(vmem_limit_bytes=28 << 20),
        cost_estimate=pl.CostEstimate(
            flops=2 * PARTS * PARTS * rows * rows * 3 * rank,
            bytes_accessed=6 << 20,
            transcendentals=0,
        ),
    )(info, mask, sims, *arrays)


def swapped(array, bit):
    return lax.ppermute(array, BLK, [(i, i ^ (1 << bit)) for i in range(PARTS)])


def spread(array, axes):
    return lax.all_to_all(array, axes, split_axis=0, concat_axis=0, tiled=True)


def halves_out(array, bit, core):
    half = array.shape[0] // 2
    return swapped(lax.dynamic_slice_in_dim(array, core * half, half, 0), bit)


def halves_in(first, core):
    second = swapped(first, 0)
    return jnp.where(core == 0, jnp.concatenate([first, second]), jnp.concatenate([second, first]))


def local(features, factor_u, factor_v, tile_mask, matching):
    group = lax.axis_index(GRP).astype(jnp.int32)
    part = lax.axis_index(BLK).astype(jnp.int32)
    slot_rows, rank = factor_u.shape
    bits = [(part >> t) & 1 for t in range(SUB - 1)]

    pieces = spread(pack_call(features, factor_u, factor_v).reshape(GROUPS, PIECE, rank), GRP)
    leaf_table, info, tile = tables_call(jnp.stack([group, part]), matching, tile_mask)
    got = spread(pick_call(leaf_table, tile, pieces), FAR)
    got = spread(regroup_call(got), NEAR).reshape(XS * CORES, -1, rank)
    half = YL * slot_rows // 2
    left_x = got[:, :half]
    mask = got[:, 2 * half :]

    coming_x = swapped(left_x, 0)
    kept, sent = sub_epoch_call(0, slot_rows, info, mask, sim_call(slot_rows, got, got), got)
    for level in range(1, SUB):
        right = swapped(sent, level - 1)
        kept, coming_x = lax.optimization_barrier((kept, coming_x))
        right_x = coming_x if level == 1 else halves_in(coming_x, bits[0])
        sims = sim_call(slot_rows, left_x, right_x)
        if level + 1 < SUB:
            left_x = jnp.where(bits[level] == bits[level - 1], left_x, right_x)
            coming_x = halves_out(left_x, level, bits[0])
        kept, sent = sub_epoch_call(level, slot_rows, info, mask, sims, kept, right)
    return kept, sent


def solution(mesh):
    fine = Mesh(mesh.devices.reshape(YH, XS, ZS, YL, CORES), ALL)
    in_specs = (P(ALL, None), P(ALL, None), P(ALL, None), P(ALL, None), P())
    out_specs = (P(ALL, None), P(ALL, None))
    return jax.shard_map(local, mesh=fine, in_specs=in_specs, out_specs=out_specs, check_vma=False)
```

time: 213 us -> 162 us (0.76)
  waiting for transfers between devices: 99.1 us -> 30.5 us
  blocking collectives: 0 us -> 56 us
  starting transfers between devices: 68.7 us -> 42 us
  local copies, waits for them, and re-layouts: 7.06 us -> 1.46 us
  Pallas kernels: 33.9 us -> 29.5 us
    all_to_all x6 -> x1, waiting for transfers between devices: 71.1 us -> 9.86 us  [spread(): return lax.all_to_all(array, axes, split_axis=0, concat_axis=0, tiled=True)]
    all_to_all x0 -> x2, blocking collectives: none -> 56 us  [spread(): return lax.all_to_all(array, axes, split_axis=0, concat_axis=0, tiled=True)]
    all_to_all x6 -> x1, starting transfers between devices: 52.8 us -> 19.6 us  [spread(): return lax.all_to_all(array, axes, split_axis=0, concat_axis=0, tiled=True)]
    ppermute x6 -> x8, waiting for transfers between devices: 28 us -> 20.6 us  [swapped(): return lax.ppermute(array, BLK, [(i, i ^ 1 << bit) for i in range(PARTS)])]
    ppermute x6 -> x8, starting transfers between devices: 15.9 us -> 22.4 us  [swapped(): return lax.ppermute(array, BLK, [(i, i ^ 1 << bit) for i in range(PARTS)])]
    pallas_call x6 -> x12, Pallas kernels: 33.9 us -> 29.5 us  [the longest x4 20.3 us: sub_epoch_call(): pl.pallas_call(functools.partial(sub_epoch_kernel, 4.0 / rows, level, las...]
  transfers between devices with their start and end apart: 12 -> 9, of which waited for: 9 -> 5; matrix products, arithmetic and copies ran while one was open for 2% -> 1% of each run, Pallas kernels for 11% -> 13%
where the time goes in v2:
time: 162 us; the launch traced here: 161 us
  blocking collectives  56 us (35%)
  starting transfers between devices  42 us (26%)
  waiting for transfers between devices  30.5 us (19%)
  Pallas kernels  29.5 us (18%)
    all_to_all x2, blocking collectives, spread(): return lax.all_to_all(array, axes, split_axis=0, concat_axis=0, tiled=True)  56 us
    ppermute x8, starting transfers between devices, swapped(): return lax.ppermute(array, BLK, [(i, i ^ 1 << bit) for i in range(PARTS)])  22.4 us
    ppermute x8, waiting for transfers between devices, swapped(): return lax.ppermute(array, BLK, [(i, i ^ 1 << bit) for i in range(PARTS)])  20.6 us
    pallas_call x4, Pallas kernels, sub_epoch_call(): pl.pallas_call(functools.partial(sub_epoch_kernel, 4.0 / rows, level, las...  20.3 us
    all_to_all x1, starting transfers between devices, spread(): return lax.all_to_all(array, axes, split_axis=0, concat_axis=0, tiled=True)  19.6 us
    all_to_all x1, waiting for transfers between devices, spread(): return lax.all_to_all(array, axes, split_axis=0, concat_axis=0, tiled=True)  9.86 us
  transfers between devices with their start and end apart: 9, of which 5 were waited for; matrix products, arithmetic and copies ran while one was open for 1% of the time, Pallas kernels for 13%

profile of v2, /device:TPU:1, one launch (start us, length us, event | category | flops | bytes accessed | tf_op | source)
XLA Modules:
  0.0 161.2 jit_solution(5121167074460858061)
XLA Ops:
  0.6 1.6 %shard_map.69 = bf16[512,128]{1,0:T(8,128)(2,1)} custom-call(f32[128,256]{1,0:T(8,128)} %x_ref.1, f32[128,128]{1,0:T(8,128)} %u_ref.1, f32[128,128]{1,0:T(8,128)} %v_ref.1), custom_call_target="tpu_custom_call" | custom-call | flops 100000 | bytes 400000 | tf_op jit(solution)/shard_map/pallas_call | solution.py:36
  2.2 19.6 %all-to-all-start = ((bf16[64,8,128]{2,1,0:T(8,128)(2,1)}), bf16[64,8,128]{2,1,0:T(8,128)(2,1)S(1)}, u32[]{:S(2)}, u32[]{:S(2)}) async-start(bf16[64,8,128]{2,1,0:T(8,128)(2,1)} %bitcast.10), calls=%async_computation | async-start | bytes 262144 | tf_op jit(solution)/shard_map/all_to_all | solution.py:319
  21.9 0.6 pad_add_fusion.here_ref
  22.5 3.1 %shard_map.68 = (s32[512]{0:T(512)}, s32[8]{0:T(128)}, bf16[8,128]{1,0:T(8,128)(2,1)}) custom-call(s32[2]{0:T(128)} %pad_add_fusion.here_ref, s32[3,64]{1,0:T(4,128)} %matching_ref.1, s32[1,512]{1,0:T(1,128)} %mask_ref.1), custom_call_target="tpu_custom_call" | custom-call | flops 2000000 | bytes 4096 | tf_op jit(solution)/shard_map/pallas_call | solution.py:97
  25.6 9.9 %all-to-all-done.pieces_ref = bf16[64,8,128]{2,1,0:T(8,128)(2,1)S(1)} async-done(((bf16[64,8,128]{2,1,0:T(8,128)(2,1)}), bf16[64,8,128]{2,1,0:T(8,128)(2,1)S(1)}, u32[]{:S(2)}, u32[]{:S(2)}) %all-to-all-start) | async-done | bytes 131104 | tf_op jit(solution)/shard_map/all_to_all | solution.py:319
  35.5 0.0 copy-start.1
  35.5 0.7 copy-done.1
  36.1 0.0 copy-start.2
  36.1 0.7 copy-done.2
  36.8 1.2 shard_map.70
  38.0 33.5 %all_to_all.15.got_ref = bf16[64,9,8,128]{3,2,1,0:T(8,128)(2,1)S(1)} all-to-all(bf16[64,9,8,128]{3,2,1,0:T(8,128)(2,1)S(1)} %shard_map.70), channel_id=1, replica_groups=mesh['yh'=2,'x'=4,'z'=8,'yl'=4,'core'=2] {'yh','yl','z'}, dimensions={0} | all-to-all | bytes 2359296 | tf_op jit(solution)/shard_map/all_to_all | solution.py:319
  71.5 0.2 shard_map.71
  71.7 22.5 %all_to_all.16 = bf16[8,66,8,128]{3,2,1,0:T(8,128)(2,1)S(1)} all-to-all(bf16[8,66,8,128]{3,2,1,0:T(8,128)(2,1)S(1)} %shard_map.71), channel_id=1, replica_groups=mesh['yh'=2,'x'=4,'z'=8,'yl'=4,'core'=2] {'x','core'}, dimensions={0} | all-to-all | bytes 2162688 | tf_op jit(solution)/shard_map/all_to_all | solution.py:319
  94.3 2.5 %collective-permute-start = (bf16[8,256,128]{2,1,0:T(8,128)(2,1)S(1)}, bf16[8,256,128]{2,1,0:T(8,128)(2,1)S(1)}, u32[]{:S(2)}, u32[]{:S(2)}) collective-permute-start(bf16[8,256,128]{2,1,0:T(8,128)(2,1)S(1)} %slice.9.xl_ref), channel_id=1, source_target_pairs={{0,1},{1,0},{2,3},{3,2},{4,5},{5,4},{6,7},{7,6},{8,9},{9,8},{10,11... | collective-permute-start | bytes 1572872 | tf_op jit(solution)/shard_map/ppermute | solution.py:315
  96.8 0.0 copy-start
  96.8 0.8 shard_map.72.sim_ref
  97.6 0.0 copy-done
  97.6 4.9 %shard_map.73 = (f32[8,128,128]{2,1,0:T(8,128)S(1)}, bf16[8,128,128]{2,1,0:T(8,128)(2,1)S(1)}) custom-call(s32[8]{0:T(128)S(1)} %copy-done, bf16[8,16,128]{2,1,0:T(8,128)(2,1)S(1)} %slice.8.mask_ref, f32[8,8,128,128]{3,2,1,0:T(8,128)S(1)} %shard_map.72.sim_ref, bf16[8,528,128]{2,1,0:T(8,128)(2,1)S(1)} %bitcast.8), custom_call_target="tpu_custom_call" | custom-call | flops 805306368 | bytes 6291456 | tf_op jit(solution)/shard_map/pallas_call | solution.py:291
  102.5 1.9 %collective-permute-start.1 = (bf16[8,128,128]{2,1,0:T(8,128)(2,1)S(1)}, bf16[8,128,128]{2,1,0:T(8,128)(2,1)S(1)}, u32[]{:S(2)}, u32[]{:S(2)}) collective-permute-start(bf16[8,128,128]{2,1,0:T(8,128)(2,1)S(1)} %get-tuple-element.23), channel_id=1, source_target_pairs={{0,1},{1,0},{2,3},{3,2},{4,5},{5,4},{6,7},{7,6},{8,9},{9,8},{10,11... | collective-permute-start | bytes 786440 | tf_op jit(solution)/shard_map/ppermute | solution.py:315
  104.5 0.0 collective-permute-done.xr_ref
  104.5 0.1 broadcast_select_fusion.xl_ref
  104.6 2.8 %collective-permute-start.2 = (bf16[4,256,128]{2,1,0:T(8,128)(2,1)S(1)}, bf16[4,256,128]{2,1,0:T(8,128)(2,1)S(1)}, u32[]{:S(2)}, u32[]{:S(2)}) collective-permute-start(bf16[4,256,128]{2,1,0:T(8,128)(2,1)S(1)} %constant_dynamic-slice_fusion.1), channel_id=1, source_target_pairs={{0,2},{1,3},{2,0},{3,1},{4,6},{5,7},{6,4},{7,5},{8,10},{9,11},{10,... | collective-permute-start | bytes 786440 | tf_op jit(solution)/shard_map/ppermute | solution.py:315
  107.4 0.8 shard_map.74.sim_ref
  108.1 0.0 collective-permute-done.1.refs_1_
  108.2 4.9 %shard_map.75 = (f32[8,128,128]{2,1,0:T(8,128)S(1)}, bf16[8,128,128]{2,1,0:T(8,128)(2,1)S(1)}) custom-call(s32[8]{0:T(128)S(1)} %copy-done, bf16[8,16,128]{2,1,0:T(8,128)(2,1)S(1)} %slice.8.mask_ref, f32[8,8,128,128]{3,2,1,0:T(8,128)S(1)} %shard_map.74.sim_ref, f32[8,128,128]{2,1,0:T(8,128)S(1)} %get-tuple-element.22.refs_0_, ...), custom_call_target="tpu_custom_call" | custom-call | flops 805306368 | bytes 6291456 | tf_op jit(solution)/shard_map/pallas_call | solution.py:291
  113.1 0.7 collective-permute-done.2
  113.8 3.2 %collective-permute-start.3 = (bf16[4,256,128]{2,1,0:T(8,128)(2,1)S(1)}, bf16[4,256,128]{2,1,0:T(8,128)(2,1)S(1)}, u32[]{:S(2)}, u32[]{:S(2)}) collective-permute-start(bf16[4,256,128]{2,1,0:T(8,128)(2,1)S(1)} %collective-permute-done.2), channel_id=1, source_target_pairs={{0,1},{1,0},{2,3},{3,2},{4,5},{5,4},{6,7},{7,6},{8,9},{9,8},{10,11... | collective-permute-start | bytes 786440 | tf_op jit(solution)/shard_map/ppermute | solution.py:315
  117.1 2.8 %collective-permute-start.4 = (bf16[8,128,128]{2,1,0:T(8,128)(2,1)S(1)}, bf16[8,128,128]{2,1,0:T(8,128)(2,1)S(1)}, u32[]{:S(2)}, u32[]{:S(2)}) collective-permute-start(bf16[8,128,128]{2,1,0:T(8,128)(2,1)S(1)} %get-tuple-element.27), channel_id=1, source_target_pairs={{0,2},{1,3},{2,0},{3,1},{4,6},{5,7},{6,4},{7,5},{8,10},{9,11},{10,... | collective-permute-start | bytes 786440 | tf_op jit(solution)/shard_map/ppermute | solution.py:315
  119.9 0.0 collective-permute-done.3
  119.9 0.1 broadcast_select_fusion.1
  120.1 4.5 %collective-permute-start.5 = (bf16[4,256,128]{2,1,0:T(8,128)(2,1)S(1)}, bf16[4,256,128]{2,1,0:T(8,128)(2,1)S(1)}, u32[]{:S(2)}, u32[]{:S(2)}) collective-permute-start(bf16[4,256,128]{2,1,0:T(8,128)(2,1)S(1)} %constant_dynamic-slice_fusion), channel_id=1, source_target_pairs={{0,4},{1,5},{2,6},{3,7},{4,0},{5,1},{6,2},{7,3},{8,12},{9,13},{10,... | collective-permute-start | bytes 786440 | tf_op jit(solution)/shard_map/ppermute | solution.py:315
  124.6 0.8 shard_map.76.sim_ref
  125.3 5.8 %collective-permute-done.4.refs_1_ = bf16[8,128,128]{2,1,0:T(8,128)(2,1)S(1)} collective-permute-done((bf16[8,128,128]{2,1,0:T(8,128)(2,1)S(1)}, bf16[8,128,128]{2,1,0:T(8,128)(2,1)S(1)}, u32[]{:S(2)}, u32[]{:S(2)}) %collective-permute-start.4) | collective-permute-done | bytes 262176 | tf_op jit(solution)/shard_map/ppermute | solution.py:315
  131.1 4.9 %shard_map.77 = (f32[8,128,128]{2,1,0:T(8,128)S(1)}, bf16[8,128,128]{2,1,0:T(8,128)(2,1)S(1)}) custom-call(s32[8]{0:T(128)S(1)} %copy-done, bf16[8,16,128]{2,1,0:T(8,128)(2,1)S(1)} %slice.8.mask_ref, f32[8,8,128,128]{3,2,1,0:T(8,128)S(1)} %shard_map.76.sim_ref, f32[8,128,128]{2,1,0:T(8,128)S(1)} %get-tuple-element.26.refs_0_, ...), custom_call_target="tpu_custom_call" | custom-call | flops 805306368 | bytes 6291456 | tf_op jit(solution)/shard_map/pallas_call | solution.py:291
  136.1 0.6 collective-permute-done.5
  136.6 2.8 %collective-permute-start.6 = (bf16[4,256,128]{2,1,0:T(8,128)(2,1)S(1)}, bf16[4,256,128]{2,1,0:T(8,128)(2,1)S(1)}, u32[]{:S(2)}, u32[]{:S(2)}) collective-permute-start(bf16[4,256,128]{2,1,0:T(8,128)(2,1)S(1)} %collective-permute-done.5), channel_id=1, source_target_pairs={{0,1},{1,0},{2,3},{3,2},{4,5},{5,4},{6,7},{7,6},{8,9},{9,8},{10,11... | collective-permute-start | bytes 786440 | tf_op jit(solution)/shard_map/ppermute | solution.py:315
  139.4 1.9 %collective-permute-start.7 = (bf16[8,128,128]{2,1,0:T(8,128)(2,1)S(1)}, bf16[8,128,128]{2,1,0:T(8,128)(2,1)S(1)}, u32[]{:S(2)}, u32[]{:S(2)}) collective-permute-start(bf16[8,128,128]{2,1,0:T(8,128)(2,1)S(1)} %get-tuple-element.31), channel_id=1, source_target_pairs={{0,4},{1,5},{2,6},{3,7},{4,0},{5,1},{6,2},{7,3},{8,12},{9,13},{10,... | collective-permute-start | bytes 786440 | tf_op jit(solution)/shard_map/ppermute | solution.py:315
  141.3 0.0 collective-permute-done.6
  141.3 0.1 maximum_select_fusion.1.xr_ref
  141.4 0.8 shard_map.78.sim_ref
  142.2 13.5 %collective-permute-done.7.refs_1_ = bf16[8,128,128]{2,1,0:T(8,128)(2,1)S(1)} collective-permute-done((bf16[8,128,128]{2,1,0:T(8,128)(2,1)S(1)}, bf16[8,128,128]{2,1,0:T(8,128)(2,1)S(1)}, u32[]{:S(2)}, u32[]{:S(2)}) %collective-permute-start.7) | collective-permute-done | bytes 262176 | tf_op jit(solution)/shard_map/ppermute | solution.py:315
  155.7 5.5 %shard_map.79 = (f32[128,128]{1,0:T(8,128)}, f32[128,128]{1,0:T(8,128)}) custom-call(s32[8]{0:T(128)S(1)} %copy-done, bf16[8,16,128]{2,1,0:T(8,128)(2,1)S(1)} %slice.8.mask_ref, f32[8,8,128,128]{3,2,1,0:T(8,128)S(1)} %shard_map.78.sim_ref, f32[8,128,128]{2,1,0:T(8,128)S(1)} %get-tuple-element.30.refs_0_, bf16[8,128,128]{2,1,0:T(8,128)(2,1)S(1)} %collective-permute-done.7.refs_1_), custom_call_target="tpu_custom_call" | custom-call | flops 805306368 | bytes 6291456 | tf_op jit(solution)/shard_map/pallas_call | solution.py:291
  (4 shorter events, 0.1 us)
Async XLA Ops:
  2.2 33.2 %all-to-all-start = ((bf16[64,8,128]{2,1,0:T(8,128)(2,1)}), bf16[64,8,128]{2,1,0:T(8,128)(2,1)S(1)}, u32[]{:S(2)}, u32[]{:S(2)}) async-start(bf16[64,8,128]{2,1,0:T(8,128)(2,1)} %bitcast.10), calls=%async_computation | async-start | bytes 262144 | tf_op jit(solution)/shard_map/all_to_all | solution.py:319
  35.5 0.7 copy-start.1
  36.1 0.7 copy-start.2
  94.3 10.2 %collective-permute-start = (bf16[8,256,128]{2,1,0:T(8,128)(2,1)S(1)}, bf16[8,256,128]{2,1,0:T(8,128)(2,1)S(1)}, u32[]{:S(2)}, u32[]{:S(2)}) collective-permute-start(bf16[8,256,128]{2,1,0:T(8,128)(2,1)S(1)} %slice.9.xl_ref), channel_id=1, source_target_pairs={{0,1},{1,0},{2,3},{3,2},{4,5},{5,4},{6,7},{7,6},{8,9},{9,8},{10,11... | collective-permute-start | bytes 1572872 | tf_op jit(solution)/shard_map/ppermute | solution.py:315
  96.8 0.8 copy-start
  102.5 5.6 %collective-permute-start.1 = (bf16[8,128,128]{2,1,0:T(8,128)(2,1)S(1)}, bf16[8,128,128]{2,1,0:T(8,128)(2,1)S(1)}, u32[]{:S(2)}, u32[]{:S(2)}) collective-permute-start(bf16[8,128,128]{2,1,0:T(8,128)(2,1)S(1)} %get-tuple-element.23), channel_id=1, source_target_pairs={{0,1},{1,0},{2,3},{3,2},{4,5},{5,4},{6,7},{7,6},{8,9},{9,8},{10,11... | collective-permute-start | bytes 786440 | tf_op jit(solution)/shard_map/ppermute | solution.py:315
  104.6 9.3 %collective-permute-start.2 = (bf16[4,256,128]{2,1,0:T(8,128)(2,1)S(1)}, bf16[4,256,128]{2,1,0:T(8,128)(2,1)S(1)}, u32[]{:S(2)}, u32[]{:S(2)}) collective-permute-start(bf16[4,256,128]{2,1,0:T(8,128)(2,1)S(1)} %constant_dynamic-slice_fusion.1), channel_id=1, source_target_pairs={{0,2},{1,3},{2,0},{3,1},{4,6},{5,7},{6,4},{7,5},{8,10},{9,11},{10,... | collective-permute-start | bytes 786440 | tf_op jit(solution)/shard_map/ppermute | solution.py:315
  113.8 6.1 %collective-permute-start.3 = (bf16[4,256,128]{2,1,0:T(8,128)(2,1)S(1)}, bf16[4,256,128]{2,1,0:T(8,128)(2,1)S(1)}, u32[]{:S(2)}, u32[]{:S(2)}) collective-permute-start(bf16[4,256,128]{2,1,0:T(8,128)(2,1)S(1)} %collective-permute-done.2), channel_id=1, source_target_pairs={{0,1},{1,0},{2,3},{3,2},{4,5},{5,4},{6,7},{7,6},{8,9},{9,8},{10,11... | collective-permute-start | bytes 786440 | tf_op jit(solution)/shard_map/ppermute | solution.py:315
  117.1 14.0 %collective-permute-start.4 = (bf16[8,128,128]{2,1,0:T(8,128)(2,1)S(1)}, bf16[8,128,128]{2,1,0:T(8,128)(2,1)S(1)}, u32[]{:S(2)}, u32[]{:S(2)}) collective-permute-start(bf16[8,128,128]{2,1,0:T(8,128)(2,1)S(1)} %get-tuple-element.27), channel_id=1, source_target_pairs={{0,2},{1,3},{2,0},{3,1},{4,6},{5,7},{6,4},{7,5},{8,10},{9,11},{10,... | collective-permute-start | bytes 786440 | tf_op jit(solution)/shard_map/ppermute | solution.py:315
  120.1 16.5 %collective-permute-start.5 = (bf16[4,256,128]{2,1,0:T(8,128)(2,1)S(1)}, bf16[4,256,128]{2,1,0:T(8,128)(2,1)S(1)}, u32[]{:S(2)}, u32[]{:S(2)}) collective-permute-start(bf16[4,256,128]{2,1,0:T(8,128)(2,1)S(1)} %constant_dynamic-slice_fusion), channel_id=1, source_target_pairs={{0,4},{1,5},{2,6},{3,7},{4,0},{5,1},{6,2},{7,3},{8,12},{9,13},{10,... | collective-permute-start | bytes 786440 | tf_op jit(solution)/shard_map/ppermute | solution.py:315
  136.6 4.7 %collective-permute-start.6 = (bf16[4,256,128]{2,1,0:T(8,128)(2,1)S(1)}, bf16[4,256,128]{2,1,0:T(8,128)(2,1)S(1)}, u32[]{:S(2)}, u32[]{:S(2)}) collective-permute-start(bf16[4,256,128]{2,1,0:T(8,128)(2,1)S(1)} %collective-permute-done.5), channel_id=1, source_target_pairs={{0,1},{1,0},{2,3},{3,2},{4,5},{5,4},{6,7},{7,6},{8,9},{9,8},{10,11... | collective-permute-start | bytes 786440 | tf_op jit(solution)/shard_map/ppermute | solution.py:315
  139.4 16.3 %collective-permute-start.7 = (bf16[8,128,128]{2,1,0:T(8,128)(2,1)S(1)}, bf16[8,128,128]{2,1,0:T(8,128)(2,1)S(1)}, u32[]{:S(2)}, u32[]{:S(2)}) collective-permute-start(bf16[8,128,128]{2,1,0:T(8,128)(2,1)S(1)} %get-tuple-element.31), channel_id=1, source_target_pairs={{0,4},{1,5},{2,6},{3,7},{4,0},{5,1},{6,2},{7,3},{8,12},{9,13},{10,... | collective-permute-start | bytes 786440 | tf_op jit(solution)/shard_map/ppermute | solution.py:315

commit v3 on v2

--- a/solution.py
+++ b/solution.py
@@ -19,6 +19,9 @@
 F32 = jnp.float32
 LANES = 128
 PIECE = 8
+STRIDES = (1, 2 * CORES, CORES)
+INFO = GROUPS * PARTS
+VALUES = INFO + 16
 SMEM = pl.BlockSpec(memory_space=pltpu.SMEM)
 VMEM = pl.BlockSpec(memory_space=pltpu.VMEM)
 
@@ -47,7 +50,7 @@
     return (group // (XS * ZS) * YL + part // CORES) * 2 + z // 4, (z % 4) * SUB * PARTS
 
 
-def tables_kernel(here_ref, matching_ref, mask_ref, leaf_ref, info_ref, tile_ref, inv_ref):
+def tables_kernel(here_ref, matching_ref, mask_ref, table_ref, inv_ref):
     group, part = here_ref[0], here_ref[1]
 
     def invert(e, carry):
@@ -66,69 +69,67 @@
             nodes = [n for e in nodes for n in (e, before(t, e))]
         base = (d // (XS * ZS) * YL * ZS + d % ZS) * PARTS + d // ZS % XS * CORES
         for k in range(PARTS):
-            leaf_ref[base + k // CORES * ZS * PARTS + k % CORES] = nodes[k]
+            yl, core = k // 2 % 2 * 2 + k // 4, k % 2
+            table_ref[base + yl * ZS * PARTS + core] = nodes[k]
         return carry
 
     lax.fori_loop(0, GROUPS, trace_back, 0, unroll=2)
 
-    info_ref[0] = part
+    table_ref[INFO] = part
     node = group
     for t in range(SUB - 1, -1, -1):
-        info_ref[SUB + t] = node
+        table_ref[INFO + SUB + t] = node
         if t > 0:
-            bit = part // (1 << (t - 1)) % 2
-            info_ref[t] = bit
+            bit = part // STRIDES[t - 1] % 2
+            table_ref[INFO + t] = bit
             node = jnp.where(bit == 1, before(t - 1, node), node)
-
-    row, lane = mask_place(group, part)
-    lanes = lax.broadcasted_iota(jnp.int32, (PIECE, LANES), 1)
-    values = jnp.zeros((PIECE, LANES), jnp.int32)
+    table_ref[INFO + 2 * SUB] = group
     for t in range(SUB):
         held = group
         for s in range(t - 1, -1, -1):
             held = before(s, held)
         for c in range(PARTS):
-            values = jnp.where(lanes == lane + t * PARTS + c, mask_ref[0, held * PARTS + c], values)
-    rows = lax.broadcasted_iota(jnp.int32, (PIECE, LANES), 0)
-    tile_ref[...] = jnp.where(rows == row % PIECE, values, 0).astype(F32).astype(BF)
+            table_ref[VALUES + t * PARTS + c] = mask_ref[0, held * PARTS + c]
 
 
 def tables_call(here, matching, mask):
     return pl.pallas_call(
         tables_kernel,
-        out_shape=(
-            jax.ShapeDtypeStruct((GROUPS * PARTS,), jnp.int32),
-            jax.ShapeDtypeStruct((2 * SUB,), jnp.int32),
-            jax.ShapeDtypeStruct((PIECE, LANES), BF),
-        ),
+        out_shape=jax.ShapeDtypeStruct((VALUES + SUB * PARTS,), jnp.int32),
         in_specs=[SMEM, SMEM, SMEM],
-        out_specs=(SMEM, SMEM, VMEM),
+        out_specs=SMEM,
         scratch_shapes=[pltpu.SMEM((GROUPS * (SUB - 1),), jnp.int32)],
         cost_estimate=pl.CostEstimate(flops=2000000, bytes_accessed=4096, transcendentals=0),
     )(here, matching, mask)
 
 
-def pick_kernel(leaf_ref, tile_ref, pieces_ref, out_ref):
-    tile = tile_ref[...]
+def pick_kernel(table_ref, pieces_ref, out_ref):
+    row, lane = mask_place(table_ref[INFO + 2 * SUB], table_ref[INFO])
+    lanes = lax.broadcasted_iota(jnp.int32, (PIECE, LANES), 1)
+    values = jnp.zeros((PIECE, LANES), jnp.int32)
+    for i in range(SUB * PARTS):
+        values = jnp.where(lanes == lane + i, table_ref[VALUES + i], values)
+    rows = lax.broadcasted_iota(jnp.int32, (PIECE, LANES), 0)
+    tile = jnp.where(rows == row % PIECE, values, 0).astype(F32).astype(BF)
 
     def one(far, carry):
         for near in range(XS * CORES):
-            out_ref[far, near] = pieces_ref[leaf_ref[far * XS * CORES + near]]
+            out_ref[far, near] = pieces_ref[table_ref[far * XS * CORES + near]]
         out_ref[far, XS * CORES] = tile
         return carry
 
     lax.fori_loop(0, out_ref.shape[0], one, 0, unroll=4)
 
 
-def pick_call(leaf_table, tile, pieces):
+def pick_call(table, pieces):
     return pl.pallas_call(
         pick_kernel,
         out_shape=jax.ShapeDtypeStruct((YH * YL * ZS, XS * CORES + 1, PIECE, LANES), BF),
-        in_specs=[SMEM, VMEM, VMEM],
+        in_specs=[SMEM, VMEM],
         out_specs=VMEM,
         compiler_params=pltpu.CompilerParams(vmem_limit_bytes=16 << 20),
         cost_estimate=pl.CostEstimate(flops=1000000, bytes_accessed=2 << 20, transcendentals=0),
-    )(leaf_table, tile, pieces)
+    )(table, pieces)
 
 
 def regroup_kernel(got_ref, out_ref):
@@ -192,14 +193,18 @@
     )(left_x, right_x)
 
 
-def sub_epoch_kernel(step_size, level, last, info_ref, mask_ref, sim_ref, *refs):
+def sub_epoch_kernel(step_size, level, last, table_ref, mask_ref, sim_ref, *refs):
     if level == 0:
         all_ref, *refs = refs
     else:
         left_ref, right_ref, *refs = refs
-    *outs, ls, rs, lb, rb, mf, kr, ks = refs
+    *outs, ls, lb, rs0, rb0, rs1, rb1, mf, kr, ks = refs
     blocks, rows, rank = ls.shape
-    part, flip, node = info_ref[0], jnp.int32(0) if level == 0 else info_ref[level], info_ref[SUB + level]
+    part, node = table_ref[INFO], table_ref[INFO + SUB + level]
+    flip = jnp.int32(0) if level == 0 else table_ref[INFO + level]
+
+    def place(slot):
+        return slot if level == 0 else jnp.where(flip == 1, blocks - 1 - slot, slot)
 
     mf[...] = mask_ref[...].astype(F32)
     for b in range(blocks):
@@ -220,25 +225,26 @@
                 put = pl.ds(i * span, span)
                 left = all_ref[i * CORES + core, moved]
                 right = all_ref[(2 + i) * CORES + core, moved]
-                ls[b, put], rs[b, put] = left.astype(F32), right.astype(F32)
-                lb[b, put], rb[b, put] = left, right
+                ls[b, put], rs0[b, put] = left.astype(F32), right.astype(F32)
+                lb[b, put], rb0[b, put] = left, right
         else:
-            ls[b], rs[b] = left_ref[b], right_ref[b].astype(F32)
-            lb[b], rb[b] = left_ref[b].astype(BF), right_ref[b]
-
-    def cycle_step(step, carry):
-        shift = jnp.where(flip == 1, step, blocks - step)
-        places = [lax.rem(b + shift, blocks) for b in range(blocks)]
+            left, right = left_ref[place(b)], right_ref[place(b)]
+            ls[b], rs0[b] = left, right.astype(F32)
+            lb[b], rb0[b] = left.astype(BF), right
+
+    def cycle_step(step, source, target):
+        (rs, rb), (rs_next, rb_next) = source, target
         preds = [
-            lax.dot_general(lb[b], rb[places[b]], (((1,), (1,)), ((), ())), preferred_element_type=F32)
+            lax.dot_general(lb[b], rb[b], (((1,), (1,)), ((), ())), preferred_element_type=F32)
             for b in range(blocks)
         ]
         resids = []
         for b in range(blocks):
-            row = jnp.where(flip == 1, places[b], b)
-            col = jnp.where(flip == 1, b, places[b])
-            resids.append((ks[col, pl.ds(row, 1)] * (preds[b] - sim_ref[b, places[b]])).astype(BF))
-        grads_l = [jnp.dot(resids[b], rb[places[b]], preferred_element_type=F32) for b in range(blocks)]
+            left, right = place(b), place(lax.rem(b + blocks - step, blocks))
+            row = jnp.where(flip == 1, right, left)
+            col = jnp.where(flip == 1, left, right)
+            resids.append((ks[col, pl.ds(row, 1)] * (preds[b] - sim_ref[left, right])).astype(BF))
+        grads_l = [jnp.dot(resids[b], rb[b], preferred_element_type=F32) for b in range(blocks)]
         grads_r = [
             lax.dot_general(resids[b], lb[b], (((0,), (0,)), ((), ())), preferred_element_type=F32)
             for b in range(blocks)
@@ -248,40 +254,46 @@
             ls[b] = new_left
             lb[b] = new_left.astype(BF)
         for b in range(blocks):
-            new_right = rs[places[b]] - step_size * grads_r[b]
-            rs[places[b]] = new_right
-            rb[places[b]] = new_right.astype(BF)
+            new_right = rs[b] - step_size * grads_r[b]
+            rs_next[(b + 1) % blocks] = new_right
+            rb_next[(b + 1) % blocks] = new_right.astype(BF)
+
+    def two_steps(pair, carry):
+        cycle_step(2 * pair, (rs0, rb0), (rs1, rb1))
+        cycle_step(2 * pair + 1, (rs1, rb1), (rs0, rb0))
         return carry
 
-    lax.fori_loop(0, blocks, cycle_step, 0)
+    lax.fori_loop(0, blocks // 2, two_steps, 0)
     if last:
         uo_ref, vo_ref = outs
 
         @pl.when(flip == 0)
         def _():
-            uo_ref[...] = ls[part]
-            vo_ref[...] = rs[part]
+            uo_ref[...] = ls[place(part)]
+            vo_ref[...] = rs0[place(part)]
 
         @pl.when(flip == 1)
         def _():
-            uo_ref[...] = rs[part]
-            vo_ref[...] = ls[part]
+            uo_ref[...] = rs0[place(part)]
+            vo_ref[...] = ls[place(part)]
     else:
         kept_ref, sent_ref = outs
-        same = info_ref[1 + level] == flip
+        same = table_ref[INFO + 1 + level] == flip
 
         @pl.when(same)
         def _():
-            kept_ref[...] = ls[...]
-            sent_ref[...] = lb[...]
+            for b in range(blocks):
+                kept_ref[place(b)] = ls[b]
+                sent_ref[place(b)] = lb[b]
 
         @pl.when(jnp.logical_not(same))
         def _():
-            kept_ref[...] = rs[...]
-            sent_ref[...] = rb[...]
-
-
-def sub_epoch_call(level, rows, info, mask, sims, *arrays):
+            for b in range(blocks):
+                kept_ref[place(b)] = rs0[b]
+                sent_ref[place(b)] = rb0[b]
+
+
+def sub_epoch_call(level, rows, table, mask, sims, *arrays):
     rank, last = LANES, level + 1 == SUB
     whole = (PARTS, rows, rank)
     if last:
@@ -293,11 +305,8 @@
         out_shape=outs,
         in_specs=[SMEM] + [VMEM] * (2 + len(arrays)),
         out_specs=(VMEM, VMEM),
-        scratch_shapes=[
-            pltpu.VMEM(whole, F32),
-            pltpu.VMEM(whole, F32),
-            pltpu.VMEM(whole, BF),
-            pltpu.VMEM(whole, BF),
+        scratch_shapes=[pltpu.VMEM(whole, F32), pltpu.VMEM(whole, BF)] * 3
+        + [
             pltpu.VMEM(mask.shape, F32),
             pltpu.VMEM((PARTS, LANES), F32),
             pltpu.VMEM((PARTS, PARTS, LANES), F32),
@@ -308,52 +317,50 @@
             bytes_accessed=6 << 20,
             transcendentals=0,
         ),
-    )(info, mask, sims, *arrays)
-
-
-def swapped(array, bit):
-    return lax.ppermute(array, BLK, [(i, i ^ (1 << bit)) for i in range(PARTS)])
+    )(table, mask, sims, *arrays)
+
+
+def swapped(array, stride):
+    return lax.ppermute(array, BLK, [(i, i ^ stride) for i in range(PARTS)])
 
 
 def spread(array, axes):
     return lax.all_to_all(array, axes, split_axis=0, concat_axis=0, tiled=True)
-
-
-def halves_out(array, bit, core):
-    half = array.shape[0] // 2
-    return swapped(lax.dynamic_slice_in_dim(array, core * half, half, 0), bit)
-
-
-def halves_in(first, core):
-    second = swapped(first, 0)
-    return jnp.where(core == 0, jnp.concatenate([first, second]), jnp.concatenate([second, first]))
 
 
 def local(features, factor_u, factor_v, tile_mask, matching):
     group = lax.axis_index(GRP).astype(jnp.int32)
     part = lax.axis_index(BLK).astype(jnp.int32)
+    core = lax.axis_index("core")
     slot_rows, rank = factor_u.shape
-    bits = [(part >> t) & 1 for t in range(SUB - 1)]
+    bits = [part // stride % 2 for stride in STRIDES]
 
     pieces = spread(pack_call(features, factor_u, factor_v).reshape(GROUPS, PIECE, rank), GRP)
-    leaf_table, info, tile = tables_call(jnp.stack([group, part]), matching, tile_mask)
-    got = spread(pick_call(leaf_table, tile, pieces), FAR)
+    table = tables_call(jnp.stack([group, part]), matching, tile_mask)
+    got = spread(pick_call(table, pieces), FAR)
     got = spread(regroup_call(got), NEAR).reshape(XS * CORES, -1, rank)
     half = YL * slot_rows // 2
-    left_x = got[:, :half]
+    x0 = got[:, :half]
     mask = got[:, 2 * half :]
 
-    coming_x = swapped(left_x, 0)
-    kept, sent = sub_epoch_call(0, slot_rows, info, mask, sim_call(slot_rows, got, got), got)
+    def work(level, sims, *arrays):
+        return sub_epoch_call(level, slot_rows, table, mask, sims, *arrays)
+
+    left_x, coming_x = x0, swapped(x0, STRIDES[0])
+    kept, sent = work(0, sim_call(slot_rows, got, got), got)
     for level in range(1, SUB):
-        right = swapped(sent, level - 1)
+        right = swapped(sent, STRIDES[level - 1])
         kept, coming_x = lax.optimization_barrier((kept, coming_x))
-        right_x = coming_x if level == 1 else halves_in(coming_x, bits[0])
+        right_x = coming_x
+        if level > 1:
+            other = swapped(coming_x, STRIDES[0])
+            right_x = jnp.where(core == 0, jnp.concatenate([coming_x, other]), jnp.concatenate([other, coming_x]))
         sims = sim_call(slot_rows, left_x, right_x)
         if level + 1 < SUB:
             left_x = jnp.where(bits[level] == bits[level - 1], left_x, right_x)
-            coming_x = halves_out(left_x, level, bits[0])
-        kept, sent = sub_epoch_call(level, slot_rows, info, mask, sims, kept, right)
+            near = left_x.shape[0] // 2
+            coming_x = swapped(lax.dynamic_slice_in_dim(left_x, core * near, near, 0), STRIDES[level])
+        kept, sent = work(level, sims, kept, right)
     return kept, sent
 
 

time: 162 us -> 163 us (level)
  waiting for transfers between devices: 30.5 us -> 32.2 us
    ppermute x8, waiting for transfers between devices: 20.6 us -> 22.3 us  [swapped(): return lax.ppermute(array, BLK, [(i, i ^ stride) for i in range(PARTS)])]
  transfers between devices with their start and end apart: 9 -> 9, of which waited for: 5 -> 4; matrix products, arithmetic and copies ran while one was open for 1% -> 1% of each run, Pallas kernels for 13% -> 13%
where the time goes in v3:
time: 163 us
  blocking collectives  56 us (34%)
  starting transfers between devices  42.8 us (26%)
  waiting for transfers between devices  32.2 us (20%)
  Pallas kernels  29.2 us (18%)
    all_to_all x2, blocking collectives, spread(): return lax.all_to_all(array, axes, split_axis=0, concat_axis=0, tiled=True)  56 us
    ppermute x8, starting transfers between devices, swapped(): return lax.ppermute(array, BLK, [(i, i ^ stride) for i in range(PARTS)])  23.2 us
    ppermute x8, waiting for transfers between devices, swapped(): return lax.ppermute(array, BLK, [(i, i ^ stride) for i in range(PARTS)])  22.3 us
    pallas_call x4, Pallas kernels, sub_epoch_call(): pl.pallas_call(functools.partial(sub_epoch_kernel, 4.0 / rows, level, las...  19.9 us
    all_to_all x1, starting transfers between devices, spread(): return lax.all_to_all(array, axes, split_axis=0, concat_axis=0, tiled=True)  19.6 us
    all_to_all x1, waiting for transfers between devices, spread(): return lax.all_to_all(array, axes, split_axis=0, concat_axis=0, tiled=True)  9.86 us
  transfers between devices with their start and end apart: 9, of which 4 were waited for; matrix products, arithmetic and copies ran while one was open for 1% of the time, Pallas kernels for 13%

profile of v3, /device:TPU:1, one launch (start us, length us, event | category | flops | bytes accessed | tf_op | source)
XLA Modules:
  0.0 162.7 jit_solution(8240818906594253418)
XLA Ops:
  0.6 1.6 shard_map.69
  2.2 19.6 %all-to-all-start = ((bf16[64,8,128]{2,1,0:T(8,128)(2,1)}), bf16[64,8,128]{2,1,0:T(8,128)(2,1)S(1)}, u32[]{:S(2)}, u32[]{:S(2)}) async-start(bf16[64,8,128]{2,1,0:T(8,128)(2,1)} %bitcast.10), calls=%async_computation | async-start | bytes 262144 | tf_op jit(solution)/shard_map/all_to_all | solution.py:328
  21.9 0.7 pad_add_fusion.here_ref
  22.5 3.1 %shard_map.68.table_ref = s32[560]{0:T(1024)} custom-call(s32[2]{0:T(128)} %pad_add_fusion.here_ref, s32[3,64]{1,0:T(4,128)} %matching_ref.1, s32[1,512]{1,0:T(1,128)} %mask_ref.1), custom_call_target="tpu_custom_call" | custom-call | flops 2000000 | bytes 4096 | tf_op jit(solution)/shard_map/pallas_call | solution.py:96
  25.6 9.9 %all-to-all-done.pieces_ref = bf16[64,8,128]{2,1,0:T(8,128)(2,1)S(1)} async-done(((bf16[64,8,128]{2,1,0:T(8,128)(2,1)}), bf16[64,8,128]{2,1,0:T(8,128)(2,1)S(1)}, u32[]{:S(2)}, u32[]{:S(2)}) %all-to-all-start) | async-done | bytes 131104 | tf_op jit(solution)/shard_map/all_to_all | solution.py:328
  35.5 0.0 copy-start
  35.5 0.7 copy-done
  36.2 1.2 shard_map.70
  37.4 33.5 %all_to_all.15.got_ref = bf16[64,9,8,128]{3,2,1,0:T(8,128)(2,1)S(1)} all-to-all(bf16[64,9,8,128]{3,2,1,0:T(8,128)(2,1)S(1)} %shard_map.70), channel_id=1, replica_groups=mesh['yh'=2,'x'=4,'z'=8,'yl'=4,'core'=2] {'yh','yl','z'}, dimensions={0} | all-to-all | bytes 2359296 | tf_op jit(solution)/shard_map/all_to_all | solution.py:328
  70.9 0.2 shard_map.71
  71.1 22.5 %all_to_all.16 = bf16[8,66,8,128]{3,2,1,0:T(8,128)(2,1)S(1)} all-to-all(bf16[8,66,8,128]{3,2,1,0:T(8,128)(2,1)S(1)} %shard_map.71), channel_id=1, replica_groups=mesh['yh'=2,'x'=4,'z'=8,'yl'=4,'core'=2] {'x','core'}, dimensions={0} | all-to-all | bytes 2162688 | tf_op jit(solution)/shard_map/all_to_all | solution.py:328
  93.7 2.5 %collective-permute-start = (bf16[8,256,128]{2,1,0:T(8,128)(2,1)S(1)}, bf16[8,256,128]{2,1,0:T(8,128)(2,1)S(1)}, u32[]{:S(2)}, u32[]{:S(2)}) collective-permute-start(bf16[8,256,128]{2,1,0:T(8,128)(2,1)S(1)} %slice.9.xl_ref), channel_id=1, source_target_pairs={{0,1},{1,0},{2,3},{3,2},{4,5},{5,4},{6,7},{7,6},{8,9},{9,8},{10,11... | collective-permute-start | bytes 1572872 | tf_op jit(solution)/shard_map/ppermute | solution.py:324
  96.2 0.0 copy-start.1
  96.2 0.8 shard_map.72.sim_ref
  97.0 0.0 copy-done.1
  97.0 4.8 %shard_map.73 = (f32[8,128,128]{2,1,0:T(8,128)S(1)}, bf16[8,128,128]{2,1,0:T(8,128)(2,1)S(1)}) custom-call(s32[560]{0:T(1024)S(1)} %copy-done.1, bf16[8,16,128]{2,1,0:T(8,128)(2,1)S(1)} %slice.8.mask_ref, f32[8,8,128,128]{3,2,1,0:T(8,128)S(1)} %shard_map.72.sim_ref, bf16[8,528,128]{2,1,0:T(8,128)(2,1)S(1)} %bitcast.8), custom_call_target="tpu_custom_call" | custom-call | flops 805306368 | bytes 6291456 | tf_op jit(solution)/shard_map/pallas_call | solution.py:303
  101.8 1.9 %collective-permute-start.1 = (bf16[8,128,128]{2,1,0:T(8,128)(2,1)S(1)}, bf16[8,128,128]{2,1,0:T(8,128)(2,1)S(1)}, u32[]{:S(2)}, u32[]{:S(2)}) collective-permute-start(bf16[8,128,128]{2,1,0:T(8,128)(2,1)S(1)} %get-tuple-element.17), channel_id=1, source_target_pairs={{0,1},{1,0},{2,3},{3,2},{4,5},{5,4},{6,7},{7,6},{8,9},{9,8},{10,11... | collective-permute-start | bytes 786440 | tf_op jit(solution)/shard_map/ppermute | solution.py:324
  103.8 0.0 collective-permute-done.xr_ref
  103.8 0.1 broadcast_select_fusion.xl_ref
  103.9 4.8 %collective-permute-start.2 = (bf16[4,256,128]{2,1,0:T(8,128)(2,1)S(1)}, bf16[4,256,128]{2,1,0:T(8,128)(2,1)S(1)}, u32[]{:S(2)}, u32[]{:S(2)}) collective-permute-start(bf16[4,256,128]{2,1,0:T(8,128)(2,1)S(1)} %constant_dynamic-slice_fusion.1), channel_id=1, source_target_pairs={{0,4},{1,5},{2,6},{3,7},{4,0},{5,1},{6,2},{7,3},{8,12},{9,13},{10,... | collective-permute-start | bytes 786440 | tf_op jit(solution)/shard_map/ppermute | solution.py:324
  108.7 0.8 shard_map.74.sim_ref
  109.5 0.0 collective-permute-done.1.refs_1_
  109.5 4.8 %shard_map.75 = (f32[8,128,128]{2,1,0:T(8,128)S(1)}, bf16[8,128,128]{2,1,0:T(8,128)(2,1)S(1)}) custom-call(s32[560]{0:T(1024)S(1)} %copy-done.1, bf16[8,16,128]{2,1,0:T(8,128)(2,1)S(1)} %slice.8.mask_ref, f32[8,8,128,128]{3,2,1,0:T(8,128)S(1)} %shard_map.74.sim_ref, f32[8,128,128]{2,1,0:T(8,128)S(1)} %get-tuple-element.16.refs_0_, ...), custom_call_target="tpu_custom_call" | custom-call | flops 805306368 | bytes 6291456 | tf_op jit(solution)/shard_map/pallas_call | solution.py:303
  114.3 6.5 %collective-permute-done.2 = bf16[4,256,128]{2,1,0:T(8,128)(2,1)S(1)} collective-permute-done((bf16[4,256,128]{2,1,0:T(8,128)(2,1)S(1)}, bf16[4,256,128]{2,1,0:T(8,128)(2,1)S(1)}, u32[]{:S(2)}, u32[]{:S(2)}) %collective-permute-start.2) | collective-permute-done | bytes 262176 | tf_op jit(solution)/shard_map/ppermute | solution.py:324
  120.8 2.6 %collective-permute-start.3 = (bf16[4,256,128]{2,1,0:T(8,128)(2,1)S(1)}, bf16[4,256,128]{2,1,0:T(8,128)(2,1)S(1)}, u32[]{:S(2)}, u32[]{:S(2)}) collective-permute-start(bf16[4,256,128]{2,1,0:T(8,128)(2,1)S(1)} %collective-permute-done.2), channel_id=1, source_target_pairs={{0,1},{1,0},{2,3},{3,2},{4,5},{5,4},{6,7},{7,6},{8,9},{9,8},{10,11... | collective-permute-start | bytes 786440 | tf_op jit(solution)/shard_map/ppermute | solution.py:324
  123.5 1.9 %collective-permute-start.4 = (bf16[8,128,128]{2,1,0:T(8,128)(2,1)S(1)}, bf16[8,128,128]{2,1,0:T(8,128)(2,1)S(1)}, u32[]{:S(2)}, u32[]{:S(2)}) collective-permute-start(bf16[8,128,128]{2,1,0:T(8,128)(2,1)S(1)} %get-tuple-element.21), channel_id=1, source_target_pairs={{0,4},{1,5},{2,6},{3,7},{4,0},{5,1},{6,2},{7,3},{8,12},{9,13},{10,... | collective-permute-start | bytes 786440 | tf_op jit(solution)/shard_map/ppermute | solution.py:324
  125.4 0.0 collective-permute-done.3
  125.4 0.1 broadcast_select_fusion.1
  125.6 4.8 %collective-permute-start.5 = (bf16[4,256,128]{2,1,0:T(8,128)(2,1)S(1)}, bf16[4,256,128]{2,1,0:T(8,128)(2,1)S(1)}, u32[]{:S(2)}, u32[]{:S(2)}) collective-permute-start(bf16[4,256,128]{2,1,0:T(8,128)(2,1)S(1)} %constant_dynamic-slice_fusion), channel_id=1, source_target_pairs={{0,2},{1,3},{2,0},{3,1},{4,6},{5,7},{6,4},{7,5},{8,10},{9,11},{10,... | collective-permute-start | bytes 786440 | tf_op jit(solution)/shard_map/ppermute | solution.py:324
  130.4 0.8 shard_map.76.sim_ref
  131.2 8.8 %collective-permute-done.4.refs_1_ = bf16[8,128,128]{2,1,0:T(8,128)(2,1)S(1)} collective-permute-done((bf16[8,128,128]{2,1,0:T(8,128)(2,1)S(1)}, bf16[8,128,128]{2,1,0:T(8,128)(2,1)S(1)}, u32[]{:S(2)}, u32[]{:S(2)}) %collective-permute-start.4) | collective-permute-done | bytes 262176 | tf_op jit(solution)/shard_map/ppermute | solution.py:324
  140.0 4.8 %shard_map.77 = (f32[8,128,128]{2,1,0:T(8,128)S(1)}, bf16[8,128,128]{2,1,0:T(8,128)(2,1)S(1)}) custom-call(s32[560]{0:T(1024)S(1)} %copy-done.1, bf16[8,16,128]{2,1,0:T(8,128)(2,1)S(1)} %slice.8.mask_ref, f32[8,8,128,128]{3,2,1,0:T(8,128)S(1)} %shard_map.76.sim_ref, f32[8,128,128]{2,1,0:T(8,128)S(1)} %get-tuple-element.20.refs_0_, ...), custom_call_target="tpu_custom_call" | custom-call | flops 805306368 | bytes 6291456 | tf_op jit(solution)/shard_map/pallas_call | solution.py:303
  144.8 0.0 collective-permute-done.5
  144.8 2.7 %collective-permute-start.6 = (bf16[4,256,128]{2,1,0:T(8,128)(2,1)S(1)}, bf16[4,256,128]{2,1,0:T(8,128)(2,1)S(1)}, u32[]{:S(2)}, u32[]{:S(2)}) collective-permute-start(bf16[4,256,128]{2,1,0:T(8,128)(2,1)S(1)} %collective-permute-done.5), channel_id=1, source_target_pairs={{0,1},{1,0},{2,3},{3,2},{4,5},{5,4},{6,7},{7,6},{8,9},{9,8},{10,11... | collective-permute-start | bytes 786440 | tf_op jit(solution)/shard_map/ppermute | solution.py:324
  147.5 1.9 %collective-permute-start.7 = (bf16[8,128,128]{2,1,0:T(8,128)(2,1)S(1)}, bf16[8,128,128]{2,1,0:T(8,128)(2,1)S(1)}, u32[]{:S(2)}, u32[]{:S(2)}) collective-permute-start(bf16[8,128,128]{2,1,0:T(8,128)(2,1)S(1)} %get-tuple-element.25), channel_id=1, source_target_pairs={{0,2},{1,3},{2,0},{3,1},{4,6},{5,7},{6,4},{7,5},{8,10},{9,11},{10,... | collective-permute-start | bytes 786440 | tf_op jit(solution)/shard_map/ppermute | solution.py:324
  149.4 0.0 collective-permute-done.6
  149.4 0.1 maximum_select_fusion.1.xr_ref
  149.5 0.8 shard_map.78.sim_ref
  150.3 7.0 %collective-permute-done.7.refs_1_ = bf16[8,128,128]{2,1,0:T(8,128)(2,1)S(1)} collective-permute-done((bf16[8,128,128]{2,1,0:T(8,128)(2,1)S(1)}, bf16[8,128,128]{2,1,0:T(8,128)(2,1)S(1)}, u32[]{:S(2)}, u32[]{:S(2)}) %collective-permute-start.7) | collective-permute-done | bytes 262176 | tf_op jit(solution)/shard_map/ppermute | solution.py:324
  157.3 5.4 %shard_map.79 = (f32[128,128]{1,0:T(8,128)}, f32[128,128]{1,0:T(8,128)}) custom-call(s32[560]{0:T(1024)S(1)} %copy-done.1, bf16[8,16,128]{2,1,0:T(8,128)(2,1)S(1)} %slice.8.mask_ref, f32[8,8,128,128]{3,2,1,0:T(8,128)S(1)} %shard_map.78.sim_ref, f32[8,128,128]{2,1,0:T(8,128)S(1)} %get-tuple-element.24.refs_0_, ...), custom_call_target="tpu_custom_call" | custom-call | flops 805306368 | bytes 6291456 | tf_op jit(solution)/shard_map/pallas_call | solution.py:303
  (4 shorter events, 0.1 us)
Async XLA Ops:
  2.2 33.2 %all-to-all-start = ((bf16[64,8,128]{2,1,0:T(8,128)(2,1)}), bf16[64,8,128]{2,1,0:T(8,128)(2,1)S(1)}, u32[]{:S(2)}, u32[]{:S(2)}) async-start(bf16[64,8,128]{2,1,0:T(8,128)(2,1)} %bitcast.10), calls=%async_computation | async-start | bytes 262144 | tf_op jit(solution)/shard_map/all_to_all | solution.py:328
  35.5 0.7 copy-start
  93.7 10.1 %collective-permute-start = (bf16[8,256,128]{2,1,0:T(8,128)(2,1)S(1)}, bf16[8,256,128]{2,1,0:T(8,128)(2,1)S(1)}, u32[]{:S(2)}, u32[]{:S(2)}) collective-permute-start(bf16[8,256,128]{2,1,0:T(8,128)(2,1)S(1)} %slice.9.xl_ref), channel_id=1, source_target_pairs={{0,1},{1,0},{2,3},{3,2},{4,5},{5,4},{6,7},{7,6},{8,9},{9,8},{10,11... | collective-permute-start | bytes 1572872 | tf_op jit(solution)/shard_map/ppermute | solution.py:324
  96.2 0.8 copy-start.1
  101.8 7.6 %collective-permute-start.1 = (bf16[8,128,128]{2,1,0:T(8,128)(2,1)S(1)}, bf16[8,128,128]{2,1,0:T(8,128)(2,1)S(1)}, u32[]{:S(2)}, u32[]{:S(2)}) collective-permute-start(bf16[8,128,128]{2,1,0:T(8,128)(2,1)S(1)} %get-tuple-element.17), channel_id=1, source_target_pairs={{0,1},{1,0},{2,3},{3,2},{4,5},{5,4},{6,7},{7,6},{8,9},{9,8},{10,11... | collective-permute-start | bytes 786440 | tf_op jit(solution)/shard_map/ppermute | solution.py:324
  103.9 16.9 %collective-permute-start.2 = (bf16[4,256,128]{2,1,0:T(8,128)(2,1)S(1)}, bf16[4,256,128]{2,1,0:T(8,128)(2,1)S(1)}, u32[]{:S(2)}, u32[]{:S(2)}) collective-permute-start(bf16[4,256,128]{2,1,0:T(8,128)(2,1)S(1)} %constant_dynamic-slice_fusion.1), channel_id=1, source_target_pairs={{0,4},{1,5},{2,6},{3,7},{4,0},{5,1},{6,2},{7,3},{8,12},{9,13},{10,... | collective-permute-start | bytes 786440 | tf_op jit(solution)/shard_map/ppermute | solution.py:324
  120.8 4.6 %collective-permute-start.3 = (bf16[4,256,128]{2,1,0:T(8,128)(2,1)S(1)}, bf16[4,256,128]{2,1,0:T(8,128)(2,1)S(1)}, u32[]{:S(2)}, u32[]{:S(2)}) collective-permute-start(bf16[4,256,128]{2,1,0:T(8,128)(2,1)S(1)} %collective-permute-done.2), channel_id=1, source_target_pairs={{0,1},{1,0},{2,3},{3,2},{4,5},{5,4},{6,7},{7,6},{8,9},{9,8},{10,11... | collective-permute-start | bytes 786440 | tf_op jit(solution)/shard_map/ppermute | solution.py:324
  123.5 16.5 %collective-permute-start.4 = (bf16[8,128,128]{2,1,0:T(8,128)(2,1)S(1)}, bf16[8,128,128]{2,1,0:T(8,128)(2,1)S(1)}, u32[]{:S(2)}, u32[]{:S(2)}) collective-permute-start(bf16[8,128,128]{2,1,0:T(8,128)(2,1)S(1)} %get-tuple-element.21), channel_id=1, source_target_pairs={{0,4},{1,5},{2,6},{3,7},{4,0},{5,1},{6,2},{7,3},{8,12},{9,13},{10,... | collective-permute-start | bytes 786440 | tf_op jit(solution)/shard_map/ppermute | solution.py:324
  125.6 19.2 %collective-permute-start.5 = (bf16[4,256,128]{2,1,0:T(8,128)(2,1)S(1)}, bf16[4,256,128]{2,1,0:T(8,128)(2,1)S(1)}, u32[]{:S(2)}, u32[]{:S(2)}) collective-permute-start(bf16[4,256,128]{2,1,0:T(8,128)(2,1)S(1)} %constant_dynamic-slice_fusion), channel_id=1, source_target_pairs={{0,2},{1,3},{2,0},{3,1},{4,6},{5,7},{6,4},{7,5},{8,10},{9,11},{10,... | collective-permute-start | bytes 786440 | tf_op jit(solution)/shard_map/ppermute | solution.py:324
  144.8 4.6 %collective-permute-start.6 = (bf16[4,256,128]{2,1,0:T(8,128)(2,1)S(1)}, bf16[4,256,128]{2,1,0:T(8,128)(2,1)S(1)}, u32[]{:S(2)}, u32[]{:S(2)}) collective-permute-start(bf16[4,256,128]{2,1,0:T(8,128)(2,1)S(1)} %collective-permute-done.5), channel_id=1, source_target_pairs={{0,1},{1,0},{2,3},{3,2},{4,5},{5,4},{6,7},{7,6},{8,9},{9,8},{10,11... | collective-permute-start | bytes 786440 | tf_op jit(solution)/shard_map/ppermute | solution.py:324
  147.5 9.8 %collective-permute-start.7 = (bf16[8,128,128]{2,1,0:T(8,128)(2,1)S(1)}, bf16[8,128,128]{2,1,0:T(8,128)(2,1)S(1)}, u32[]{:S(2)}, u32[]{:S(2)}) collective-permute-start(bf16[8,128,128]{2,1,0:T(8,128)(2,1)S(1)} %get-tuple-element.25), channel_id=1, source_target_pairs={{0,2},{1,3},{2,0},{3,1},{4,6},{5,7},{6,4},{7,5},{8,10},{9,11},{10,... | collective-permute-start | bytes 786440 | tf_op jit(solution)/shard_map/ppermute | solution.py:324

commit v4 on v3

--- a/solution.py
+++ b/solution.py
@@ -132,23 +132,27 @@
     )(table, pieces)
 
 
-def regroup_kernel(got_ref, out_ref):
-    far = YH * YL * ZS
+def regroup_kernel(got_ref, x_ref, uv_ref):
+    half = YL * ZS
     for near in range(XS * CORES):
-        out_ref[near, :far] = got_ref[:, near]
+        x_ref[near] = got_ref[:half, near]
+        uv_ref[near, :half] = got_ref[half:, near]
     for yh in range(YH):
-        span = far // YH
-        total = jnp.sum(got_ref[yh * span : (yh + 1) * span, XS * CORES].astype(F32), axis=0).astype(BF)
+        total = jnp.sum(got_ref[yh * half : (yh + 1) * half, XS * CORES].astype(F32), axis=0).astype(BF)
         for near in range(XS * CORES):
-            out_ref[near, far + yh] = total
+            uv_ref[near, half + yh] = total
 
 
 def regroup_call(got):
+    half = YL * ZS
     return pl.pallas_call(
         regroup_kernel,
-        out_shape=jax.ShapeDtypeStruct((XS * CORES, YH * YL * ZS + YH, PIECE, LANES), BF),
+        out_shape=(
+            jax.ShapeDtypeStruct((XS * CORES, half, PIECE, LANES), BF),
+            jax.ShapeDtypeStruct((XS * CORES, half + YH, PIECE, LANES), BF),
+        ),
         in_specs=[VMEM],
-        out_specs=VMEM,
+        out_specs=(VMEM, VMEM),
         compiler_params=pltpu.CompilerParams(vmem_limit_bytes=16 << 20),
         cost_estimate=pl.CostEstimate(flops=1000000, bytes_accessed=2 << 20, transcendentals=0),
     )(got)
@@ -220,7 +224,7 @@
     for b in range(blocks):
         if level == 0:
             yl, core = b // CORES, b % CORES
-            moved = pl.ds((YL + yl) * span, span)
+            moved = pl.ds(yl * span, span)
             for i in range(2):
                 put = pl.ds(i * span, span)
                 left = all_ref[i * CORES + core, moved]
@@ -232,38 +236,47 @@
             ls[b], rs0[b] = left, right.astype(F32)
             lb[b], rb0[b] = left.astype(BF), right
 
-    def cycle_step(step, source, target):
+    def cycle_step(step, source, target, spots):
         (rs, rb), (rs_next, rb_next) = source, target
         preds = [
-            lax.dot_general(lb[b], rb[b], (((1,), (1,)), ((), ())), preferred_element_type=F32)
-            for b in range(blocks)
+            lax.dot_general(lb[b], rb[b], (((1,), (1,)), ((), ())), preferred_element_type=F32) for b in spots
         ]
         resids = []
-        for b in range(blocks):
+        for b, pred in zip(spots, preds):
             left, right = place(b), place(lax.rem(b + blocks - step, blocks))
             row = jnp.where(flip == 1, right, left)
             col = jnp.where(flip == 1, left, right)
-            resids.append((ks[col, pl.ds(row, 1)] * (preds[b] - sim_ref[left, right])).astype(BF))
-        grads_l = [jnp.dot(resids[b], rb[b], preferred_element_type=F32) for b in range(blocks)]
+            resids.append((ks[col, pl.ds(row, 1)] * (pred - sim_ref[left, right])).astype(BF))
+        grads_l = [jnp.dot(resid, rb[b], preferred_element_type=F32) for b, resid in zip(spots, resids)]
         grads_r = [
-            lax.dot_general(resids[b], lb[b], (((0,), (0,)), ((), ())), preferred_element_type=F32)
-            for b in range(blocks)
+            lax.dot_general(resid, lb[b], (((0,), (0,)), ((), ())), preferred_element_type=F32)
+            for b, resid in zip(spots, resids)
         ]
-        for b in range(blocks):
-            new_left = ls[b] - step_size * grads_l[b]
+        for b, grad in zip(spots, grads_l):
+            new_left = ls[b] - step_size * grad
             ls[b] = new_left
             lb[b] = new_left.astype(BF)
-        for b in range(blocks):
-            new_right = rs[b] - step_size * grads_r[b]
-            rs_next[(b + 1) % blocks] = new_right
-            rb_next[(b + 1) % blocks] = new_right.astype(BF)
-
-    def two_steps(pair, carry):
-        cycle_step(2 * pair, (rs0, rb0), (rs1, rb1))
-        cycle_step(2 * pair + 1, (rs1, rb1), (rs0, rb0))
-        return carry
-
-    lax.fori_loop(0, blocks // 2, two_steps, 0)
+        for b, grad in zip(spots, grads_r):
+            new_right = rs[b] - step_size * grad
+            after = (b + 1) % blocks if isinstance(b, int) else lax.rem(b + 1, blocks)
+            rs_next[after] = new_right
+            rb_next[after] = new_right.astype(BF)
+
+    turns = ((rs0, rb0), (rs1, rb1))
+    every = list(range(blocks))
+    if last:
+        for step in range(blocks):
+            count = blocks + 1 - step
+            mine = [lax.rem(place(part) + blocks - i, blocks) for i in range(count)]
+            cycle_step(step, turns[step % 2], turns[1 - step % 2], every if count >= blocks else mine)
+    else:
+
+        def two_steps(pair, carry):
+            cycle_step(2 * pair, *turns, every)
+            cycle_step(2 * pair + 1, *turns[::-1], every)
+            return carry
+
+        lax.fori_loop(0, blocks // 2, two_steps, 0)
     if last:
         uo_ref, vo_ref = outs
 
@@ -338,30 +351,39 @@
     pieces = spread(pack_call(features, factor_u, factor_v).reshape(GROUPS, PIECE, rank), GRP)
     table = tables_call(jnp.stack([group, part]), matching, tile_mask)
     got = spread(pick_call(table, pieces), FAR)
-    got = spread(regroup_call(got), NEAR).reshape(XS * CORES, -1, rank)
-    half = YL * slot_rows // 2
-    x0 = got[:, :half]
-    mask = got[:, 2 * half :]
+    x0, uv = regroup_call(got)
+    x0 = spread(x0, NEAR).reshape(XS * CORES, -1, rank)
+    uv = spread(uv, NEAR).reshape(XS * CORES, -1, rank)
+    mask = uv[:, x0.shape[1] :]
 
     def work(level, sims, *arrays):
         return sub_epoch_call(level, slot_rows, table, mask, sims, *arrays)
 
-    left_x, coming_x = x0, swapped(x0, STRIDES[0])
-    kept, sent = work(0, sim_call(slot_rows, got, got), got)
-    for level in range(1, SUB):
-        right = swapped(sent, STRIDES[level - 1])
-        kept, coming_x = lax.optimization_barrier((kept, coming_x))
-        right_x = coming_x
-        if level > 1:
-            other = swapped(coming_x, STRIDES[0])
-            right_x = jnp.where(core == 0, jnp.concatenate([coming_x, other]), jnp.concatenate([other, coming_x]))
-        sims = sim_call(slot_rows, left_x, right_x)
-        if level + 1 < SUB:
-            left_x = jnp.where(bits[level] == bits[level - 1], left_x, right_x)
-            near = left_x.shape[0] // 2
-            coming_x = swapped(lax.dynamic_slice_in_dim(left_x, core * near, near, 0), STRIDES[level])
-        kept, sent = work(level, sims, kept, right)
-    return kept, sent
+    def joined(first):
+        second = swapped(first, STRIDES[0])
+        return jnp.where(core == 0, jnp.concatenate([first, second]), jnp.concatenate([second, first]))
+
+    def half_of(x):
+        return lax.dynamic_slice_in_dim(x, core * (XS * CORES // 2), XS * CORES // 2, 0)
+
+    y0 = swapped(x0, STRIDES[0])
+    sims = sim_call(slot_rows, x0, x0)
+    x1 = jnp.where(bits[1] == bits[0], x0, y0)
+    first = swapped(half_of(x1), STRIDES[1])
+    sims_next = sim_call(slot_rows, x0, y0)
+    kept, sent = work(0, sims, uv)
+    right = swapped(sent, STRIDES[0])
+    kept, first = lax.optimization_barrier((kept, first))
+    y1 = joined(first)
+    x2 = jnp.where(bits[2] == bits[1], x1, y1)
+    first = swapped(half_of(x2), STRIDES[2])
+    kept, sent = work(1, sims_next, kept, right)
+    right = swapped(sent, STRIDES[1])
+    sims = sim_call(slot_rows, x1, y1)
+    kept, sent = work(2, sims, kept, right)
+    right = swapped(sent, STRIDES[2])
+    kept, first = lax.optimization_barrier((kept, first))
+    return work(3, sim_call(slot_rows, x2, joined(first)), kept, right)
 
 
 def solution(mesh):

time: 163 us -> 162 us (level)
  blocking collectives: 56 us -> 49.5 us
  starting transfers between devices: 42.8 us -> 47.6 us
  waiting for transfers between devices: 32.2 us -> 27.6 us
  local copies, waits for them, and re-layouts: 0.79 us -> 4.88 us
    ppermute x8, waiting for transfers between devices: 22.3 us -> 15.6 us  [swapped(): return lax.ppermute(array, BLK, [(i, i ^ stride) for i in range(PARTS)])]
    all_to_all x2, blocking collectives: 56 us -> 49.5 us  [spread(): return lax.all_to_all(array, axes, split_axis=0, concat_axis=0, tiled=True)]
    unnamed x4 -> x8, local copies, waits for them, and re-layouts: 0.69 us -> 4.82 us
    all_to_all x1 -> x2, starting transfers between devices: 19.6 us -> 23.1 us  [spread(): return lax.all_to_all(array, axes, split_axis=0, concat_axis=0, tiled=True)]
    all_to_all x1 -> x2, waiting for transfers between devices: 9.86 us -> 12 us  [spread(): return lax.all_to_all(array, axes, split_axis=0, concat_axis=0, tiled=True)]
  transfers between devices with their start and end apart: 9 -> 10, of which waited for: 4 -> 4; matrix products, arithmetic and copies ran while one was open for 1% -> 1% of each run, Pallas kernels for 13% -> 13%
where the time goes in v4:
time: 162 us; the launch traced here: 161 us
  blocking collectives  49.5 us (31%)
  starting transfers between devices  47.6 us (29%)
  Pallas kernels  29.4 us (18%)
  waiting for transfers between devices  27.6 us (17%)
  local copies, waits for them, and re-layouts  4.88 us (3%)
    all_to_all x2, blocking collectives, spread(): return lax.all_to_all(array, axes, split_axis=0, concat_axis=0, tiled=True)  49.5 us
    ppermute x8, starting transfers between devices, swapped(): return lax.ppermute(array, BLK, [(i, i ^ stride) for i in range(PARTS)])  24.5 us
    all_to_all x2, starting transfers between devices, spread(): return lax.all_to_all(array, axes, split_axis=0, concat_axis=0, tiled=True)  23.1 us
    pallas_call x4, Pallas kernels, sub_epoch_call(): pl.pallas_call(functools.partial(sub_epoch_kernel, 4.0 / rows, level, las...  19.4 us
    ppermute x8, waiting for transfers between devices, swapped(): return lax.ppermute(array, BLK, [(i, i ^ stride) for i in range(PARTS)])  15.6 us
    all_to_all x2, waiting for transfers between devices, spread(): return lax.all_to_all(array, axes, split_axis=0, concat_axis=0, tiled=True)  12 us
    unnamed x8, local copies, waits for them, and re-layouts  4.82 us
  transfers between devices with their start and end apart: 10, of which 4 were waited for; matrix products, arithmetic and copies ran while one was open for 1% of the time, Pallas kernels for 13%

profile of v4, /device:TPU:1, one launch (start us, length us, event | category | flops | bytes accessed | tf_op | source)
XLA Modules:
  0.0 160.9 jit_solution(15995490222123806152)
XLA Ops:
  0.6 1.6 shard_map.69
  2.2 19.6 %all-to-all-start = ((bf16[64,8,128]{2,1,0:T(8,128)(2,1)}), bf16[64,8,128]{2,1,0:T(8,128)(2,1)S(1)}, u32[]{:S(2)}, u32[]{:S(2)}) async-start(bf16[64,8,128]{2,1,0:T(8,128)(2,1)} %bitcast.12), calls=%async_computation | async-start | bytes 262144 | tf_op jit(solution)/shard_map/all_to_all | solution.py:341
  21.9 0.7 pad_add_fusion.here_ref
  22.5 3.1 %shard_map.68.table_ref = s32[560]{0:T(1024)} custom-call(s32[2]{0:T(128)} %pad_add_fusion.here_ref, s32[3,64]{1,0:T(4,128)} %matching_ref.1, s32[1,512]{1,0:T(1,128)} %mask_ref.1), custom_call_target="tpu_custom_call" | custom-call | flops 2000000 | bytes 4096 | tf_op jit(solution)/shard_map/pallas_call | solution.py:96
  25.6 9.8 %all-to-all-done.pieces_ref = bf16[64,8,128]{2,1,0:T(8,128)(2,1)S(1)} async-done(((bf16[64,8,128]{2,1,0:T(8,128)(2,1)}), bf16[64,8,128]{2,1,0:T(8,128)(2,1)S(1)}, u32[]{:S(2)}, u32[]{:S(2)}) %all-to-all-start) | async-done | bytes 131104 | tf_op jit(solution)/shard_map/all_to_all | solution.py:341
  35.5 0.0 copy-start.2
  35.5 0.7 copy-done.2
  36.1 1.2 shard_map.70
  37.4 33.5 %all_to_all.20.got_ref = bf16[64,9,8,128]{3,2,1,0:T(8,128)(2,1)S(1)} all-to-all(bf16[64,9,8,128]{3,2,1,0:T(8,128)(2,1)S(1)} %shard_map.70), channel_id=1, replica_groups=mesh['yh'=2,'x'=4,'z'=8,'yl'=4,'core'=2] {'yh','yl','z'}, dimensions={0} | all-to-all | bytes 2359296 | tf_op jit(solution)/shard_map/all_to_all | solution.py:341
  70.9 1.0 shard_map.71
  71.9 16.0 %all_to_all.21 = bf16[8,32,8,128]{3,2,1,0:T(8,128)(2,1)S(1)} all-to-all(bf16[8,32,8,128]{3,2,1,0:T(8,128)(2,1)S(1)} %get-tuple-element.15), channel_id=1, replica_groups=mesh['yh'=2,'x'=4,'z'=8,'yl'=4,'core'=2] {'x','core'}, dimensions={0} | all-to-all | bytes 1048576 | tf_op jit(solution)/shard_map/all_to_all | solution.py:341
  87.9 2.9 %collective-permute-start = (bf16[8,256,128]{2,1,0:T(8,128)(2,1)S(1)}, bf16[8,256,128]{2,1,0:T(8,128)(2,1)S(1)}, u32[]{:S(2)}, u32[]{:S(2)}) collective-permute-start(bf16[8,256,128]{2,1,0:T(8,128)(2,1)S(1)} %bitcast.6), channel_id=1, source_target_pairs={{0,1},{1,0},{2,3},{3,2},{4,5},{5,4},{6,7},{7,6},{8,9},{9,8},{10,11... | collective-permute-start | bytes 1572872 | tf_op jit(solution)/shard_map/ppermute | solution.py:337
  90.9 0.0 copy-start.3
  90.9 3.5 %all-to-all-start.2 = ((bf16[8,34,8,128]{3,2,1,0:T(8,128)(2,1)}), bf16[8,34,8,128]{3,2,1,0:T(8,128)(2,1)S(1)}, u32[]{:S(2)}, u32[]{:S(2)}) async-start(bf16[8,34,8,128]{3,2,1,0:T(8,128)(2,1)} %get-tuple-element.14), calls=%async_computation.2 | async-start | bytes 1114112 | tf_op jit(solution)/shard_map/all_to_all | solution.py:341
  94.4 0.0 collective-permute-done.xr_ref
  94.4 0.1 broadcast_select_fusion.xl_ref
  94.5 4.8 %collective-permute-start.1 = (bf16[4,256,128]{2,1,0:T(8,128)(2,1)S(1)}, bf16[4,256,128]{2,1,0:T(8,128)(2,1)S(1)}, u32[]{:S(2)}, u32[]{:S(2)}) collective-permute-start(bf16[4,256,128]{2,1,0:T(8,128)(2,1)S(1)} %constant_dynamic-slice_fusion.1), channel_id=1, source_target_pairs={{0,4},{1,5},{2,6},{3,7},{4,0},{5,1},{6,2},{7,3},{8,12},{9,13},{10,... | collective-permute-start | bytes 786440 | tf_op jit(solution)/shard_map/ppermute | solution.py:337
  99.3 0.8 shard_map.72.sim_ref
  100.1 0.0 copy-start
  100.1 1.9 %copy-done = f32[8,8,128,128]{3,2,1,0:T(8,128)} copy-done((f32[8,8,128,128]{3,2,1,0:T(8,128)}, f32[8,8,128,128]{3,2,1,0:T(8,128)S(1)}, u32[]{:S(2)}) %copy-start) | copy-done | bytes 4194328
  102.0 2.2 %all-to-all-done.2 = bf16[8,34,8,128]{3,2,1,0:T(8,128)(2,1)S(1)} async-done(((bf16[8,34,8,128]{3,2,1,0:T(8,128)(2,1)}), bf16[8,34,8,128]{3,2,1,0:T(8,128)(2,1)S(1)}, u32[]{:S(2)}, u32[]{:S(2)}) %all-to-all-start.2) | async-done | bytes 557088 | tf_op jit(solution)/shard_map/all_to_all | solution.py:341
  104.2 0.0 copy-done.3
  104.2 0.0 copy-start.1
  104.2 2.2 %copy-done.1 = f32[8,8,128,128]{3,2,1,0:T(8,128)S(1)} copy-done((f32[8,8,128,128]{3,2,1,0:T(8,128)S(1)}, f32[8,8,128,128]{3,2,1,0:T(8,128)}, u32[]{:S(2)}) %copy-start.1) | copy-done | bytes 4194328
  106.4 4.8 %shard_map.73 = (f32[8,128,128]{2,1,0:T(8,128)S(1)}, bf16[8,128,128]{2,1,0:T(8,128)(2,1)S(1)}) custom-call(s32[560]{0:T(1024)S(1)} %copy-done.3, bf16[8,16,128]{2,1,0:T(8,128)(2,1)S(1)} %slice.4.mask_ref, f32[8,8,128,128]{3,2,1,0:T(8,128)S(1)} %copy-done.1, bf16[8,272,128]{2,1,0:T(8,128)(2,1)S(1)} %bitcast.11), custom_call_target="tpu_custom_call" | custom-call | flops 805306368 | bytes 6291456 | tf_op jit(solution)/shard_map/pallas_call | solution.py:316
  111.2 2.8 %collective-permute-start.3 = (bf16[8,128,128]{2,1,0:T(8,128)(2,1)S(1)}, bf16[8,128,128]{2,1,0:T(8,128)(2,1)S(1)}, u32[]{:S(2)}, u32[]{:S(2)}) collective-permute-start(bf16[8,128,128]{2,1,0:T(8,128)(2,1)S(1)} %get-tuple-element.19), channel_id=1, source_target_pairs={{0,1},{1,0},{2,3},{3,2},{4,5},{5,4},{6,7},{7,6},{8,9},{9,8},{10,11... | collective-permute-start | bytes 786440 | tf_op jit(solution)/shard_map/ppermute | solution.py:337
  114.0 0.0 collective-permute-done.1
  114.0 1.9 %collective-permute-start.2 = (bf16[4,256,128]{2,1,0:T(8,128)(2,1)S(1)}, bf16[4,256,128]{2,1,0:T(8,128)(2,1)S(1)}, u32[]{:S(2)}, u32[]{:S(2)}) collective-permute-start(bf16[4,256,128]{2,1,0:T(8,128)(2,1)S(1)} %collective-permute-done.1), channel_id=1, source_target_pairs={{0,1},{1,0},{2,3},{3,2},{4,5},{5,4},{6,7},{7,6},{8,9},{9,8},{10,11... | collective-permute-start | bytes 786440 | tf_op jit(solution)/shard_map/ppermute | solution.py:337
  116.0 0.8 shard_map.75.sim_ref
  116.8 0.0 collective-permute-done.3.refs_1_
  116.8 4.8 %shard_map.76 = (f32[8,128,128]{2,1,0:T(8,128)S(1)}, bf16[8,128,128]{2,1,0:T(8,128)(2,1)S(1)}) custom-call(s32[560]{0:T(1024)S(1)} %copy-done.3, bf16[8,16,128]{2,1,0:T(8,128)(2,1)S(1)} %slice.4.mask_ref, f32[8,8,128,128]{3,2,1,0:T(8,128)S(1)} %shard_map.75.sim_ref, f32[8,128,128]{2,1,0:T(8,128)S(1)} %get-tuple-element.18.refs_0_, ...), custom_call_target="tpu_custom_call" | custom-call | flops 805306368 | bytes 6291456 | tf_op jit(solution)/shard_map/pallas_call | solution.py:316
  121.6 4.8 %collective-permute-start.4 = (bf16[8,128,128]{2,1,0:T(8,128)(2,1)S(1)}, bf16[8,128,128]{2,1,0:T(8,128)(2,1)S(1)}, u32[]{:S(2)}, u32[]{:S(2)}) collective-permute-start(bf16[8,128,128]{2,1,0:T(8,128)(2,1)S(1)} %get-tuple-element.21), channel_id=1, source_target_pairs={{0,4},{1,5},{2,6},{3,7},{4,0},{5,1},{6,2},{7,3},{8,12},{9,13},{10,... | collective-permute-start | bytes 786440 | tf_op jit(solution)/shard_map/ppermute | solution.py:337
  126.4 0.0 collective-permute-done.2
  126.4 0.1 broadcast_select_fusion.1
  126.6 2.5 %collective-permute-start.5 = (bf16[4,256,128]{2,1,0:T(8,128)(2,1)S(1)}, bf16[4,256,128]{2,1,0:T(8,128)(2,1)S(1)}, u32[]{:S(2)}, u32[]{:S(2)}) collective-permute-start(bf16[4,256,128]{2,1,0:T(8,128)(2,1)S(1)} %constant_dynamic-slice_fusion), channel_id=1, source_target_pairs={{0,2},{1,3},{2,0},{3,1},{4,6},{5,7},{6,4},{7,5},{8,10},{9,11},{10,... | collective-permute-start | bytes 786440 | tf_op jit(solution)/shard_map/ppermute | solution.py:337
  129.1 0.8 shard_map.74.sim_ref
  129.8 8.7 %collective-permute-done.4.refs_1_ = bf16[8,128,128]{2,1,0:T(8,128)(2,1)S(1)} collective-permute-done((bf16[8,128,128]{2,1,0:T(8,128)(2,1)S(1)}, bf16[8,128,128]{2,1,0:T(8,128)(2,1)S(1)}, u32[]{:S(2)}, u32[]{:S(2)}) %collective-permute-start.4) | collective-permute-done | bytes 262176 | tf_op jit(solution)/shard_map/ppermute | solution.py:337
  138.6 4.8 %shard_map.77 = (f32[8,128,128]{2,1,0:T(8,128)S(1)}, bf16[8,128,128]{2,1,0:T(8,128)(2,1)S(1)}) custom-call(s32[560]{0:T(1024)S(1)} %copy-done.3, bf16[8,16,128]{2,1,0:T(8,128)(2,1)S(1)} %slice.4.mask_ref, f32[8,8,128,128]{3,2,1,0:T(8,128)S(1)} %shard_map.74.sim_ref, f32[8,128,128]{2,1,0:T(8,128)S(1)} %get-tuple-element.20.refs_0_, ...), custom_call_target="tpu_custom_call" | custom-call | flops 805306368 | bytes 6291456 | tf_op jit(solution)/shard_map/pallas_call | solution.py:316
  143.4 0.0 collective-permute-done.5
  143.4 2.7 %collective-permute-start.6 = (bf16[4,256,128]{2,1,0:T(8,128)(2,1)S(1)}, bf16[4,256,128]{2,1,0:T(8,128)(2,1)S(1)}, u32[]{:S(2)}, u32[]{:S(2)}) collective-permute-start(bf16[4,256,128]{2,1,0:T(8,128)(2,1)S(1)} %collective-permute-done.5), channel_id=1, source_target_pairs={{0,1},{1,0},{2,3},{3,2},{4,5},{5,4},{6,7},{7,6},{8,9},{9,8},{10,11... | collective-permute-start | bytes 786440 | tf_op jit(solution)/shard_map/ppermute | solution.py:337
  146.1 2.1 %collective-permute-start.7 = (bf16[8,128,128]{2,1,0:T(8,128)(2,1)S(1)}, bf16[8,128,128]{2,1,0:T(8,128)(2,1)S(1)}, u32[]{:S(2)}, u32[]{:S(2)}) collective-permute-start(bf16[8,128,128]{2,1,0:T(8,128)(2,1)S(1)} %get-tuple-element.25), channel_id=1, source_target_pairs={{0,2},{1,3},{2,0},{3,1},{4,6},{5,7},{6,4},{7,5},{8,10},{9,11},{10,... | collective-permute-start | bytes 786440 | tf_op jit(solution)/shard_map/ppermute | solution.py:337
  148.2 0.0 collective-permute-done.6
  148.3 0.1 maximum_select_fusion.1.xr_ref
  148.4 0.8 shard_map.78.sim_ref
  149.1 6.8 %collective-permute-done.7.refs_1_ = bf16[8,128,128]{2,1,0:T(8,128)(2,1)S(1)} collective-permute-done((bf16[8,128,128]{2,1,0:T(8,128)(2,1)S(1)}, bf16[8,128,128]{2,1,0:T(8,128)(2,1)S(1)}, u32[]{:S(2)}, u32[]{:S(2)}) %collective-permute-start.7) | collective-permute-done | bytes 262176 | tf_op jit(solution)/shard_map/ppermute | solution.py:337
  156.0 4.9 %shard_map.79 = (f32[128,128]{1,0:T(8,128)}, f32[128,128]{1,0:T(8,128)}) custom-call(s32[560]{0:T(1024)S(1)} %copy-done.3, bf16[8,16,128]{2,1,0:T(8,128)(2,1)S(1)} %slice.4.mask_ref, f32[8,8,128,128]{3,2,1,0:T(8,128)S(1)} %shard_map.78.sim_ref, f32[8,128,128]{2,1,0:T(8,128)S(1)} %get-tuple-element.24.refs_0_, ...), custom_call_target="tpu_custom_call" | custom-call | flops 805306368 | bytes 6291456 | tf_op jit(solution)/shard_map/pallas_call | solution.py:316
  (3 shorter events, 0.1 us)
Async XLA Ops:
  2.2 33.2 %all-to-all-start = ((bf16[64,8,128]{2,1,0:T(8,128)(2,1)}), bf16[64,8,128]{2,1,0:T(8,128)(2,1)S(1)}, u32[]{:S(2)}, u32[]{:S(2)}) async-start(bf16[64,8,128]{2,1,0:T(8,128)(2,1)} %bitcast.12), calls=%async_computation | async-start | bytes 262144 | tf_op jit(solution)/shard_map/all_to_all | solution.py:341
  35.5 0.7 copy-start.2
  87.9 6.5 %collective-permute-start = (bf16[8,256,128]{2,1,0:T(8,128)(2,1)S(1)}, bf16[8,256,128]{2,1,0:T(8,128)(2,1)S(1)}, u32[]{:S(2)}, u32[]{:S(2)}) collective-permute-start(bf16[8,256,128]{2,1,0:T(8,128)(2,1)S(1)} %bitcast.6), channel_id=1, source_target_pairs={{0,1},{1,0},{2,3},{3,2},{4,5},{5,4},{6,7},{7,6},{8,9},{9,8},{10,11... | collective-permute-start | bytes 1572872 | tf_op jit(solution)/shard_map/ppermute | solution.py:337
  90.9 13.3 %copy-start.3 = (s32[560]{0:T(1024)S(1)}, s32[560]{0:T(1024)}, u32[]{:S(2)}) copy-start(s32[560]{0:T(1024)} %shard_map.68.table_ref) | copy-start | bytes 6724
  90.9 13.3 %all-to-all-start.2 = ((bf16[8,34,8,128]{3,2,1,0:T(8,128)(2,1)}), bf16[8,34,8,128]{3,2,1,0:T(8,128)(2,1)S(1)}, u32[]{:S(2)}, u32[]{:S(2)}) async-start(bf16[8,34,8,128]{3,2,1,0:T(8,128)(2,1)} %get-tuple-element.14), calls=%async_computation.2 | async-start | bytes 1114112 | tf_op jit(solution)/shard_map/all_to_all | solution.py:341
  94.5 19.5 %collective-permute-start.1 = (bf16[4,256,128]{2,1,0:T(8,128)(2,1)S(1)}, bf16[4,256,128]{2,1,0:T(8,128)(2,1)S(1)}, u32[]{:S(2)}, u32[]{:S(2)}) collective-permute-start(bf16[4,256,128]{2,1,0:T(8,128)(2,1)S(1)} %constant_dynamic-slice_fusion.1), channel_id=1, source_target_pairs={{0,4},{1,5},{2,6},{3,7},{4,0},{5,1},{6,2},{7,3},{8,12},{9,13},{10,... | collective-permute-start | bytes 786440 | tf_op jit(solution)/shard_map/ppermute | solution.py:337
  100.1 2.0 %copy-start = (f32[8,8,128,128]{3,2,1,0:T(8,128)}, f32[8,8,128,128]{3,2,1,0:T(8,128)S(1)}, u32[]{:S(2)}) copy-start(f32[8,8,128,128]{3,2,1,0:T(8,128)S(1)} %shard_map.72.sim_ref) | copy-start | bytes 12582916
  104.2 2.2 %copy-start.1 = (f32[8,8,128,128]{3,2,1,0:T(8,128)S(1)}, f32[8,8,128,128]{3,2,1,0:T(8,128)}, u32[]{:S(2)}) copy-start(f32[8,8,128,128]{3,2,1,0:T(8,128)} %copy-done) | copy-start | bytes 12582916
  111.2 5.5 %collective-permute-start.3 = (bf16[8,128,128]{2,1,0:T(8,128)(2,1)S(1)}, bf16[8,128,128]{2,1,0:T(8,128)(2,1)S(1)}, u32[]{:S(2)}, u32[]{:S(2)}) collective-permute-start(bf16[8,128,128]{2,1,0:T(8,128)(2,1)S(1)} %get-tuple-element.19), channel_id=1, source_target_pairs={{0,1},{1,0},{2,3},{3,2},{4,5},{5,4},{6,7},{7,6},{8,9},{9,8},{10,11... | collective-permute-start | bytes 786440 | tf_op jit(solution)/shard_map/ppermute | solution.py:337
  114.0 12.4 %collective-permute-start.2 = (bf16[4,256,128]{2,1,0:T(8,128)(2,1)S(1)}, bf16[4,256,128]{2,1,0:T(8,128)(2,1)S(1)}, u32[]{:S(2)}, u32[]{:S(2)}) collective-permute-start(bf16[4,256,128]{2,1,0:T(8,128)(2,1)S(1)} %collective-permute-done.1), channel_id=1, source_target_pairs={{0,1},{1,0},{2,3},{3,2},{4,5},{5,4},{6,7},{7,6},{8,9},{9,8},{10,11... | collective-permute-start | bytes 786440 | tf_op jit(solution)/shard_map/ppermute | solution.py:337
  121.6 17.0 %collective-permute-start.4 = (bf16[8,128,128]{2,1,0:T(8,128)(2,1)S(1)}, bf16[8,128,128]{2,1,0:T(8,128)(2,1)S(1)}, u32[]{:S(2)}, u32[]{:S(2)}) collective-permute-start(bf16[8,128,128]{2,1,0:T(8,128)(2,1)S(1)} %get-tuple-element.21), channel_id=1, source_target_pairs={{0,4},{1,5},{2,6},{3,7},{4,0},{5,1},{6,2},{7,3},{8,12},{9,13},{10,... | collective-permute-start | bytes 786440 | tf_op jit(solution)/shard_map/ppermute | solution.py:337
  126.6 16.8 %collective-permute-start.5 = (bf16[4,256,128]{2,1,0:T(8,128)(2,1)S(1)}, bf16[4,256,128]{2,1,0:T(8,128)(2,1)S(1)}, u32[]{:S(2)}, u32[]{:S(2)}) collective-permute-start(bf16[4,256,128]{2,1,0:T(8,128)(2,1)S(1)} %constant_dynamic-slice_fusion), channel_id=1, source_target_pairs={{0,2},{1,3},{2,0},{3,1},{4,6},{5,7},{6,4},{7,5},{8,10},{9,11},{10,... | collective-permute-start | bytes 786440 | tf_op jit(solution)/shard_map/ppermute | solution.py:337
  143.4 4.8 %collective-permute-start.6 = (bf16[4,256,128]{2,1,0:T(8,128)(2,1)S(1)}, bf16[4,256,128]{2,1,0:T(8,128)(2,1)S(1)}, u32[]{:S(2)}, u32[]{:S(2)}) collective-permute-start(bf16[4,256,128]{2,1,0:T(8,128)(2,1)S(1)} %collective-permute-done.5), channel_id=1, source_target_pairs={{0,1},{1,0},{2,3},{3,2},{4,5},{5,4},{6,7},{7,6},{8,9},{9,8},{10,11... | collective-permute-start | bytes 786440 | tf_op jit(solution)/shard_map/ppermute | solution.py:337
  146.1 9.8 %collective-permute-start.7 = (bf16[8,128,128]{2,1,0:T(8,128)(2,1)S(1)}, bf16[8,128,128]{2,1,0:T(8,128)(2,1)S(1)}, u32[]{:S(2)}, u32[]{:S(2)}) collective-permute-start(bf16[8,128,128]{2,1,0:T(8,128)(2,1)S(1)} %get-tuple-element.25), channel_id=1, source_target_pairs={{0,2},{1,3},{2,0},{3,1},{4,6},{5,7},{6,4},{7,5},{8,10},{9,11},{10,... | collective-permute-start | bytes 786440 | tf_op jit(solution)/shard_map/ppermute | solution.py:337

commit v5 on v4

--- a/solution.py
+++ b/solution.py
@@ -132,27 +132,23 @@
     )(table, pieces)
 
 
-def regroup_kernel(got_ref, x_ref, uv_ref):
-    half = YL * ZS
+def regroup_kernel(got_ref, out_ref):
+    far = YH * YL * ZS
     for near in range(XS * CORES):
-        x_ref[near] = got_ref[:half, near]
-        uv_ref[near, :half] = got_ref[half:, near]
+        out_ref[near, :far] = got_ref[:, near]
     for yh in range(YH):
-        total = jnp.sum(got_ref[yh * half : (yh + 1) * half, XS * CORES].astype(F32), axis=0).astype(BF)
+        span = far // YH
+        total = jnp.sum(got_ref[yh * span : (yh + 1) * span, XS * CORES].astype(F32), axis=0).astype(BF)
         for near in range(XS * CORES):
-            uv_ref[near, half + yh] = total
+            out_ref[near, far + yh] = total
 
 
 def regroup_call(got):
-    half = YL * ZS
     return pl.pallas_call(
         regroup_kernel,
-        out_shape=(
-            jax.ShapeDtypeStruct((XS * CORES, half, PIECE, LANES), BF),
-            jax.ShapeDtypeStruct((XS * CORES, half + YH, PIECE, LANES), BF),
-        ),
+        out_shape=jax.ShapeDtypeStruct((XS * CORES, YH * YL * ZS + YH, PIECE, LANES), BF),
         in_specs=[VMEM],
-        out_specs=(VMEM, VMEM),
+        out_specs=VMEM,
         compiler_params=pltpu.CompilerParams(vmem_limit_bytes=16 << 20),
         cost_estimate=pl.CostEstimate(flops=1000000, bytes_accessed=2 << 20, transcendentals=0),
     )(got)
@@ -218,13 +214,13 @@
     lanes = lax.broadcasted_iota(jnp.int32, values.shape, 1)
     for c in range(blocks):
         mine = jnp.where(lanes == lane + level * PARTS + c, values, 0.0)
-        ks[c] = jnp.broadcast_to(jnp.sum(mine, axis=1, keepdims=True), values.shape)
+        ks[c] = jnp.broadcast_to(step_size * jnp.sum(mine, axis=1, keepdims=True), values.shape)
 
     span = rows // 2
     for b in range(blocks):
         if level == 0:
             yl, core = b // CORES, b % CORES
-            moved = pl.ds(yl * span, span)
+            moved = pl.ds((YL + yl) * span, span)
             for i in range(2):
                 put = pl.ds(i * span, span)
                 left = all_ref[i * CORES + core, moved]
@@ -253,11 +249,11 @@
             for b, resid in zip(spots, resids)
         ]
         for b, grad in zip(spots, grads_l):
-            new_left = ls[b] - step_size * grad
+            new_left = ls[b] - grad
             ls[b] = new_left
             lb[b] = new_left.astype(BF)
         for b, grad in zip(spots, grads_r):
-            new_right = rs[b] - step_size * grad
+            new_right = rs[b] - grad
             after = (b + 1) % blocks if isinstance(b, int) else lax.rem(b + 1, blocks)
             rs_next[after] = new_right
             rb_next[after] = new_right.astype(BF)
@@ -351,10 +347,9 @@
     pieces = spread(pack_call(features, factor_u, factor_v).reshape(GROUPS, PIECE, rank), GRP)
     table = tables_call(jnp.stack([group, part]), matching, tile_mask)
     got = spread(pick_call(table, pieces), FAR)
-    x0, uv = regroup_call(got)
-    x0 = spread(x0, NEAR).reshape(XS * CORES, -1, rank)
-    uv = spread(uv, NEAR).reshape(XS * CORES, -1, rank)
-    mask = uv[:, x0.shape[1] :]
+    got = spread(regroup_call(got), NEAR).reshape(XS * CORES, -1, rank)
+    half = YL * slot_rows // 2
+    x0, mask = got[:, :half], got[:, 2 * half :]
 
     def work(level, sims, *arrays):
         return sub_epoch_call(level, slot_rows, table, mask, sims, *arrays)
@@ -366,20 +361,22 @@
     def half_of(x):
         return lax.dynamic_slice_in_dim(x, core * (XS * CORES // 2), XS * CORES // 2, 0)
 
+    away, next_bit = STRIDES[1], [b // STRIDES[1] % 2 for b in range(PARTS)]
+    first = lax.ppermute(x0, BLK, [(b, b ^ away) for b in range(PARTS) if b % CORES == next_bit[b]])
     y0 = swapped(x0, STRIDES[0])
-    sims = sim_call(slot_rows, x0, x0)
+    sims = sim_call(slot_rows, got, got)
     x1 = jnp.where(bits[1] == bits[0], x0, y0)
-    first = swapped(half_of(x1), STRIDES[1])
-    sims_next = sim_call(slot_rows, x0, y0)
-    kept, sent = work(0, sims, uv)
+    kept, sent = work(0, sims, got)
     right = swapped(sent, STRIDES[0])
-    kept, first = lax.optimization_barrier((kept, first))
-    y1 = joined(first)
+    sims = sim_call(slot_rows, x0, y0)
+    right, first = lax.optimization_barrier((right, first))
+    second = lax.ppermute(first, BLK, [(b, b ^ STRIDES[0]) for b in range(PARTS) if b % CORES != next_bit[b]])
+    kept, sent = work(1, sims, kept, right)
+    right = swapped(sent, STRIDES[1])
+    y1 = jnp.where(bits[0] == bits[1], second, first)
+    sims = sim_call(slot_rows, x1, y1)
     x2 = jnp.where(bits[2] == bits[1], x1, y1)
     first = swapped(half_of(x2), STRIDES[2])
-    kept, sent = work(1, sims_next, kept, right)
-    right = swapped(sent, STRIDES[1])
-    sims = sim_call(slot_rows, x1, y1)
     kept, sent = work(2, sims, kept, right)
     right = swapped(sent, STRIDES[2])
     kept, first = lax.optimization_barrier((kept, first))

time: 162 us -> 155 us (0.957)
  blocking collectives: 49.5 us -> 56 us
  starting transfers between devices: 47.6 us -> 41.7 us
  local copies, waits for them, and re-layouts: 4.88 us -> 0.76 us
  waiting for transfers between devices: 27.6 us -> 25.5 us
    all_to_all x2, blocking collectives: 49.5 us -> 56 us  [spread(): return lax.all_to_all(array, axes, split_axis=0, concat_axis=0, tiled=True)]
    ppermute x8 -> x6, starting transfers between devices: 24.5 us -> 18.7 us  [swapped(): return lax.ppermute(array, BLK, [(i, i ^ stride) for i in range(PARTS)])]
    unnamed x8 -> x4, local copies, waits for them, and re-layouts: 4.82 us -> 0.69 us
    all_to_all x2 -> x1, starting transfers between devices: 23.1 us -> 19.6 us  [spread(): return lax.all_to_all(array, axes, split_axis=0, concat_axis=0, tiled=True)]
    ppermute x0 -> x2, starting transfers between devices: none -> 3.37 us  [the longest x1 2.08 us: local(): lax.ppermute(first, BLK, [(b, b ^ STRIDES[0]) for b in range(PARTS) if b...]
    all_to_all x2 -> x1, waiting for transfers between devices: 12 us -> 9.86 us  [spread(): return lax.all_to_all(array, axes, split_axis=0, concat_axis=0, tiled=True)]
    ppermute x8 -> x6, waiting for transfers between devices: 15.6 us -> 14.4 us  [swapped(): return lax.ppermute(array, BLK, [(i, i ^ stride) for i in range(PARTS)])]
  transfers between devices with their start and end apart: 10 -> 9, of which waited for: 4 -> 4; matrix products, arithmetic and copies ran while one was open for 1% -> 1% of each run, Pallas kernels for 13% -> 13%
where the time goes in v5:
time: 155 us
  blocking collectives  56 us (36%)
  starting transfers between devices  41.7 us (27%)
  Pallas kernels  28.7 us (19%)
  waiting for transfers between devices  25.5 us (16%)
    all_to_all x2, blocking collectives, spread(): return lax.all_to_all(array, axes, split_axis=0, concat_axis=0, tiled=True)  56 us
    all_to_all x1, starting transfers between devices, spread(): return lax.all_to_all(array, axes, split_axis=0, concat_axis=0, tiled=True)  19.6 us
    pallas_call x4, Pallas kernels, sub_epoch_call(): pl.pallas_call(functools.partial(sub_epoch_kernel, 4.0 / rows, level, las...  19.5 us
    ppermute x6, starting transfers between devices, swapped(): return lax.ppermute(array, BLK, [(i, i ^ stride) for i in range(PARTS)])  18.7 us
    ppermute x6, waiting for transfers between devices, swapped(): return lax.ppermute(array, BLK, [(i, i ^ stride) for i in range(PARTS)])  14.4 us
    all_to_all x1, waiting for transfers between devices, spread(): return lax.all_to_all(array, axes, split_axis=0, concat_axis=0, tiled=True)  9.86 us
    pallas_call x4, Pallas kernels, sim_call(): pl.pallas_call(sim_kernel, out_shape=jax.ShapeDtypeStruct((PARTS, PARTS,...  3.11 us
  transfers between devices with their start and end apart: 9, of which 4 were waited for; matrix products, arithmetic and copies ran while one was open for 1% of the time, Pallas kernels for 13%

profile of v5, /device:TPU:1, one launch (start us, length us, event | category | flops | bytes accessed | tf_op | source)
XLA Modules:
  0.0 154.5 jit_solution(6260567985666722704)
XLA Ops:
  0.6 1.6 %shard_map.69 = bf16[512,128]{1,0:T(8,128)(2,1)} custom-call(f32[128,256]{1,0:T(8,128)} %x_ref.1, f32[128,128]{1,0:T(8,128)} %u_ref.1, f32[128,128]{1,0:T(8,128)} %v_ref.1), custom_call_target="tpu_custom_call" | custom-call | flops 100000 | bytes 400000 | tf_op jit(solution)/shard_map/pallas_call | solution.py:39
  2.2 19.6 %all-to-all-start = ((bf16[64,8,128]{2,1,0:T(8,128)(2,1)}), bf16[64,8,128]{2,1,0:T(8,128)(2,1)S(1)}, u32[]{:S(2)}, u32[]{:S(2)}) async-start(bf16[64,8,128]{2,1,0:T(8,128)(2,1)} %bitcast.10), calls=%async_computation | async-start | bytes 262144 | tf_op jit(solution)/shard_map/all_to_all | solution.py:337
  21.9 0.7 pad_add_fusion.here_ref
  22.5 3.1 %shard_map.68.table_ref = s32[560]{0:T(1024)} custom-call(s32[2]{0:T(128)} %pad_add_fusion.here_ref, s32[3,64]{1,0:T(4,128)} %matching_ref.1, s32[1,512]{1,0:T(1,128)} %mask_ref.1), custom_call_target="tpu_custom_call" | custom-call | flops 2000000 | bytes 4096 | tf_op jit(solution)/shard_map/pallas_call | solution.py:96
  25.6 9.9 %all-to-all-done.pieces_ref = bf16[64,8,128]{2,1,0:T(8,128)(2,1)S(1)} async-done(((bf16[64,8,128]{2,1,0:T(8,128)(2,1)}), bf16[64,8,128]{2,1,0:T(8,128)(2,1)S(1)}, u32[]{:S(2)}, u32[]{:S(2)}) %all-to-all-start) | async-done | bytes 131104 | tf_op jit(solution)/shard_map/all_to_all | solution.py:337
  35.5 0.0 copy-start
  35.5 0.7 copy-done
  36.2 1.2 shard_map.70
  37.4 33.5 %all_to_all.15.got_ref = bf16[64,9,8,128]{3,2,1,0:T(8,128)(2,1)S(1)} all-to-all(bf16[64,9,8,128]{3,2,1,0:T(8,128)(2,1)S(1)} %shard_map.70), channel_id=1, replica_groups=mesh['yh'=2,'x'=4,'z'=8,'yl'=4,'core'=2] {'yh','yl','z'}, dimensions={0} | all-to-all | bytes 2359296 | tf_op jit(solution)/shard_map/all_to_all | solution.py:337
  70.9 0.2 shard_map.71
  71.1 22.5 %all_to_all.16 = bf16[8,66,8,128]{3,2,1,0:T(8,128)(2,1)S(1)} all-to-all(bf16[8,66,8,128]{3,2,1,0:T(8,128)(2,1)S(1)} %shard_map.71), channel_id=1, replica_groups=mesh['yh'=2,'x'=4,'z'=8,'yl'=4,'core'=2] {'x','core'}, dimensions={0} | all-to-all | bytes 2162688 | tf_op jit(solution)/shard_map/all_to_all | solution.py:337
  93.7 1.3 collective-permute-start.2
  95.0 0.0 copy-start.1
  95.0 0.8 shard_map.72.sim_ref
  95.8 0.0 copy-done.1
  95.8 4.9 %shard_map.73 = (f32[8,128,128]{2,1,0:T(8,128)S(1)}, bf16[8,128,128]{2,1,0:T(8,128)(2,1)S(1)}) custom-call(s32[560]{0:T(1024)S(1)} %copy-done.1, bf16[8,16,128]{2,1,0:T(8,128)(2,1)S(1)} %slice.8.mask_ref, f32[8,8,128,128]{3,2,1,0:T(8,128)S(1)} %shard_map.72.sim_ref, bf16[8,528,128]{2,1,0:T(8,128)(2,1)S(1)} %bitcast.8), custom_call_target="tpu_custom_call" | custom-call | flops 805306368 | bytes 6291456 | tf_op jit(solution)/shard_map/pallas_call | solution.py:312
  100.7 6.3 %collective-permute-start.1 = (bf16[8,128,128]{2,1,0:T(8,128)(2,1)S(1)}, bf16[8,128,128]{2,1,0:T(8,128)(2,1)S(1)}, u32[]{:S(2)}, u32[]{:S(2)}) collective-permute-start(bf16[8,128,128]{2,1,0:T(8,128)(2,1)S(1)} %get-tuple-element.12), channel_id=1, source_target_pairs={{0,1},{1,0},{2,3},{3,2},{4,5},{5,4},{6,7},{7,6},{8,9},{9,8},{10,11... | collective-permute-start | bytes 786440 | tf_op jit(solution)/shard_map/ppermute | solution.py:333
  106.9 1.9 %collective-permute-start = (bf16[8,256,128]{2,1,0:T(8,128)(2,1)S(1)}, bf16[8,256,128]{2,1,0:T(8,128)(2,1)S(1)}, u32[]{:S(2)}, u32[]{:S(2)}) collective-permute-start(bf16[8,256,128]{2,1,0:T(8,128)(2,1)S(1)} %slice.9.xl_ref), channel_id=1, source_target_pairs={{0,1},{1,0},{2,3},{3,2},{4,5},{5,4},{6,7},{7,6},{8,9},{9,8},{10,11... | collective-permute-start | bytes 1572872 | tf_op jit(solution)/shard_map/ppermute | solution.py:333
  108.9 0.0 collective-permute-done.1.refs_1_
  108.9 1.2 collective-permute-done.2
  110.1 2.1 %collective-permute-start.3 = (bf16[8,256,128]{2,1,0:T(8,128)(2,1)S(1)}, bf16[8,256,128]{2,1,0:T(8,128)(2,1)}, u32[]{:S(2)}, u32[]{:S(2)}) collective-permute-start(bf16[8,256,128]{2,1,0:T(8,128)(2,1)S(1)} %collective-permute-done.2), channel_id=1, source_target_pairs={{1,0},{3,2},{4,5},{6,7},{9,8},{11,10},{12,13},{14,15},{17,16},{19,... | collective-permute-start | bytes 1572872 | tf_op jit(solution)/shard_map/ppermute | solution.py:373
  112.2 0.0 collective-permute-done.xr_ref
  112.2 0.8 shard_map.75.sim_ref
  113.0 4.8 %shard_map.76 = (f32[8,128,128]{2,1,0:T(8,128)S(1)}, bf16[8,128,128]{2,1,0:T(8,128)(2,1)S(1)}) custom-call(s32[560]{0:T(1024)S(1)} %copy-done.1, bf16[8,16,128]{2,1,0:T(8,128)(2,1)S(1)} %slice.8.mask_ref, f32[8,8,128,128]{3,2,1,0:T(8,128)S(1)} %shard_map.75.sim_ref, f32[8,128,128]{2,1,0:T(8,128)S(1)} %get-tuple-element.14.refs_0_, ...), custom_call_target="tpu_custom_call" | custom-call | flops 805306368 | bytes 6291456 | tf_op jit(solution)/shard_map/pallas_call | solution.py:312
  117.8 1.9 %collective-permute-start.4 = (bf16[8,128,128]{2,1,0:T(8,128)(2,1)S(1)}, bf16[8,128,128]{2,1,0:T(8,128)(2,1)S(1)}, u32[]{:S(2)}, u32[]{:S(2)}) collective-permute-start(bf16[8,128,128]{2,1,0:T(8,128)(2,1)S(1)} %get-tuple-element.17), channel_id=1, source_target_pairs={{0,4},{1,5},{2,6},{3,7},{4,0},{5,1},{6,2},{7,3},{8,12},{9,13},{10,... | collective-permute-start | bytes 786440 | tf_op jit(solution)/shard_map/ppermute | solution.py:333
  119.8 0.0 collective-permute-done.3
  119.8 0.2 broadcast_select_fusion.2
  120.0 4.6 %collective-permute-start.5 = (bf16[4,256,128]{2,1,0:T(8,128)(2,1)S(1)}, bf16[4,256,128]{2,1,0:T(8,128)(2,1)S(1)}, u32[]{:S(2)}, u32[]{:S(2)}) collective-permute-start(bf16[4,256,128]{2,1,0:T(8,128)(2,1)S(1)} %constant_dynamic-slice_fusion), channel_id=1, source_target_pairs={{0,2},{1,3},{2,0},{3,1},{4,6},{5,7},{6,4},{7,5},{8,10},{9,11},{10,... | collective-permute-start | bytes 786440 | tf_op jit(solution)/shard_map/ppermute | solution.py:333
  124.6 0.8 shard_map.74.sim_ref
  125.4 8.1 %collective-permute-done.4.refs_1_ = bf16[8,128,128]{2,1,0:T(8,128)(2,1)S(1)} collective-permute-done((bf16[8,128,128]{2,1,0:T(8,128)(2,1)S(1)}, bf16[8,128,128]{2,1,0:T(8,128)(2,1)S(1)}, u32[]{:S(2)}, u32[]{:S(2)}) %collective-permute-start.4) | collective-permute-done | bytes 262176 | tf_op jit(solution)/shard_map/ppermute | solution.py:333
  133.5 4.9 %shard_map.77 = (f32[8,128,128]{2,1,0:T(8,128)S(1)}, bf16[8,128,128]{2,1,0:T(8,128)(2,1)S(1)}) custom-call(s32[560]{0:T(1024)S(1)} %copy-done.1, bf16[8,16,128]{2,1,0:T(8,128)(2,1)S(1)} %slice.8.mask_ref, f32[8,8,128,128]{3,2,1,0:T(8,128)S(1)} %shard_map.74.sim_ref, f32[8,128,128]{2,1,0:T(8,128)S(1)} %get-tuple-element.16.refs_0_, ...), custom_call_target="tpu_custom_call" | custom-call | flops 805306368 | bytes 6291456 | tf_op jit(solution)/shard_map/pallas_call | solution.py:312
  138.4 0.0 collective-permute-done.5
  138.4 1.9 %collective-permute-start.6 = (bf16[4,256,128]{2,1,0:T(8,128)(2,1)S(1)}, bf16[4,256,128]{2,1,0:T(8,128)(2,1)S(1)}, u32[]{:S(2)}, u32[]{:S(2)}) collective-permute-start(bf16[4,256,128]{2,1,0:T(8,128)(2,1)S(1)} %collective-permute-done.5), channel_id=1, source_target_pairs={{0,1},{1,0},{2,3},{3,2},{4,5},{5,4},{6,7},{7,6},{8,9},{9,8},{10,11... | collective-permute-start | bytes 786440 | tf_op jit(solution)/shard_map/ppermute | solution.py:333
  140.3 2.1 %collective-permute-start.7 = (bf16[8,128,128]{2,1,0:T(8,128)(2,1)S(1)}, bf16[8,128,128]{2,1,0:T(8,128)(2,1)S(1)}, u32[]{:S(2)}, u32[]{:S(2)}) collective-permute-start(bf16[8,128,128]{2,1,0:T(8,128)(2,1)S(1)} %get-tuple-element.21), channel_id=1, source_target_pairs={{0,2},{1,3},{2,0},{3,1},{4,6},{5,7},{6,4},{7,5},{8,10},{9,11},{10,... | collective-permute-start | bytes 786440 | tf_op jit(solution)/shard_map/ppermute | solution.py:333
  142.4 0.0 collective-permute-done.6
  142.5 0.1 maximum_select_fusion.xr_ref
  142.5 0.8 shard_map.78.sim_ref
  143.3 6.3 %collective-permute-done.7.refs_1_ = bf16[8,128,128]{2,1,0:T(8,128)(2,1)S(1)} collective-permute-done((bf16[8,128,128]{2,1,0:T(8,128)(2,1)S(1)}, bf16[8,128,128]{2,1,0:T(8,128)(2,1)S(1)}, u32[]{:S(2)}, u32[]{:S(2)}) %collective-permute-start.7) | collective-permute-done | bytes 262176 | tf_op jit(solution)/shard_map/ppermute | solution.py:333
  149.6 4.9 %shard_map.79 = (f32[128,128]{1,0:T(8,128)}, f32[128,128]{1,0:T(8,128)}) custom-call(s32[560]{0:T(1024)S(1)} %copy-done.1, bf16[8,16,128]{2,1,0:T(8,128)(2,1)S(1)} %slice.8.mask_ref, f32[8,8,128,128]{3,2,1,0:T(8,128)S(1)} %shard_map.78.sim_ref, f32[8,128,128]{2,1,0:T(8,128)S(1)} %get-tuple-element.20.refs_0_, ...), custom_call_target="tpu_custom_call" | custom-call | flops 805306368 | bytes 6291456 | tf_op jit(solution)/shard_map/pallas_call | solution.py:312
  (3 shorter events, 0.1 us)
Async XLA Ops:
  2.2 33.2 %all-to-all-start = ((bf16[64,8,128]{2,1,0:T(8,128)(2,1)}), bf16[64,8,128]{2,1,0:T(8,128)(2,1)S(1)}, u32[]{:S(2)}, u32[]{:S(2)}) async-start(bf16[64,8,128]{2,1,0:T(8,128)(2,1)} %bitcast.10), calls=%async_computation | async-start | bytes 262144 | tf_op jit(solution)/shard_map/all_to_all | solution.py:337
  35.5 0.7 copy-start
  93.7 16.4 %collective-permute-start.2 = (bf16[8,256,128]{2,1,0:T(8,128)(2,1)S(1)}, bf16[8,256,128]{2,1,0:T(8,128)(2,1)S(1)}, u32[]{:S(2)}, u32[]{:S(2)}) collective-permute-start(bf16[8,256,128]{2,1,0:T(8,128)(2,1)S(1)} %slice.9.xl_ref), channel_id=1, source_target_pairs={{0,4},{2,6},{5,1},{7,3},{8,12},{10,14},{13,9},{15,11},{16,20},{18,... | collective-permute-start | bytes 1572872 | tf_op jit(solution)/shard_map/ppermute | solution.py:365
  95.0 0.8 copy-start.1
  100.7 8.2 %collective-permute-start.1 = (bf16[8,128,128]{2,1,0:T(8,128)(2,1)S(1)}, bf16[8,128,128]{2,1,0:T(8,128)(2,1)S(1)}, u32[]{:S(2)}, u32[]{:S(2)}) collective-permute-start(bf16[8,128,128]{2,1,0:T(8,128)(2,1)S(1)} %get-tuple-element.12), channel_id=1, source_target_pairs={{0,1},{1,0},{2,3},{3,2},{4,5},{5,4},{6,7},{7,6},{8,9},{9,8},{10,11... | collective-permute-start | bytes 786440 | tf_op jit(solution)/shard_map/ppermute | solution.py:333
  106.9 5.3 %collective-permute-start = (bf16[8,256,128]{2,1,0:T(8,128)(2,1)S(1)}, bf16[8,256,128]{2,1,0:T(8,128)(2,1)S(1)}, u32[]{:S(2)}, u32[]{:S(2)}) collective-permute-start(bf16[8,256,128]{2,1,0:T(8,128)(2,1)S(1)} %slice.9.xl_ref), channel_id=1, source_target_pairs={{0,1},{1,0},{2,3},{3,2},{4,5},{5,4},{6,7},{7,6},{8,9},{9,8},{10,11... | collective-permute-start | bytes 1572872 | tf_op jit(solution)/shard_map/ppermute | solution.py:333
  110.1 9.6 %collective-permute-start.3 = (bf16[8,256,128]{2,1,0:T(8,128)(2,1)S(1)}, bf16[8,256,128]{2,1,0:T(8,128)(2,1)}, u32[]{:S(2)}, u32[]{:S(2)}) collective-permute-start(bf16[8,256,128]{2,1,0:T(8,128)(2,1)S(1)} %collective-permute-done.2), channel_id=1, source_target_pairs={{1,0},{3,2},{4,5},{6,7},{9,8},{11,10},{12,13},{14,15},{17,16},{19,... | collective-permute-start | bytes 1572872 | tf_op jit(solution)/shard_map/ppermute | solution.py:373
  117.8 15.7 %collective-permute-start.4 = (bf16[8,128,128]{2,1,0:T(8,128)(2,1)S(1)}, bf16[8,128,128]{2,1,0:T(8,128)(2,1)S(1)}, u32[]{:S(2)}, u32[]{:S(2)}) collective-permute-start(bf16[8,128,128]{2,1,0:T(8,128)(2,1)S(1)} %get-tuple-element.17), channel_id=1, source_target_pairs={{0,4},{1,5},{2,6},{3,7},{4,0},{5,1},{6,2},{7,3},{8,12},{9,13},{10,... | collective-permute-start | bytes 786440 | tf_op jit(solution)/shard_map/ppermute | solution.py:333
  120.0 18.4 %collective-permute-start.5 = (bf16[4,256,128]{2,1,0:T(8,128)(2,1)S(1)}, bf16[4,256,128]{2,1,0:T(8,128)(2,1)S(1)}, u32[]{:S(2)}, u32[]{:S(2)}) collective-permute-start(bf16[4,256,128]{2,1,0:T(8,128)(2,1)S(1)} %constant_dynamic-slice_fusion), channel_id=1, source_target_pairs={{0,2},{1,3},{2,0},{3,1},{4,6},{5,7},{6,4},{7,5},{8,10},{9,11},{10,... | collective-permute-start | bytes 786440 | tf_op jit(solution)/shard_map/ppermute | solution.py:333
  138.4 4.0 %collective-permute-start.6 = (bf16[4,256,128]{2,1,0:T(8,128)(2,1)S(1)}, bf16[4,256,128]{2,1,0:T(8,128)(2,1)S(1)}, u32[]{:S(2)}, u32[]{:S(2)}) collective-permute-start(bf16[4,256,128]{2,1,0:T(8,128)(2,1)S(1)} %collective-permute-done.5), channel_id=1, source_target_pairs={{0,1},{1,0},{2,3},{3,2},{4,5},{5,4},{6,7},{7,6},{8,9},{9,8},{10,11... | collective-permute-start | bytes 786440 | tf_op jit(solution)/shard_map/ppermute | solution.py:333
  140.3 9.3 %collective-permute-start.7 = (bf16[8,128,128]{2,1,0:T(8,128)(2,1)S(1)}, bf16[8,128,128]{2,1,0:T(8,128)(2,1)S(1)}, u32[]{:S(2)}, u32[]{:S(2)}) collective-permute-start(bf16[8,128,128]{2,1,0:T(8,128)(2,1)S(1)} %get-tuple-element.21), channel_id=1, source_target_pairs={{0,2},{1,3},{2,0},{3,1},{4,6},{5,7},{6,4},{7,5},{8,10},{9,11},{10,... | collective-permute-start | bytes 786440 | tf_op jit(solution)/shard_map/ppermute | solution.py:333

commit v6 on v5

--- a/solution.py
+++ b/solution.py
@@ -221,31 +221,29 @@
         if level == 0:
             yl, core = b // CORES, b % CORES
             moved = pl.ds((YL + yl) * span, span)
-            for i in range(2):
-                put = pl.ds(i * span, span)
-                left = all_ref[i * CORES + core, moved]
-                right = all_ref[(2 + i) * CORES + core, moved]
-                ls[b, put], rs0[b, put] = left.astype(F32), right.astype(F32)
-                lb[b, put], rb0[b, put] = left, right
+            left = jnp.concatenate([all_ref[core, moved], all_ref[CORES + core, moved]]).astype(F32)
+            right = jnp.concatenate([all_ref[2 * CORES + core, moved], all_ref[3 * CORES + core, moved]])
         else:
             left, right = left_ref[place(b)], right_ref[place(b)]
-            ls[b], rs0[b] = left, right.astype(F32)
-            lb[b], rb0[b] = left.astype(BF), right
+        right = right.astype(F32).T
+        ls[b], rs0[b] = left, right
+        lb[b], rb0[b] = left.astype(BF), right.astype(BF)
 
     def cycle_step(step, source, target, spots):
         (rs, rb), (rs_next, rb_next) = source, target
-        preds = [
-            lax.dot_general(lb[b], rb[b], (((1,), (1,)), ((), ())), preferred_element_type=F32) for b in spots
-        ]
+        preds = [jnp.dot(lb[b], rb[b], preferred_element_type=F32) for b in spots]
         resids = []
         for b, pred in zip(spots, preds):
             left, right = place(b), place(lax.rem(b + blocks - step, blocks))
             row = jnp.where(flip == 1, right, left)
             col = jnp.where(flip == 1, left, right)
             resids.append((ks[col, pl.ds(row, 1)] * (pred - sim_ref[left, right])).astype(BF))
-        grads_l = [jnp.dot(resid, rb[b], preferred_element_type=F32) for b, resid in zip(spots, resids)]
+        grads_l = [
+            lax.dot_general(resid, rb[b], (((1,), (1,)), ((), ())), preferred_element_type=F32)
+            for b, resid in zip(spots, resids)
+        ]
         grads_r = [
-            lax.dot_general(resid, lb[b], (((0,), (0,)), ((), ())), preferred_element_type=F32)
+            lax.dot_general(lb[b], resid, (((0,), (0,)), ((), ())), preferred_element_type=F32)
             for b, resid in zip(spots, resids)
         ]
         for b, grad in zip(spots, grads_l):
@@ -279,11 +277,11 @@
         @pl.when(flip == 0)
         def _():
             uo_ref[...] = ls[place(part)]
-            vo_ref[...] = rs0[place(part)]
+            vo_ref[...] = rs0[place(part)].T
 
         @pl.when(flip == 1)
         def _():
-            uo_ref[...] = rs0[place(part)]
+            uo_ref[...] = rs0[place(part)].T
             vo_ref[...] = ls[place(part)]
     else:
         kept_ref, sent_ref = outs
@@ -298,8 +296,9 @@
         @pl.when(jnp.logical_not(same))
         def _():
             for b in range(blocks):
-                kept_ref[place(b)] = rs0[b]
-                sent_ref[place(b)] = rb0[b]
+                right = rs0[b].T
+                kept_ref[place(b)] = right
+                sent_ref[place(b)] = right.astype(BF)
 
 
 def sub_epoch_call(level, rows, table, mask, sims, *arrays):
@@ -340,7 +339,6 @@
 def local(features, factor_u, factor_v, tile_mask, matching):
     group = lax.axis_index(GRP).astype(jnp.int32)
     part = lax.axis_index(BLK).astype(jnp.int32)
-    core = lax.axis_index("core")
     slot_rows, rank = factor_u.shape
     bits = [part // stride % 2 for stride in STRIDES]
 
@@ -353,13 +351,6 @@
 
     def work(level, sims, *arrays):
         return sub_epoch_call(level, slot_rows, table, mask, sims, *arrays)
-
-    def joined(first):
-        second = swapped(first, STRIDES[0])
-        return jnp.where(core == 0, jnp.concatenate([first, second]), jnp.concatenate([second, first]))
-
-    def half_of(x):
-        return lax.dynamic_slice_in_dim(x, core * (XS * CORES // 2), XS * CORES // 2, 0)
 
     away, next_bit = STRIDES[1], [b // STRIDES[1] % 2 for b in range(PARTS)]
     first = lax.ppermute(x0, BLK, [(b, b ^ away) for b in range(PARTS) if b % CORES == next_bit[b]])
@@ -376,11 +367,11 @@
     y1 = jnp.where(bits[0] == bits[1], second, first)
     sims = sim_call(slot_rows, x1, y1)
     x2 = jnp.where(bits[2] == bits[1], x1, y1)
-    first = swapped(half_of(x2), STRIDES[2])
+    y2 = swapped(x2, STRIDES[2])
     kept, sent = work(2, sims, kept, right)
     right = swapped(sent, STRIDES[2])
-    kept, first = lax.optimization_barrier((kept, first))
-    return work(3, sim_call(slot_rows, x2, joined(first)), kept, right)
+    kept, y2 = lax.optimization_barrier((kept, y2))
+    return work(3, sim_call(slot_rows, x2, y2), kept, right)
 
 
 def solution(mesh):

time: 155 us -> 154 us (level)
  starting transfers between devices: 41.7 us -> 39.7 us
    ppermute x6 -> x5, starting transfers between devices: 18.7 us -> 16.7 us  [swapped(): return lax.ppermute(array, BLK, [(i, i ^ stride) for i in range(PARTS)])]
    ppermute x6 -> x5, waiting for transfers between devices: 14.4 us -> 15.2 us  [swapped(): return lax.ppermute(array, BLK, [(i, i ^ stride) for i in range(PARTS)])]
  transfers between devices with their start and end apart: 9 -> 8, of which waited for: 4 -> 4; matrix products, arithmetic and copies ran while one was open for 1% -> 1% of each run, Pallas kernels for 13% -> 14%
where the time goes in v6:
time: 154 us; the launch traced here: 153 us
  blocking collectives  56 us (36%)
  starting transfers between devices  39.7 us (26%)
  Pallas kernels  29 us (19%)
  waiting for transfers between devices  26.3 us (17%)
    all_to_all x2, blocking collectives, spread(): return lax.all_to_all(array, axes, split_axis=0, concat_axis=0, tiled=True)  56 us
    pallas_call x4, Pallas kernels, sub_epoch_call(): pl.pallas_call(functools.partial(sub_epoch_kernel, 4.0 / rows, level, las...  19.8 us
    all_to_all x1, starting transfers between devices, spread(): return lax.all_to_all(array, axes, split_axis=0, concat_axis=0, tiled=True)  19.6 us
    ppermute x5, starting transfers between devices, swapped(): return lax.ppermute(array, BLK, [(i, i ^ stride) for i in range(PARTS)])  16.7 us
    ppermute x5, waiting for transfers between devices, swapped(): return lax.ppermute(array, BLK, [(i, i ^ stride) for i in range(PARTS)])  15.2 us
    all_to_all x1, waiting for transfers between devices, spread(): return lax.all_to_all(array, axes, split_axis=0, concat_axis=0, tiled=True)  9.89 us
    pallas_call x4, Pallas kernels, sim_call(): pl.pallas_call(sim_kernel, out_shape=jax.ShapeDtypeStruct((PARTS, PARTS,...  3.12 us
  transfers between devices with their start and end apart: 8, of which 4 were waited for; matrix products, arithmetic and copies ran while one was open for 1% of the time, Pallas kernels for 14%

profile of v6, /device:TPU:1, one launch (start us, length us, event | category | flops | bytes accessed | tf_op | source)
XLA Modules:
  0.0 153.3 jit_solution(2501622052271189110)
XLA Ops:
  0.6 1.6 %shard_map.69 = bf16[512,128]{1,0:T(8,128)(2,1)} custom-call(f32[128,256]{1,0:T(8,128)} %x_ref.1, f32[128,128]{1,0:T(8,128)} %u_ref.1, f32[128,128]{1,0:T(8,128)} %v_ref.1), custom_call_target="tpu_custom_call" | custom-call | flops 100000 | bytes 400000 | tf_op jit(solution)/shard_map/pallas_call | solution.py:39
  2.2 19.6 %all-to-all-start = ((bf16[64,8,128]{2,1,0:T(8,128)(2,1)}), bf16[64,8,128]{2,1,0:T(8,128)(2,1)S(1)}, u32[]{:S(2)}, u32[]{:S(2)}) async-start(bf16[64,8,128]{2,1,0:T(8,128)(2,1)} %bitcast.10), calls=%async_computation | async-start | bytes 262144 | tf_op jit(solution)/shard_map/all_to_all | solution.py:336
  21.9 0.6 pad_add_fusion.here_ref
  22.5 3.1 %shard_map.68.table_ref = s32[560]{0:T(1024)} custom-call(s32[2]{0:T(128)} %pad_add_fusion.here_ref, s32[3,64]{1,0:T(4,128)} %matching_ref.1, s32[1,512]{1,0:T(1,128)} %mask_ref.1), custom_call_target="tpu_custom_call" | custom-call | flops 2000000 | bytes 4096 | tf_op jit(solution)/shard_map/pallas_call | solution.py:96
  25.6 9.9 %all-to-all-done.pieces_ref = bf16[64,8,128]{2,1,0:T(8,128)(2,1)S(1)} async-done(((bf16[64,8,128]{2,1,0:T(8,128)(2,1)}), bf16[64,8,128]{2,1,0:T(8,128)(2,1)S(1)}, u32[]{:S(2)}, u32[]{:S(2)}) %all-to-all-start) | async-done | bytes 131104 | tf_op jit(solution)/shard_map/all_to_all | solution.py:336
  35.5 0.0 copy-start
  35.5 0.7 copy-done
  36.1 1.2 shard_map.70
  37.4 33.5 %all_to_all.15.got_ref = bf16[64,9,8,128]{3,2,1,0:T(8,128)(2,1)S(1)} all-to-all(bf16[64,9,8,128]{3,2,1,0:T(8,128)(2,1)S(1)} %shard_map.70), channel_id=1, replica_groups=mesh['yh'=2,'x'=4,'z'=8,'yl'=4,'core'=2] {'yh','yl','z'}, dimensions={0} | all-to-all | bytes 2359296 | tf_op jit(solution)/shard_map/all_to_all | solution.py:336
  70.9 0.2 shard_map.71
  71.1 22.5 %all_to_all.16 = bf16[8,66,8,128]{3,2,1,0:T(8,128)(2,1)S(1)} all-to-all(bf16[8,66,8,128]{3,2,1,0:T(8,128)(2,1)S(1)} %shard_map.71), channel_id=1, replica_groups=mesh['yh'=2,'x'=4,'z'=8,'yl'=4,'core'=2] {'x','core'}, dimensions={0} | all-to-all | bytes 2162688 | tf_op jit(solution)/shard_map/all_to_all | solution.py:336
  93.7 1.3 collective-permute-start.2
  95.0 0.0 copy-start.1
  95.0 0.8 shard_map.72.sim_ref
  95.8 0.0 copy-done.1
  95.8 5.0 %shard_map.73 = (f32[8,128,128]{2,1,0:T(8,128)S(1)}, bf16[8,128,128]{2,1,0:T(8,128)(2,1)S(1)}) custom-call(s32[560]{0:T(1024)S(1)} %copy-done.1, bf16[8,16,128]{2,1,0:T(8,128)(2,1)S(1)} %slice.8.mask_ref, f32[8,8,128,128]{3,2,1,0:T(8,128)S(1)} %shard_map.72.sim_ref, bf16[8,528,128]{2,1,0:T(8,128)(2,1)S(1)} %bitcast.8), custom_call_target="tpu_custom_call" | custom-call | flops 805306368 | bytes 6291456 | tf_op jit(solution)/shard_map/pallas_call | solution.py:311
  100.8 6.1 %collective-permute-start.1 = (bf16[8,128,128]{2,1,0:T(8,128)(2,1)S(1)}, bf16[8,128,128]{2,1,0:T(8,128)(2,1)S(1)}, u32[]{:S(2)}, u32[]{:S(2)}) collective-permute-start(bf16[8,128,128]{2,1,0:T(8,128)(2,1)S(1)} %get-tuple-element.12), channel_id=1, source_target_pairs={{0,1},{1,0},{2,3},{3,2},{4,5},{5,4},{6,7},{7,6},{8,9},{9,8},{10,11... | collective-permute-start | bytes 786440 | tf_op jit(solution)/shard_map/ppermute | solution.py:332
  107.0 1.9 %collective-permute-start = (bf16[8,256,128]{2,1,0:T(8,128)(2,1)S(1)}, bf16[8,256,128]{2,1,0:T(8,128)(2,1)S(1)}, u32[]{:S(2)}, u32[]{:S(2)}) collective-permute-start(bf16[8,256,128]{2,1,0:T(8,128)(2,1)S(1)} %slice.9.xl_ref), channel_id=1, source_target_pairs={{0,1},{1,0},{2,3},{3,2},{4,5},{5,4},{6,7},{7,6},{8,9},{9,8},{10,11... | collective-permute-start | bytes 1572872 | tf_op jit(solution)/shard_map/ppermute | solution.py:332
  108.9 0.0 collective-permute-done.1.refs_1_
  108.9 1.2 collective-permute-done.2
  110.1 2.1 %collective-permute-start.3 = (bf16[8,256,128]{2,1,0:T(8,128)(2,1)S(1)}, bf16[8,256,128]{2,1,0:T(8,128)(2,1)}, u32[]{:S(2)}, u32[]{:S(2)}) collective-permute-start(bf16[8,256,128]{2,1,0:T(8,128)(2,1)S(1)} %collective-permute-done.2), channel_id=1, source_target_pairs={{1,0},{3,2},{4,5},{6,7},{9,8},{11,10},{12,13},{14,15},{17,16},{19,... | collective-permute-start | bytes 1572872 | tf_op jit(solution)/shard_map/ppermute | solution.py:364
  112.2 0.0 collective-permute-done.xr_ref
  112.2 0.8 shard_map.75.sim_ref
  113.0 5.0 %shard_map.76 = (f32[8,128,128]{2,1,0:T(8,128)S(1)}, bf16[8,128,128]{2,1,0:T(8,128)(2,1)S(1)}) custom-call(s32[560]{0:T(1024)S(1)} %copy-done.1, bf16[8,16,128]{2,1,0:T(8,128)(2,1)S(1)} %slice.8.mask_ref, f32[8,8,128,128]{3,2,1,0:T(8,128)S(1)} %shard_map.75.sim_ref, f32[8,128,128]{2,1,0:T(8,128)S(1)} %get-tuple-element.14.refs_0_, ...), custom_call_target="tpu_custom_call" | custom-call | flops 805306368 | bytes 6291456 | tf_op jit(solution)/shard_map/pallas_call | solution.py:311
  118.0 1.9 %collective-permute-start.4 = (bf16[8,128,128]{2,1,0:T(8,128)(2,1)S(1)}, bf16[8,128,128]{2,1,0:T(8,128)(2,1)S(1)}, u32[]{:S(2)}, u32[]{:S(2)}) collective-permute-start(bf16[8,128,128]{2,1,0:T(8,128)(2,1)S(1)} %get-tuple-element.17), channel_id=1, source_target_pairs={{0,4},{1,5},{2,6},{3,7},{4,0},{5,1},{6,2},{7,3},{8,12},{9,13},{10,... | collective-permute-start | bytes 786440 | tf_op jit(solution)/shard_map/ppermute | solution.py:332
  119.9 0.0 collective-permute-done.3
  119.9 0.2 broadcast_select_fusion.2
  120.1 4.6 %collective-permute-start.5 = (bf16[8,256,128]{2,1,0:T(8,128)(2,1)S(1)}, bf16[8,256,128]{2,1,0:T(8,128)(2,1)S(1)}, u32[]{:S(2)}, u32[]{:S(2)}) collective-permute-start(bf16[8,256,128]{2,1,0:T(8,128)(2,1)S(1)} %get-tuple-element.22.xl_ref), channel_id=1, source_target_pairs={{0,2},{1,3},{2,0},{3,1},{4,6},{5,7},{6,4},{7,5},{8,10},{9,11},{10,... | collective-permute-start | bytes 1572872 | tf_op jit(solution)/shard_map/ppermute | solution.py:332
  124.7 0.8 shard_map.74.sim_ref
  125.5 8.1 %collective-permute-done.4.refs_1_ = bf16[8,128,128]{2,1,0:T(8,128)(2,1)S(1)} collective-permute-done((bf16[8,128,128]{2,1,0:T(8,128)(2,1)S(1)}, bf16[8,128,128]{2,1,0:T(8,128)(2,1)S(1)}, u32[]{:S(2)}, u32[]{:S(2)}) %collective-permute-start.4) | collective-permute-done | bytes 262176 | tf_op jit(solution)/shard_map/ppermute | solution.py:332
  133.6 4.8 %shard_map.77 = (f32[8,128,128]{2,1,0:T(8,128)S(1)}, bf16[8,128,128]{2,1,0:T(8,128)(2,1)S(1)}) custom-call(s32[560]{0:T(1024)S(1)} %copy-done.1, bf16[8,16,128]{2,1,0:T(8,128)(2,1)S(1)} %slice.8.mask_ref, f32[8,8,128,128]{3,2,1,0:T(8,128)S(1)} %shard_map.74.sim_ref, f32[8,128,128]{2,1,0:T(8,128)S(1)} %get-tuple-element.16.refs_0_, ...), custom_call_target="tpu_custom_call" | custom-call | flops 805306368 | bytes 6291456 | tf_op jit(solution)/shard_map/pallas_call | solution.py:311
  138.4 2.1 %collective-permute-start.6 = (bf16[8,128,128]{2,1,0:T(8,128)(2,1)S(1)}, bf16[8,128,128]{2,1,0:T(8,128)(2,1)S(1)}, u32[]{:S(2)}, u32[]{:S(2)}) collective-permute-start(bf16[8,128,128]{2,1,0:T(8,128)(2,1)S(1)} %get-tuple-element.21), channel_id=1, source_target_pairs={{0,2},{1,3},{2,0},{3,1},{4,6},{5,7},{6,4},{7,5},{8,10},{9,11},{10,... | collective-permute-start | bytes 786440 | tf_op jit(solution)/shard_map/ppermute | solution.py:332
  140.5 0.0 collective-permute-done.5.xr_ref
  140.5 0.8 shard_map.78.sim_ref
  141.3 7.1 %collective-permute-done.6.refs_1_ = bf16[8,128,128]{2,1,0:T(8,128)(2,1)S(1)} collective-permute-done((bf16[8,128,128]{2,1,0:T(8,128)(2,1)S(1)}, bf16[8,128,128]{2,1,0:T(8,128)(2,1)S(1)}, u32[]{:S(2)}, u32[]{:S(2)}) %collective-permute-start.6) | collective-permute-done | bytes 262176 | tf_op jit(solution)/shard_map/ppermute | solution.py:332
  148.4 4.9 %shard_map.79 = (f32[128,128]{1,0:T(8,128)}, f32[128,128]{1,0:T(8,128)}) custom-call(s32[560]{0:T(1024)S(1)} %copy-done.1, bf16[8,16,128]{2,1,0:T(8,128)(2,1)S(1)} %slice.8.mask_ref, f32[8,8,128,128]{3,2,1,0:T(8,128)S(1)} %shard_map.78.sim_ref, f32[8,128,128]{2,1,0:T(8,128)S(1)} %get-tuple-element.20.refs_0_, ...), custom_call_target="tpu_custom_call" | custom-call | flops 805306368 | bytes 6291456 | tf_op jit(solution)/shard_map/pallas_call | solution.py:311
  (2 shorter events, 0.0 us)
Async XLA Ops:
  2.2 33.2 %all-to-all-start = ((bf16[64,8,128]{2,1,0:T(8,128)(2,1)}), bf16[64,8,128]{2,1,0:T(8,128)(2,1)S(1)}, u32[]{:S(2)}, u32[]{:S(2)}) async-start(bf16[64,8,128]{2,1,0:T(8,128)(2,1)} %bitcast.10), calls=%async_computation | async-start | bytes 262144 | tf_op jit(solution)/shard_map/all_to_all | solution.py:336
  35.5 0.7 copy-start
  93.7 16.4 %collective-permute-start.2 = (bf16[8,256,128]{2,1,0:T(8,128)(2,1)S(1)}, bf16[8,256,128]{2,1,0:T(8,128)(2,1)S(1)}, u32[]{:S(2)}, u32[]{:S(2)}) collective-permute-start(bf16[8,256,128]{2,1,0:T(8,128)(2,1)S(1)} %slice.9.xl_ref), channel_id=1, source_target_pairs={{0,4},{2,6},{5,1},{7,3},{8,12},{10,14},{13,9},{15,11},{16,20},{18,... | collective-permute-start | bytes 1572872 | tf_op jit(solution)/shard_map/ppermute | solution.py:356
  95.0 0.8 copy-start.1
  100.8 8.1 %collective-permute-start.1 = (bf16[8,128,128]{2,1,0:T(8,128)(2,1)S(1)}, bf16[8,128,128]{2,1,0:T(8,128)(2,1)S(1)}, u32[]{:S(2)}, u32[]{:S(2)}) collective-permute-start(bf16[8,128,128]{2,1,0:T(8,128)(2,1)S(1)} %get-tuple-element.12), channel_id=1, source_target_pairs={{0,1},{1,0},{2,3},{3,2},{4,5},{5,4},{6,7},{7,6},{8,9},{9,8},{10,11... | collective-permute-start | bytes 786440 | tf_op jit(solution)/shard_map/ppermute | solution.py:332
  107.0 5.2 %collective-permute-start = (bf16[8,256,128]{2,1,0:T(8,128)(2,1)S(1)}, bf16[8,256,128]{2,1,0:T(8,128)(2,1)S(1)}, u32[]{:S(2)}, u32[]{:S(2)}) collective-permute-start(bf16[8,256,128]{2,1,0:T(8,128)(2,1)S(1)} %slice.9.xl_ref), channel_id=1, source_target_pairs={{0,1},{1,0},{2,3},{3,2},{4,5},{5,4},{6,7},{7,6},{8,9},{9,8},{10,11... | collective-permute-start | bytes 1572872 | tf_op jit(solution)/shard_map/ppermute | solution.py:332
  110.1 9.8 %collective-permute-start.3 = (bf16[8,256,128]{2,1,0:T(8,128)(2,1)S(1)}, bf16[8,256,128]{2,1,0:T(8,128)(2,1)}, u32[]{:S(2)}, u32[]{:S(2)}) collective-permute-start(bf16[8,256,128]{2,1,0:T(8,128)(2,1)S(1)} %collective-permute-done.2), channel_id=1, source_target_pairs={{1,0},{3,2},{4,5},{6,7},{9,8},{11,10},{12,13},{14,15},{17,16},{19,... | collective-permute-start | bytes 1572872 | tf_op jit(solution)/shard_map/ppermute | solution.py:364
  118.0 15.6 %collective-permute-start.4 = (bf16[8,128,128]{2,1,0:T(8,128)(2,1)S(1)}, bf16[8,128,128]{2,1,0:T(8,128)(2,1)S(1)}, u32[]{:S(2)}, u32[]{:S(2)}) collective-permute-start(bf16[8,128,128]{2,1,0:T(8,128)(2,1)S(1)} %get-tuple-element.17), channel_id=1, source_target_pairs={{0,4},{1,5},{2,6},{3,7},{4,0},{5,1},{6,2},{7,3},{8,12},{9,13},{10,... | collective-permute-start | bytes 786440 | tf_op jit(solution)/shard_map/ppermute | solution.py:332
  120.1 20.4 %collective-permute-start.5 = (bf16[8,256,128]{2,1,0:T(8,128)(2,1)S(1)}, bf16[8,256,128]{2,1,0:T(8,128)(2,1)S(1)}, u32[]{:S(2)}, u32[]{:S(2)}) collective-permute-start(bf16[8,256,128]{2,1,0:T(8,128)(2,1)S(1)} %get-tuple-element.22.xl_ref), channel_id=1, source_target_pairs={{0,2},{1,3},{2,0},{3,1},{4,6},{5,7},{6,4},{7,5},{8,10},{9,11},{10,... | collective-permute-start | bytes 1572872 | tf_op jit(solution)/shard_map/ppermute | solution.py:332
  138.4 10.0 %collective-permute-start.6 = (bf16[8,128,128]{2,1,0:T(8,128)(2,1)S(1)}, bf16[8,128,128]{2,1,0:T(8,128)(2,1)S(1)}, u32[]{:S(2)}, u32[]{:S(2)}) collective-permute-start(bf16[8,128,128]{2,1,0:T(8,128)(2,1)S(1)} %get-tuple-element.21), channel_id=1, source_target_pairs={{0,2},{1,3},{2,0},{3,1},{4,6},{5,7},{6,4},{7,5},{8,10},{9,11},{10,... | collective-permute-start | bytes 786440 | tf_op jit(solution)/shard_map/ppermute | solution.py:332

commit v7 on v6

--- a/solution.py
+++ b/solution.py
@@ -154,9 +154,20 @@
     )(got)
 
 
-def sim_kernel(xl_ref, xr_ref, out_ref, lx, rx):
+def sim_kernel(level, table_ref, mask_ref, xl_ref, xr_ref, out_ref, ks, lx, rx, mf, kr):
     blocks, _, rows, _ = out_ref.shape
-    rank, span = LANES, rows // 2
+    rank, span, step_size = LANES, rows // 2, 4.0 / rows
+    node = table_ref[INFO + SUB + level]
+    mf[...] = mask_ref[...].astype(F32)
+    for b in range(blocks):
+        row, lane = mask_place(node, b)
+        kr[pl.ds(b, 1)] = mf[node // ZS % XS * CORES + b % CORES, pl.ds(row, 1)]
+    values = kr[...]
+    lanes = lax.broadcasted_iota(jnp.int32, values.shape, 1)
+    for c in range(blocks):
+        mine = jnp.where(lanes == lane + level * PARTS + c, values, 0.0)
+        ks[c] = jnp.broadcast_to(step_size * jnp.sum(mine, axis=1, keepdims=True), values.shape)
+
     for b in range(blocks):
         yl, core = b // CORES, b % CORES
         taken = pl.ds(yl * span, span)
@@ -178,43 +189,36 @@
                     out_ref[b + i, r + j] = sims[i * rows : (i + 1) * rows, j * rows : (j + 1) * rows]
 
 
-def sim_call(rows, left_x, right_x):
+def sim_call(level, rows, table, mask, left_x, right_x):
     operand = pltpu.VMEM((PARTS * rows, 2 * LANES), BF)
     return pl.pallas_call(
-        sim_kernel,
-        out_shape=jax.ShapeDtypeStruct((PARTS, PARTS, rows, rows), F32),
-        in_specs=[VMEM, VMEM],
-        out_specs=VMEM,
-        scratch_shapes=[operand, operand],
+        functools.partial(sim_kernel, level),
+        out_shape=(
+            jax.ShapeDtypeStruct((PARTS, PARTS, rows, rows), F32),
+            jax.ShapeDtypeStruct((PARTS, PARTS, LANES), F32),
+        ),
+        in_specs=[SMEM, VMEM, VMEM, VMEM],
+        out_specs=(VMEM, VMEM),
+        scratch_shapes=[operand, operand, pltpu.VMEM(mask.shape, F32), pltpu.VMEM((PARTS, LANES), F32)],
         compiler_params=pltpu.CompilerParams(vmem_limit_bytes=24 << 20),
         cost_estimate=pl.CostEstimate(
             flops=4 * PARTS * PARTS * rows * rows * LANES, bytes_accessed=4 << 20, transcendentals=0
         ),
-    )(left_x, right_x)
-
-
-def sub_epoch_kernel(step_size, level, last, table_ref, mask_ref, sim_ref, *refs):
+    )(table, mask, left_x, right_x)
+
+
+def sub_epoch_kernel(level, last, table_ref, ks, sim_ref, *refs):
     if level == 0:
         all_ref, *refs = refs
     else:
         left_ref, right_ref, *refs = refs
-    *outs, ls, lb, rs0, rb0, rs1, rb1, mf, kr, ks = refs
+    *outs, ls, lb, rs0, rb0, rs1, rb1 = refs
     blocks, rows, rank = ls.shape
-    part, node = table_ref[INFO], table_ref[INFO + SUB + level]
+    part = table_ref[INFO]
     flip = jnp.int32(0) if level == 0 else table_ref[INFO + level]
 
     def place(slot):
         return slot if level == 0 else jnp.where(flip == 1, blocks - 1 - slot, slot)
-
-    mf[...] = mask_ref[...].astype(F32)
-    for b in range(blocks):
-        row, lane = mask_place(node, b)
-        kr[pl.ds(b, 1)] = mf[node // ZS % XS * CORES + b % CORES, pl.ds(row, 1)]
-    values = kr[...]
-    lanes = lax.broadcasted_iota(jnp.int32, values.shape, 1)
-    for c in range(blocks):
-        mine = jnp.where(lanes == lane + level * PARTS + c, values, 0.0)
-        ks[c] = jnp.broadcast_to(step_size * jnp.sum(mine, axis=1, keepdims=True), values.shape)
 
     span = rows // 2
     for b in range(blocks):
@@ -301,7 +305,7 @@
                 sent_ref[place(b)] = right.astype(BF)
 
 
-def sub_epoch_call(level, rows, table, mask, sims, *arrays):
+def sub_epoch_call(level, rows, table, keeps, sims, *arrays):
     rank, last = LANES, level + 1 == SUB
     whole = (PARTS, rows, rank)
     if last:
@@ -309,23 +313,18 @@
     else:
         outs = (jax.ShapeDtypeStruct(whole, F32), jax.ShapeDtypeStruct(whole, BF))
     return pl.pallas_call(
-        functools.partial(sub_epoch_kernel, 4.0 / rows, level, last),
+        functools.partial(sub_epoch_kernel, level, last),
         out_shape=outs,
         in_specs=[SMEM] + [VMEM] * (2 + len(arrays)),
         out_specs=(VMEM, VMEM),
-        scratch_shapes=[pltpu.VMEM(whole, F32), pltpu.VMEM(whole, BF)] * 3
-        + [
-            pltpu.VMEM(mask.shape, F32),
-            pltpu.VMEM((PARTS, LANES), F32),
-            pltpu.VMEM((PARTS, PARTS, LANES), F32),
-        ],
+        scratch_shapes=[pltpu.VMEM(whole, F32), pltpu.VMEM(whole, BF)] * 3,
         compiler_params=pltpu.CompilerParams(vmem_limit_bytes=28 << 20),
         cost_estimate=pl.CostEstimate(
             flops=2 * PARTS * PARTS * rows * rows * 3 * rank,
             bytes_accessed=6 << 20,
             transcendentals=0,
         ),
-    )(table, mask, sims, *arrays)
+    )(table, keeps, sims, *arrays)
 
 
 def swapped(array, stride):
@@ -350,28 +349,28 @@
     x0, mask = got[:, :half], got[:, 2 * half :]
 
     def work(level, sims, *arrays):
-        return sub_epoch_call(level, slot_rows, table, mask, sims, *arrays)
+        return sub_epoch_call(level, slot_rows, table, sims[1], sims[0], *arrays)
 
     away, next_bit = STRIDES[1], [b // STRIDES[1] % 2 for b in range(PARTS)]
     first = lax.ppermute(x0, BLK, [(b, b ^ away) for b in range(PARTS) if b % CORES == next_bit[b]])
     y0 = swapped(x0, STRIDES[0])
-    sims = sim_call(slot_rows, got, got)
+    sims = sim_call(0, slot_rows, table, mask, got, got)
     x1 = jnp.where(bits[1] == bits[0], x0, y0)
     kept, sent = work(0, sims, got)
     right = swapped(sent, STRIDES[0])
-    sims = sim_call(slot_rows, x0, y0)
+    sims = sim_call(1, slot_rows, table, mask, x0, y0)
     right, first = lax.optimization_barrier((right, first))
     second = lax.ppermute(first, BLK, [(b, b ^ STRIDES[0]) for b in range(PARTS) if b % CORES != next_bit[b]])
     kept, sent = work(1, sims, kept, right)
     right = swapped(sent, STRIDES[1])
     y1 = jnp.where(bits[0] == bits[1], second, first)
-    sims = sim_call(slot_rows, x1, y1)
+    sims = sim_call(2, slot_rows, table, mask, x1, y1)
     x2 = jnp.where(bits[2] == bits[1], x1, y1)
     y2 = swapped(x2, STRIDES[2])
     kept, sent = work(2, sims, kept, right)
     right = swapped(sent, STRIDES[2])
     kept, y2 = lax.optimization_barrier((kept, y2))
-    return work(3, sim_call(slot_rows, x2, y2), kept, right)
+    return work(3, sim_call(3, slot_rows, table, mask, x2, y2), kept, right)
 
 
 def solution(mesh):

time: 154 us -> 155 us (level)
  Pallas kernels: 29 us -> 31.1 us
    pallas_call x8, Pallas kernels: 22.9 us -> 25 us  [the longest x4 19.6 us: sub_epoch_call(): pl.pallas_call(functools.partial(sub_epoch_kernel, level, last), out_shap...]
  transfers between devices with their start and end apart: 8 -> 8, of which waited for: 4 -> 4; matrix products, arithmetic and copies ran while one was open for 1% -> 1% of each run, Pallas kernels for 14% -> 15%
where the time goes in v7:
time: 155 us; the launch traced here: 154 us
  blocking collectives  56 us (36%)
  starting transfers between devices  39.7 us (26%)
  Pallas kernels  31.1 us (20%)
  waiting for transfers between devices  25.1 us (16%)
    all_to_all x2, blocking collectives, spread(): return lax.all_to_all(array, axes, split_axis=0, concat_axis=0, tiled=True)  56 us
    pallas_call x4, Pallas kernels, sub_epoch_call(): pl.pallas_call(functools.partial(sub_epoch_kernel, level, last), out_shap...  19.6 us
    all_to_all x1, starting transfers between devices, spread(): return lax.all_to_all(array, axes, split_axis=0, concat_axis=0, tiled=True)  19.6 us
    ppermute x5, starting transfers between devices, swapped(): return lax.ppermute(array, BLK, [(i, i ^ stride) for i in range(PARTS)])  16.3 us
    ppermute x5, waiting for transfers between devices, swapped(): return lax.ppermute(array, BLK, [(i, i ^ stride) for i in range(PARTS)])  14.5 us
    all_to_all x1, waiting for transfers between devices, spread(): return lax.all_to_all(array, axes, split_axis=0, concat_axis=0, tiled=True)  9.93 us
    pallas_call x4, Pallas kernels, sim_call(): pl.pallas_call(functools.partial(sim_kernel, level), out_shape=(jax.Shape...  5.4 us
  transfers between devices with their start and end apart: 8, of which 4 were waited for; matrix products, arithmetic and copies ran while one was open for 1% of the time, Pallas kernels for 15%

profile of v7, /device:TPU:1, one launch (start us, length us, event | category | flops | bytes accessed | tf_op | source)
XLA Modules:
  0.0 154.3 jit_solution(11080316175015159673)
XLA Ops:
  0.6 1.6 %shard_map.69 = bf16[512,128]{1,0:T(8,128)(2,1)} custom-call(f32[128,256]{1,0:T(8,128)} %x_ref.1, f32[128,128]{1,0:T(8,128)} %u_ref.1, f32[128,128]{1,0:T(8,128)} %v_ref.1), custom_call_target="tpu_custom_call" | custom-call | flops 100000 | bytes 400000 | tf_op jit(solution)/shard_map/pallas_call | solution.py:39
  2.3 19.6 %all-to-all-start = ((bf16[64,8,128]{2,1,0:T(8,128)(2,1)}), bf16[64,8,128]{2,1,0:T(8,128)(2,1)S(1)}, u32[]{:S(2)}, u32[]{:S(2)}) async-start(bf16[64,8,128]{2,1,0:T(8,128)(2,1)} %bitcast.10), calls=%async_computation | async-start | bytes 262144 | tf_op jit(solution)/shard_map/all_to_all | solution.py:335
  21.9 0.6 pad_add_fusion.here_ref
  22.5 3.1 %shard_map.68.table_ref = s32[560]{0:T(1024)} custom-call(s32[2]{0:T(128)} %pad_add_fusion.here_ref, s32[3,64]{1,0:T(4,128)} %matching_ref.1, s32[1,512]{1,0:T(1,128)} %mask_ref.1), custom_call_target="tpu_custom_call" | custom-call | flops 2000000 | bytes 4096 | tf_op jit(solution)/shard_map/pallas_call | solution.py:96
  25.6 9.9 %all-to-all-done.pieces_ref = bf16[64,8,128]{2,1,0:T(8,128)(2,1)S(1)} async-done(((bf16[64,8,128]{2,1,0:T(8,128)(2,1)}), bf16[64,8,128]{2,1,0:T(8,128)(2,1)S(1)}, u32[]{:S(2)}, u32[]{:S(2)}) %all-to-all-start) | async-done | bytes 131104 | tf_op jit(solution)/shard_map/all_to_all | solution.py:335
  35.5 0.0 copy-start
  35.5 0.7 copy-done
  36.2 1.2 shard_map.70
  37.4 33.5 %all_to_all.15.got_ref = bf16[64,9,8,128]{3,2,1,0:T(8,128)(2,1)S(1)} all-to-all(bf16[64,9,8,128]{3,2,1,0:T(8,128)(2,1)S(1)} %shard_map.70), channel_id=1, replica_groups=mesh['yh'=2,'x'=4,'z'=8,'yl'=4,'core'=2] {'yh','yl','z'}, dimensions={0} | all-to-all | bytes 2359296 | tf_op jit(solution)/shard_map/all_to_all | solution.py:335
  70.9 0.2 shard_map.71
  71.1 0.0 copy-start.1
  71.1 22.5 %all_to_all.16 = bf16[8,66,8,128]{3,2,1,0:T(8,128)(2,1)S(1)} all-to-all(bf16[8,66,8,128]{3,2,1,0:T(8,128)(2,1)S(1)} %shard_map.71), channel_id=1, replica_groups=mesh['yh'=2,'x'=4,'z'=8,'yl'=4,'core'=2] {'x','core'}, dimensions={0} | all-to-all | bytes 2162688 | tf_op jit(solution)/shard_map/all_to_all | solution.py:335
  93.7 1.3 collective-permute-start.2
  95.0 0.0 copy-done.1
  95.0 1.4 shard_map.72
  96.4 5.0 %shard_map.73 = (f32[8,128,128]{2,1,0:T(8,128)S(1)}, bf16[8,128,128]{2,1,0:T(8,128)(2,1)S(1)}) custom-call(s32[560]{0:T(1024)S(1)} %copy-done.1, f32[8,8,128]{2,1,0:T(8,128)S(1)} %get-tuple-element.20.ks, f32[8,8,128,128]{3,2,1,0:T(8,128)S(1)} %get-tuple-element.21.sim_ref, bf16[8,528,128]{2,1,0:T(8,128)(2,1)S(1)} %bitcast.8), custom_call_target="tpu_custom_call" | custom-call | flops 805306368 | bytes 6291456 | tf_op jit(solution)/shard_map/pallas_call | solution.py:315
  101.4 6.1 %collective-permute-start.1 = (bf16[8,128,128]{2,1,0:T(8,128)(2,1)S(1)}, bf16[8,128,128]{2,1,0:T(8,128)(2,1)S(1)}, u32[]{:S(2)}, u32[]{:S(2)}) collective-permute-start(bf16[8,128,128]{2,1,0:T(8,128)(2,1)S(1)} %get-tuple-element.22), channel_id=1, source_target_pairs={{0,1},{1,0},{2,3},{3,2},{4,5},{5,4},{6,7},{7,6},{8,9},{9,8},{10,11... | collective-permute-start | bytes 786440 | tf_op jit(solution)/shard_map/ppermute | solution.py:331
  107.5 1.9 %collective-permute-start = (bf16[8,256,128]{2,1,0:T(8,128)(2,1)S(1)}, bf16[8,256,128]{2,1,0:T(8,128)(2,1)S(1)}, u32[]{:S(2)}, u32[]{:S(2)}) collective-permute-start(bf16[8,256,128]{2,1,0:T(8,128)(2,1)S(1)} %slice.9.xl_ref), channel_id=1, source_target_pairs={{0,1},{1,0},{2,3},{3,2},{4,5},{5,4},{6,7},{7,6},{8,9},{9,8},{10,11... | collective-permute-start | bytes 1572872 | tf_op jit(solution)/shard_map/ppermute | solution.py:331
  109.4 0.0 collective-permute-done.1.refs_1_
  109.4 0.7 collective-permute-done.2
  110.1 2.5 %collective-permute-start.3 = (bf16[8,256,128]{2,1,0:T(8,128)(2,1)S(1)}, bf16[8,256,128]{2,1,0:T(8,128)(2,1)}, u32[]{:S(2)}, u32[]{:S(2)}) collective-permute-start(bf16[8,256,128]{2,1,0:T(8,128)(2,1)S(1)} %collective-permute-done.2), channel_id=1, source_target_pairs={{1,0},{3,2},{4,5},{6,7},{9,8},{11,10},{12,13},{14,15},{17,16},{19,... | collective-permute-start | bytes 1572872 | tf_op jit(solution)/shard_map/ppermute | solution.py:363
  112.7 0.0 collective-permute-done.xr_ref
  112.7 1.3 shard_map.75
  114.0 5.0 %shard_map.76 = (f32[8,128,128]{2,1,0:T(8,128)S(1)}, bf16[8,128,128]{2,1,0:T(8,128)(2,1)S(1)}) custom-call(s32[560]{0:T(1024)S(1)} %copy-done.1, f32[8,8,128]{2,1,0:T(8,128)S(1)} %get-tuple-element.26.ks, f32[8,8,128,128]{3,2,1,0:T(8,128)S(1)} %get-tuple-element.27.sim_ref, f32[8,128,128]{2,1,0:T(8,128)S(1)} %get-tuple-element.28.refs_0_, ...), custom_call_target="tpu_custom_call" | custom-call | flops 805306368 | bytes 6291456 | tf_op jit(solution)/shard_map/pallas_call | solution.py:315
  119.0 1.9 %collective-permute-start.4 = (bf16[8,128,128]{2,1,0:T(8,128)(2,1)S(1)}, bf16[8,128,128]{2,1,0:T(8,128)(2,1)S(1)}, u32[]{:S(2)}, u32[]{:S(2)}) collective-permute-start(bf16[8,128,128]{2,1,0:T(8,128)(2,1)S(1)} %get-tuple-element.31), channel_id=1, source_target_pairs={{0,4},{1,5},{2,6},{3,7},{4,0},{5,1},{6,2},{7,3},{8,12},{9,13},{10,... | collective-permute-start | bytes 786440 | tf_op jit(solution)/shard_map/ppermute | solution.py:331
  120.9 0.0 collective-permute-done.3
  120.9 0.2 broadcast_select_fusion.2
  121.1 4.2 %collective-permute-start.5 = (bf16[8,256,128]{2,1,0:T(8,128)(2,1)S(1)}, bf16[8,256,128]{2,1,0:T(8,128)(2,1)S(1)}, u32[]{:S(2)}, u32[]{:S(2)}) collective-permute-start(bf16[8,256,128]{2,1,0:T(8,128)(2,1)S(1)} %get-tuple-element.38.xl_ref), channel_id=1, source_target_pairs={{0,2},{1,3},{2,0},{3,1},{4,6},{5,7},{6,4},{7,5},{8,10},{9,11},{10,... | collective-permute-start | bytes 1572872 | tf_op jit(solution)/shard_map/ppermute | solution.py:331
  125.3 1.3 shard_map.74
  126.6 8.0 %collective-permute-done.4.refs_1_ = bf16[8,128,128]{2,1,0:T(8,128)(2,1)S(1)} collective-permute-done((bf16[8,128,128]{2,1,0:T(8,128)(2,1)S(1)}, bf16[8,128,128]{2,1,0:T(8,128)(2,1)S(1)}, u32[]{:S(2)}, u32[]{:S(2)}) %collective-permute-start.4) | collective-permute-done | bytes 262176 | tf_op jit(solution)/shard_map/ppermute | solution.py:331
  134.6 4.8 %shard_map.77 = (f32[8,128,128]{2,1,0:T(8,128)S(1)}, bf16[8,128,128]{2,1,0:T(8,128)(2,1)S(1)}) custom-call(s32[560]{0:T(1024)S(1)} %copy-done.1, f32[8,8,128]{2,1,0:T(8,128)S(1)} %get-tuple-element.24.ks, f32[8,8,128,128]{3,2,1,0:T(8,128)S(1)} %get-tuple-element.25.sim_ref, f32[8,128,128]{2,1,0:T(8,128)S(1)} %get-tuple-element.30.refs_0_, ...), custom_call_target="tpu_custom_call" | custom-call | flops 805306368 | bytes 6291456 | tf_op jit(solution)/shard_map/pallas_call | solution.py:315
  139.4 2.1 %collective-permute-start.6 = (bf16[8,128,128]{2,1,0:T(8,128)(2,1)S(1)}, bf16[8,128,128]{2,1,0:T(8,128)(2,1)S(1)}, u32[]{:S(2)}, u32[]{:S(2)}) collective-permute-start(bf16[8,128,128]{2,1,0:T(8,128)(2,1)S(1)} %get-tuple-element.37), channel_id=1, source_target_pairs={{0,2},{1,3},{2,0},{3,1},{4,6},{5,7},{6,4},{7,5},{8,10},{9,11},{10,... | collective-permute-start | bytes 786440 | tf_op jit(solution)/shard_map/ppermute | solution.py:331
  141.6 0.0 collective-permute-done.5.xr_ref
  141.6 1.4 shard_map.78
  142.9 6.5 %collective-permute-done.6.refs_1_ = bf16[8,128,128]{2,1,0:T(8,128)(2,1)S(1)} collective-permute-done((bf16[8,128,128]{2,1,0:T(8,128)(2,1)S(1)}, bf16[8,128,128]{2,1,0:T(8,128)(2,1)S(1)}, u32[]{:S(2)}, u32[]{:S(2)}) %collective-permute-start.6) | collective-permute-done | bytes 262176 | tf_op jit(solution)/shard_map/ppermute | solution.py:331
  149.4 4.9 %shard_map.79 = (f32[128,128]{1,0:T(8,128)}, f32[128,128]{1,0:T(8,128)}) custom-call(s32[560]{0:T(1024)S(1)} %copy-done.1, f32[8,8,128]{2,1,0:T(8,128)S(1)} %get-tuple-element.34.ks, f32[8,8,128,128]{3,2,1,0:T(8,128)S(1)} %get-tuple-element.35.sim_ref, f32[8,128,128]{2,1,0:T(8,128)S(1)} %get-tuple-element.36.refs_0_, ...), custom_call_target="tpu_custom_call" | custom-call | flops 805306368 | bytes 6291456 | tf_op jit(solution)/shard_map/pallas_call | solution.py:315
  (2 shorter events, 0.0 us)
Async XLA Ops:
  2.3 33.2 %all-to-all-start = ((bf16[64,8,128]{2,1,0:T(8,128)(2,1)}), bf16[64,8,128]{2,1,0:T(8,128)(2,1)S(1)}, u32[]{:S(2)}, u32[]{:S(2)}) async-start(bf16[64,8,128]{2,1,0:T(8,128)(2,1)} %bitcast.10), calls=%async_computation | async-start | bytes 262144 | tf_op jit(solution)/shard_map/all_to_all | solution.py:335
  35.5 0.7 copy-start
  71.1 23.9 %copy-start.1 = (s32[560]{0:T(1024)S(1)}, s32[560]{0:T(1024)}, u32[]{:S(2)}) copy-start(s32[560]{0:T(1024)} %shard_map.68.table_ref) | copy-start | bytes 6724
  93.7 16.4 %collective-permute-start.2 = (bf16[8,256,128]{2,1,0:T(8,128)(2,1)S(1)}, bf16[8,256,128]{2,1,0:T(8,128)(2,1)S(1)}, u32[]{:S(2)}, u32[]{:S(2)}) collective-permute-start(bf16[8,256,128]{2,1,0:T(8,128)(2,1)S(1)} %slice.9.xl_ref), channel_id=1, source_target_pairs={{0,4},{2,6},{5,1},{7,3},{8,12},{10,14},{13,9},{15,11},{16,20},{18,... | collective-permute-start | bytes 1572872 | tf_op jit(solution)/shard_map/ppermute | solution.py:355
  101.4 8.1 %collective-permute-start.1 = (bf16[8,128,128]{2,1,0:T(8,128)(2,1)S(1)}, bf16[8,128,128]{2,1,0:T(8,128)(2,1)S(1)}, u32[]{:S(2)}, u32[]{:S(2)}) collective-permute-start(bf16[8,128,128]{2,1,0:T(8,128)(2,1)S(1)} %get-tuple-element.22), channel_id=1, source_target_pairs={{0,1},{1,0},{2,3},{3,2},{4,5},{5,4},{6,7},{7,6},{8,9},{9,8},{10,11... | collective-permute-start | bytes 786440 | tf_op jit(solution)/shard_map/ppermute | solution.py:331
  107.5 5.2 %collective-permute-start = (bf16[8,256,128]{2,1,0:T(8,128)(2,1)S(1)}, bf16[8,256,128]{2,1,0:T(8,128)(2,1)S(1)}, u32[]{:S(2)}, u32[]{:S(2)}) collective-permute-start(bf16[8,256,128]{2,1,0:T(8,128)(2,1)S(1)} %slice.9.xl_ref), channel_id=1, source_target_pairs={{0,1},{1,0},{2,3},{3,2},{4,5},{5,4},{6,7},{7,6},{8,9},{9,8},{10,11... | collective-permute-start | bytes 1572872 | tf_op jit(solution)/shard_map/ppermute | solution.py:331
  110.1 10.8 %collective-permute-start.3 = (bf16[8,256,128]{2,1,0:T(8,128)(2,1)S(1)}, bf16[8,256,128]{2,1,0:T(8,128)(2,1)}, u32[]{:S(2)}, u32[]{:S(2)}) collective-permute-start(bf16[8,256,128]{2,1,0:T(8,128)(2,1)S(1)} %collective-permute-done.2), channel_id=1, source_target_pairs={{1,0},{3,2},{4,5},{6,7},{9,8},{11,10},{12,13},{14,15},{17,16},{19,... | collective-permute-start | bytes 1572872 | tf_op jit(solution)/shard_map/ppermute | solution.py:363
  119.0 15.6 %collective-permute-start.4 = (bf16[8,128,128]{2,1,0:T(8,128)(2,1)S(1)}, bf16[8,128,128]{2,1,0:T(8,128)(2,1)S(1)}, u32[]{:S(2)}, u32[]{:S(2)}) collective-permute-start(bf16[8,128,128]{2,1,0:T(8,128)(2,1)S(1)} %get-tuple-element.31), channel_id=1, source_target_pairs={{0,4},{1,5},{2,6},{3,7},{4,0},{5,1},{6,2},{7,3},{8,12},{9,13},{10,... | collective-permute-start | bytes 786440 | tf_op jit(solution)/shard_map/ppermute | solution.py:331
  121.1 20.4 %collective-permute-start.5 = (bf16[8,256,128]{2,1,0:T(8,128)(2,1)S(1)}, bf16[8,256,128]{2,1,0:T(8,128)(2,1)S(1)}, u32[]{:S(2)}, u32[]{:S(2)}) collective-permute-start(bf16[8,256,128]{2,1,0:T(8,128)(2,1)S(1)} %get-tuple-element.38.xl_ref), channel_id=1, source_target_pairs={{0,2},{1,3},{2,0},{3,1},{4,6},{5,7},{6,4},{7,5},{8,10},{9,11},{10,... | collective-permute-start | bytes 1572872 | tf_op jit(solution)/shard_map/ppermute | solution.py:331
  139.4 10.0 %collective-permute-start.6 = (bf16[8,128,128]{2,1,0:T(8,128)(2,1)S(1)}, bf16[8,128,128]{2,1,0:T(8,128)(2,1)S(1)}, u32[]{:S(2)}, u32[]{:S(2)}) collective-permute-start(bf16[8,128,128]{2,1,0:T(8,128)(2,1)S(1)} %get-tuple-element.37), channel_id=1, source_target_pairs={{0,2},{1,3},{2,0},{3,1},{4,6},{5,7},{6,4},{7,5},{8,10},{9,11},{10,... | collective-permute-start | bytes 786440 | tf_op jit(solution)/shard_map/ppermute | solution.py:331
